TPU v7x, 32 devices: a whole 2x2x4 slice. The times are simulated.
32 devices in a mesh: fsdp: 4 (over y, x), ctx: 2 (over core), tp: 4 (over z).
Axes of the slice: x: 2, y: 2, z: 4, core: 2. Of those that a mesh axis runs over, the one named last changes fastest.
Arguments:
- tokens: bfloat16 [8192, 2560], P(('fsdp', 'ctx'), 'tp'), may hold values from -6 to 6
- cotangent: bfloat16 [8192, 2560], P(('fsdp', 'ctx')), may hold values from -6 to 6
- lengths: int32 [4, 1], P('fsdp'), may hold values from 1024 to 2048, as said below
- w_qdown: float32 [2560, 768], P('tp', ('fsdp', 'ctx')), may hold values from -0.125 to 0.125
- w_kvdown: float32 [2560, 288], P('tp', ('fsdp', 'ctx')), may hold values from -0.125 to 0.125
- w_qup: float32 [768, 3840], P(('fsdp', 'ctx'), 'tp'), may hold values from -0.21875 to 0.21875
- w_kvup: float32 [256, 5120], P(('fsdp', 'ctx'), 'tp'), may hold values from -0.375 to 0.375
- w_out: float32 [2560, 2560], P('tp', ('fsdp', 'ctx')), may hold values from -1 to 1
- w_gateup: float32 [2, 2560, 6400], P(None, ('fsdp', 'ctx'), 'tp'), may hold values from -0.125 to 0.125
- w_down: float32 [6400, 2560], P('tp', ('fsdp', 'ctx')), may hold values from -0.625 to 0.625
- g_norms: float32 [2, 2560], P(None, 'tp'), may hold values from 0.5 to 1.5
- g_latent: float32 [1024], P(('fsdp', 'ctx')), may hold values from 0.5 to 1.5
- m_qdown: float32 [2560, 768], P('tp', ('fsdp', 'ctx')), may hold values from -0.00012207031 to 0.00012207031
- m_kvdown: float32 [2560, 288], P('tp', ('fsdp', 'ctx')), may hold values from -0.00012207031 to 0.00012207031
- m_qup: float32 [768, 3840], P(('fsdp', 'ctx'), 'tp'), may hold values from -0.00012207031 to 0.00012207031
- m_kvup: float32 [256, 5120], P(('fsdp', 'ctx'), 'tp'), may hold values from -0.00012207031 to 0.00012207031
- m_out: float32 [2560, 2560], P('tp', ('fsdp', 'ctx')), may hold values from -0.00012207031 to 0.00012207031
- m_gateup: float32 [2, 2560, 6400], P(None, ('fsdp', 'ctx'), 'tp'), may hold values from -0.00012207031 to 0.00012207031
- m_down: float32 [6400, 2560], P('tp', ('fsdp', 'ctx')), may hold values from -0.00012207031 to 0.00012207031
- m_norms: float32 [2, 2560], P(None, 'tp'), may hold values from -0.00012207031 to 0.00012207031
- m_latent: float32 [1024], P(('fsdp', 'ctx')), may hold values from -0.00012207031 to 0.00012207031
- v_qdown: float32 [2560, 768], P('tp', ('fsdp', 'ctx')), may hold values from 2e-09 to 8e-09
- v_kvdown: float32 [2560, 288], P('tp', ('fsdp', 'ctx')), may hold values from 2e-09 to 8e-09
- v_qup: float32 [768, 3840], P(('fsdp', 'ctx'), 'tp'), may hold values from 2e-09 to 8e-09
- v_kvup: float32 [256, 5120], P(('fsdp', 'ctx'), 'tp'), may hold values from 2e-09 to 8e-09
- v_out: float32 [2560, 2560], P('tp', ('fsdp', 'ctx')), may hold values from 2e-09 to 8e-09
- v_gateup: float32 [2, 2560, 6400], P(None, ('fsdp', 'ctx'), 'tp'), may hold values from 2e-09 to 8e-09
- v_down: float32 [6400, 2560], P('tp', ('fsdp', 'ctx')), may hold values from 2e-09 to 8e-09
- v_norms: float32 [2, 2560], P(None, 'tp'), may hold values from 2e-09 to 8e-09
- v_latent: float32 [1024], P(('fsdp', 'ctx')), may hold values from 2e-09 to 8e-09
Outputs:
- layer_out: bfloat16 [8192, 2560], P(('fsdp', 'ctx'), 'tp')
- grad_input: bfloat16 [8192, 2560], P(('fsdp', 'ctx'), 'tp')
- grad_qdown: float32 [2560, 768], P('tp', ('fsdp', 'ctx'))
- grad_kvdown: float32 [2560, 288], P('tp', ('fsdp', 'ctx'))
- grad_qup: float32 [768, 3840], P(('fsdp', 'ctx'), 'tp')
- grad_kvup: float32 [256, 5120], P(('fsdp', 'ctx'), 'tp')
- grad_out: float32 [2560, 2560], P('tp', ('fsdp', 'ctx'))
- grad_gateup: float32 [2, 2560, 6400], P(None, ('fsdp', 'ctx'), 'tp')
- grad_down: float32 [6400, 2560], P('tp', ('fsdp', 'ctx'))
- grad_norms: float32 [2, 2560], P(None, 'tp')
- grad_latent: float32 [1024], P(('fsdp', 'ctx'))
- new_qdown: float32 [2560, 768], P('tp', ('fsdp', 'ctx'))
- new_kvdown: float32 [2560, 288], P('tp', ('fsdp', 'ctx'))
- new_qup: float32 [768, 3840], P(('fsdp', 'ctx'), 'tp')
- new_kvup: float32 [256, 5120], P(('fsdp', 'ctx'), 'tp')
- new_out: float32 [2560, 2560], P('tp', ('fsdp', 'ctx'))
- new_gateup: float32 [2, 2560, 6400], P(None, ('fsdp', 'ctx'), 'tp')
- new_down: float32 [6400, 2560], P('tp', ('fsdp', 'ctx'))
- first_qdown: float32 [2560, 768], P('tp', ('fsdp', 'ctx'))
- first_kvdown: float32 [2560, 288], P('tp', ('fsdp', 'ctx'))
- first_qup: float32 [768, 3840], P(('fsdp', 'ctx'), 'tp')
- first_kvup: float32 [256, 5120], P(('fsdp', 'ctx'), 'tp')
- first_out: float32 [2560, 2560], P('tp', ('fsdp', 'ctx'))
- first_gateup: float32 [2, 2560, 6400], P(None, ('fsdp', 'ctx'), 'tp')
- first_down: float32 [6400, 2560], P('tp', ('fsdp', 'ctx'))
- first_norms: float32 [2, 2560], P(None, 'tp')
- first_latent: float32 [1024], P(('fsdp', 'ctx'))
- second_qdown: float32 [2560, 768], P('tp', ('fsdp', 'ctx'))
- second_kvdown: float32 [2560, 288], P('tp', ('fsdp', 'ctx'))
- second_qup: float32 [768, 3840], P(('fsdp', 'ctx'), 'tp')
- second_kvup: float32 [256, 5120], P(('fsdp', 'ctx'), 'tp')
- second_out: float32 [2560, 2560], P('tp', ('fsdp', 'ctx'))
- second_gateup: float32 [2, 2560, 6400], P(None, ('fsdp', 'ctx'), 'tp')
- second_down: float32 [6400, 2560], P('tp', ('fsdp', 'ctx'))
- second_norms: float32 [2, 2560], P(None, 'tp')
- second_latent: float32 [1024], P(('fsdp', 'ctx'))
Inputs may be any that keep to these rules, and one draw needn't show every extreme that they name: `lengths`: entry g is the length of the one sequence at the start of slot g; the rest of the slot is padding. Some slot is full and some slot is half full in every draw.
All inputs are finite; a program needn't handle non-finite values.
Results may differ from a plain program's by a relative error of at most 0.035.
Values may be sent and summed in bfloat16 or wider, within the bound.
A program may use at most 448 MiB of HBM per device.

v0:
```python
import jax
import jax.numpy as jnp
from jax import lax
from jax.sharding import PartitionSpec as P

D = 2560
H = 40
NOPE = 64
ROPE = 32
VD = 64
QR = 768
KVR = 256
FF = 6400
STEP = 3


EPS_NORM = 1e-05
RESIDUAL_SCALE = 1.4 / 62**0.5
ROPE_BASE = 10000.0
MASK_VALUE = -1e30
BETA_ONE = 0.9
BETA_TWO = 0.95
ADAM_EPS = 1e-08
LEARN_RATE = 0.1
WEIGHT_DECAY = 0.1
CLIP_RMS = 0.0002


def passed_along(shard, axis, by):
    length = lax.axis_size(axis)
    pairs = [(i, i + by) for i in range(length) if 0 <= i + by < length]
    return lax.ppermute(shard, axis, pairs)


def rounded(values):
    return lax.optimization_barrier(values.astype(jnp.bfloat16)).astype(jnp.float32)


def rotary_tables(positions, rope_width):
    half_width = rope_width // 2
    frequency = ROPE_BASE ** (-2.0 * jnp.arange(half_width, dtype=jnp.float32) / rope_width)
    angles = positions.astype(jnp.float32)[:, None] * frequency[None, :]
    cosine = jnp.cos(angles)
    sine_table = jnp.sin(angles)
    return (
        jnp.concatenate([cosine, cosine], axis=1),
        jnp.concatenate([sine_table, sine_table], axis=1),
    )


def rotate_forward(values, cosine, sine_table):
    half_width = values.shape[-1] // 2
    turned = jnp.concatenate([-values[..., half_width:], values[..., :half_width]], axis=-1)
    return values * cosine + turned * sine_table


def rotate_backward(incoming, cosine, sine_table):
    half_width = incoming.shape[-1] // 2
    scaled = incoming * sine_table
    turned = jnp.concatenate([scaled[..., half_width:], -scaled[..., :half_width]], axis=-1)
    return incoming * cosine + turned


def group_layout(seq_length, indices):
    segment = (indices >= seq_length).astype(jnp.int32)
    return (segment, indices - segment * seq_length)


def block_mask(index_block, segment_block, key_index, key_segment):
    return (
        (key_index[None, :] >= 0)
        & (key_index[None, :] <= index_block[:, None])
        & (key_segment[None, :] == segment_block[:, None])
    )


def product(spec, left_side, right_side):
    return jnp.einsum(spec, left_side, right_side, preferred_element_type=jnp.float32)


def contract_last(left_side, right_side):
    return lax.dot_general(
        left_side, right_side, (((1,), (1,)), ((), ())), preferred_element_type=jnp.float32
    )


def contract_first(left_side, right_side):
    return lax.dot_general(
        left_side, right_side, (((0,), (0,)), ((), ())), preferred_element_type=jnp.float32
    )


def row_total(values):
    return lax.psum(values, "tp")


def norm_backward(incoming, values, factor, gain):
    scaled = incoming * gain
    gain_grad = jnp.sum(incoming * values * factor, axis=0)
    result = factor * scaled - values * factor**3 * jnp.mean(scaled * values, axis=1, keepdims=True)
    return (result, gain_grad)


def split_norm_backward(incoming, values, factor, gain):
    scaled = incoming * gain
    gain_grad = jnp.sum(incoming * values * factor, axis=0)
    row_inner = row_total(jnp.sum(scaled * values, axis=1))[:, None] / D
    return (factor * scaled - values * factor**3 * row_inner, gain_grad)


def expand_keys(key_latent, key_rope, kv_up):
    row_count = key_latent.shape[0]
    head_count = kv_up.shape[1] // (NOPE + VD)
    expanded = jnp.dot(key_latent, kv_up, preferred_element_type=jnp.float32).reshape(
        row_count, head_count, NOPE + VD
    )
    rope_part = jnp.broadcast_to(key_rope[:, None, :], (row_count, head_count, ROPE))
    key_full = jnp.concatenate([expanded[..., :NOPE].astype(jnp.bfloat16), rope_part], axis=2)
    return (key_full, expanded[..., NOPE:].astype(jnp.bfloat16))


def attend_forward(queries, key_full, values, query_index, query_segment, key_index, key_segment):
    row_count, head_count, head_depth = queries.shape
    block_rows = min(512, row_count)
    block_count = row_count // block_rows
    score_scale = head_depth ** (-0.5)

    def one_block(carried, pieces):
        query_block, index_block, segment_block = pieces
        allowed = block_mask(index_block, segment_block, key_index, key_segment)
        scores = jnp.where(
            allowed[None], product("qhd,khd->hqk", query_block, key_full) * score_scale, MASK_VALUE
        )
        largest = jnp.max(scores, axis=2, keepdims=True)
        exp_scores = jnp.exp(scores - largest)
        denominator = jnp.sum(exp_scores, axis=2, keepdims=True)
        prob_block = (exp_scores / denominator).astype(jnp.bfloat16)
        result = product("hqk,khd->qhd", prob_block, values).astype(jnp.bfloat16)
        return (carried, (result, (largest + jnp.log(denominator))[:, :, 0]))

    _, (results, log_totals) = lax.scan(
        one_block,
        None,
        (
            queries.reshape(block_count, block_rows, head_count, head_depth),
            query_index.reshape(block_count, block_rows),
            query_segment.reshape(block_count, block_rows),
        ),
    )
    return (results.reshape(row_count, head_count, values.shape[2]), log_totals)


def attend_backward(
    queries,
    key_full,
    values,
    results,
    d_results,
    log_totals,
    query_index,
    query_segment,
    key_index,
    key_segment,
):
    row_count, head_count, head_depth = queries.shape
    block_rows = min(512, row_count)
    block_count = row_count // block_rows
    score_scale = head_depth ** (-0.5)
    value_depth = values.shape[2]

    def one_block(carried, pieces):
        key_sum, value_sum = carried
        query_block, result_block, grad_block, log_block, index_block, segment_block = pieces
        allowed = block_mask(index_block, segment_block, key_index, key_segment)
        scores = jnp.where(
            allowed[None], product("qhd,khd->hqk", query_block, key_full) * score_scale, MASK_VALUE
        )
        prob_full = jnp.exp(scores - log_block[:, :, None])
        prob_block = prob_full.astype(jnp.bfloat16)
        d_prob = product("qhd,khd->hqk", grad_block, values)
        row_inner = jnp.transpose(
            jnp.sum(grad_block.astype(jnp.float32) * result_block.astype(jnp.float32), axis=2)
        )
        d_score = (prob_full * (d_prob - row_inner[:, :, None]) * score_scale).astype(jnp.bfloat16)
        d_query = product("hqk,khd->qhd", d_score, key_full)
        key_sum = key_sum + product("hqk,qhd->khd", d_score, query_block)
        value_sum = value_sum + product("hqk,qhd->khd", prob_block, grad_block)
        return ((key_sum, value_sum), d_query)

    initial = (jnp.zeros(key_full.shape, jnp.float32), jnp.zeros(values.shape, jnp.float32))
    pieces = (
        queries.reshape(block_count, block_rows, head_count, head_depth),
        results.reshape(block_count, block_rows, head_count, value_depth),
        d_results.reshape(block_count, block_rows, head_count, value_depth),
        log_totals,
        query_index.reshape(block_count, block_rows),
        query_segment.reshape(block_count, block_rows),
    )
    (key_sum, value_sum), d_queries = lax.scan(one_block, initial, pieces)
    return (d_queries.reshape(row_count, head_count, head_depth), key_sum, value_sum)


def collect_weights(shards):
    return (
        lax.all_gather(shards[0], ("fsdp", "ctx"), axis=1, tiled=True),
        lax.all_gather(shards[1], ("fsdp", "ctx"), axis=1, tiled=True),
        lax.all_gather(shards[2], ("fsdp", "ctx"), axis=0, tiled=True),
        lax.all_gather(shards[3], ("fsdp", "ctx"), axis=0, tiled=True),
        lax.all_gather(shards[4], ("fsdp", "ctx"), axis=1, tiled=True),
        lax.all_gather(shards[5], ("fsdp", "ctx"), axis=1, tiled=True),
        lax.all_gather(shards[6], ("fsdp", "ctx"), axis=1, tiled=True),
        lax.all_gather(shards[7], ("fsdp", "ctx"), axis=0, tiled=True),
    )


def adamw_update(parameter, gradient, first_moment, second_moment, decay_rate):
    first_new = BETA_ONE * first_moment + (1.0 - BETA_ONE) * gradient
    second_new = BETA_TWO * second_moment + (1.0 - BETA_TWO) * gradient * gradient
    first_hat = first_new / (1.0 - BETA_ONE**STEP)
    second_hat = second_new / (1.0 - BETA_TWO**STEP)
    updated = parameter - LEARN_RATE * (
        first_hat / (jnp.sqrt(second_hat) + ADAM_EPS) + decay_rate * parameter
    )
    return (updated, first_new, second_new)


def local(
    tokens,
    cotangent,
    lengths,
    w_qdown,
    w_kvdown,
    w_qup,
    w_kvup,
    w_out,
    w_gateup,
    w_down,
    g_norms,
    g_latent,
    m_qdown,
    m_kvdown,
    m_qup,
    m_kvup,
    m_out,
    m_gateup,
    m_down,
    m_norms,
    m_latent,
    v_qdown,
    v_kvdown,
    v_qup,
    v_kvup,
    v_out,
    v_gateup,
    v_down,
    v_norms,
    v_latent,
):
    params = (w_qdown, w_kvdown, w_qup, w_kvup, w_out, w_gateup, w_down, g_norms, g_latent)
    firsts = (m_qdown, m_kvdown, m_qup, m_kvup, m_out, m_gateup, m_down, m_norms, m_latent)
    seconds = (v_qdown, v_kvdown, v_qup, v_kvup, v_out, v_gateup, v_down, v_norms, v_latent)
    block_rows = tokens.shape[0]
    local_width = tokens.shape[1]
    head_width = NOPE + ROPE
    tp_index = lax.axis_index("tp")
    ctx_index = lax.axis_index("ctx")
    shards = (
        w_qdown.astype(jnp.bfloat16),
        w_kvdown.astype(jnp.bfloat16),
        w_qup.astype(jnp.bfloat16),
        w_kvup.astype(jnp.bfloat16),
        w_out.astype(jnp.bfloat16),
        w_gateup.astype(jnp.bfloat16),
        w_down.astype(jnp.bfloat16),
        g_latent.astype(jnp.bfloat16),
    )
    q_down, kv_down, q_up, kv_up, out_weight, gate_up, down_weight, latent_gains = collect_weights(
        shards
    )
    gains_norm = rounded(g_norms)
    gain_attn = gains_norm[0]
    gain_mlp = gains_norm[1]
    gain_query = latent_gains[:QR].astype(jnp.float32)
    gain_latent = latent_gains[QR:].astype(jnp.float32)
    seq_length = lengths[0, 0]
    own_index = ctx_index * block_rows + jnp.arange(block_rows, dtype=jnp.int32)
    key_index = (ctx_index - 1) * block_rows + jnp.arange(2 * block_rows, dtype=jnp.int32)
    own_segment, own_position = group_layout(seq_length, own_index)
    key_segment, _ = group_layout(seq_length, key_index)
    cosine, sine_table = rotary_tables(own_position, ROPE)
    inputs = tokens.astype(jnp.float32)
    factor_one = lax.rsqrt(row_total(jnp.sum(inputs * inputs, axis=1)) / D + EPS_NORM)[:, None]
    normed_one = (inputs * factor_one * gain_attn).astype(jnp.bfloat16)
    down_both = jnp.concatenate([q_down, kv_down], axis=1)
    latents = lax.psum(
        jnp.dot(normed_one, down_both, preferred_element_type=jnp.float32).astype(jnp.bfloat16),
        "tp",
    ).astype(jnp.float32)
    query_latent = latents[:, :QR]
    kv_latent = latents[:, QR : QR + KVR]
    rope_raw = latents[:, QR + KVR :]
    factor_query = lax.rsqrt(
        jnp.mean(query_latent * query_latent, axis=1, keepdims=True) + EPS_NORM
    )
    query_normed = (query_latent * factor_query * gain_query).astype(jnp.bfloat16)
    factor_kv = lax.rsqrt(jnp.mean(kv_latent * kv_latent, axis=1, keepdims=True) + EPS_NORM)
    kv_normed = (kv_latent * factor_kv * gain_latent).astype(jnp.bfloat16)
    rope_key = rotate_forward(rope_raw, cosine, sine_table).astype(jnp.bfloat16)
    query_all = jnp.dot(query_normed, q_up, preferred_element_type=jnp.float32).reshape(
        block_rows, -1, head_width
    )
    queries = jnp.concatenate(
        [
            query_all[..., :NOPE],
            rotate_forward(query_all[..., NOPE:], cosine[:, None], sine_table[:, None]),
        ],
        axis=2,
    ).astype(jnp.bfloat16)
    prior_kv, prior_rope = passed_along((kv_normed, rope_key), "ctx", 1)
    key_latent = jnp.concatenate([prior_kv, kv_normed], axis=0)
    key_rope = jnp.concatenate([prior_rope, rope_key], axis=0)
    key_full, key_values = expand_keys(key_latent, key_rope, kv_up)
    attended, log_totals = attend_forward(
        queries, key_full, key_values, own_index, own_segment, key_index, key_segment
    )
    attended_flat = attended.reshape(block_rows, -1)
    attn_part = lax.psum_scatter(
        jnp.dot(attended_flat, out_weight, preferred_element_type=jnp.float32).astype(jnp.bfloat16),
        "tp",
        scatter_dimension=1,
        tiled=True,
    ).astype(jnp.float32)
    hidden = inputs + RESIDUAL_SCALE * attn_part
    factor_two = lax.rsqrt(row_total(jnp.sum(hidden * hidden, axis=1)) / D + EPS_NORM)[:, None]
    normed_two = (hidden * factor_two * gain_mlp).astype(jnp.bfloat16)
    normed_full = lax.all_gather(normed_two, "tp", axis=1, tiled=True)
    gate_proj = jnp.dot(normed_full, gate_up[0], preferred_element_type=jnp.float32)
    up_proj = jnp.dot(normed_full, gate_up[1], preferred_element_type=jnp.float32)
    sigmoid_gate = jax.nn.sigmoid(gate_proj)
    activation = (gate_proj * sigmoid_gate * up_proj).astype(jnp.bfloat16)
    mlp_part = lax.psum_scatter(
        jnp.dot(activation, down_weight, preferred_element_type=jnp.float32).astype(jnp.bfloat16),
        "tp",
        scatter_dimension=1,
        tiled=True,
    ).astype(jnp.float32)
    layer_out = (hidden + RESIDUAL_SCALE * mlp_part).astype(jnp.bfloat16)
    live_rows = (own_segment == 0).astype(jnp.float32)[:, None]
    upstream_full = cotangent.astype(jnp.float32) * live_rows
    upstream = lax.dynamic_slice_in_dim(upstream_full, tp_index * local_width, local_width, 1)
    mlp_seed = (RESIDUAL_SCALE * upstream_full).astype(jnp.bfloat16)
    d_activation = contract_last(mlp_seed, down_weight)
    grad_down = contract_first(activation, mlp_seed)
    d_gate = (
        d_activation * up_proj * sigmoid_gate * (1.0 + gate_proj * (1.0 - sigmoid_gate))
    ).astype(jnp.bfloat16)
    d_up = (d_activation * gate_proj * sigmoid_gate).astype(jnp.bfloat16)
    grad_gateup = jnp.stack(
        [contract_first(normed_full, d_gate), contract_first(normed_full, d_up)]
    )
    d_normed_two = lax.psum_scatter(
        (contract_last(d_gate, gate_up[0]) + contract_last(d_up, gate_up[1])).astype(jnp.bfloat16),
        "tp",
        scatter_dimension=1,
        tiled=True,
    ).astype(jnp.float32)
    d_hidden_norm, grad_gain_mlp = split_norm_backward(d_normed_two, hidden, factor_two, gain_mlp)
    d_hidden = upstream + d_hidden_norm
    attn_seed = (RESIDUAL_SCALE * d_hidden).astype(jnp.bfloat16)
    seed_full = lax.all_gather(attn_seed, "tp", axis=1, tiled=True)
    d_attended = (
        contract_last(seed_full, out_weight).astype(jnp.bfloat16).reshape(block_rows, -1, VD)
    )
    grad_out = contract_first(attended_flat, seed_full)
    d_query, d_key, d_value = attend_backward(
        queries,
        key_full,
        key_values,
        attended,
        d_attended,
        log_totals,
        own_index,
        own_segment,
        key_index,
        key_segment,
    )
    d_expanded = (
        jnp.concatenate([d_key[..., :NOPE], d_value], axis=2)
        .reshape(2 * block_rows, -1)
        .astype(jnp.bfloat16)
    )
    grad_kvup = contract_first(key_latent, d_expanded)
    d_key_latent = contract_last(d_expanded, kv_up)
    d_key_rope = jnp.sum(d_key[..., NOPE:], axis=1)
    later_kv, later_rope = (
        passed_along(d_key_latent[:block_rows].astype(jnp.bfloat16), "ctx", -1).astype(jnp.float32),
        passed_along(d_key_rope[:block_rows].astype(jnp.bfloat16), "ctx", -1).astype(jnp.float32),
    )
    d_kv_normed = d_key_latent[block_rows:] + later_kv
    d_rope_key = rotate_backward(d_key_rope[block_rows:] + later_rope, cosine, sine_table)
    d_query_rope = rotate_backward(d_query[..., NOPE:], cosine[:, None], sine_table[:, None])
    d_query_flat = (
        jnp.concatenate([d_query[..., :NOPE], d_query_rope], axis=2)
        .reshape(block_rows, -1)
        .astype(jnp.bfloat16)
    )
    grad_qup = contract_first(query_normed, d_query_flat)
    d_query_normed = contract_last(d_query_flat, q_up)
    latent_grads = lax.psum(
        jnp.concatenate([d_query_normed, d_kv_normed, d_rope_key], axis=1).astype(jnp.bfloat16),
        "tp",
    ).astype(jnp.float32)
    d_query_latent, grad_gain_query = norm_backward(
        latent_grads[:, :QR], query_latent, factor_query, gain_query
    )
    d_kv_latent, grad_gain_latent = norm_backward(
        latent_grads[:, QR : QR + KVR], kv_latent, factor_kv, gain_latent
    )
    d_latents = jnp.concatenate(
        [d_query_latent, d_kv_latent, latent_grads[:, QR + KVR :]], axis=1
    ).astype(jnp.bfloat16)
    grad_both = contract_first(normed_one, d_latents)
    d_normed_one = contract_last(d_latents, down_both)
    d_input_norm, grad_gain_attn = split_norm_backward(d_normed_one, inputs, factor_one, gain_attn)
    grad_input = (d_hidden + d_input_norm).astype(jnp.bfloat16)
    fold_count = lax.axis_size("fsdp") * lax.axis_size("ctx")
    norm_grads = jnp.broadcast_to(
        jnp.stack([grad_gain_attn, grad_gain_mlp])[None], (fold_count, 2, local_width)
    )
    grad_latent = jnp.concatenate([grad_gain_query, grad_gain_latent])
    grad_qdown = grad_both[:, :QR]
    grad_kvdown = grad_both[:, QR:]
    outer_sums = (
        lax.psum_scatter(
            grad_qdown.astype(jnp.bfloat16), "fsdp", scatter_dimension=1, tiled=True
        ).astype(jnp.float32),
        lax.psum_scatter(
            grad_kvdown.astype(jnp.bfloat16), "fsdp", scatter_dimension=1, tiled=True
        ).astype(jnp.float32),
        lax.psum_scatter(
            grad_qup.astype(jnp.bfloat16), "fsdp", scatter_dimension=0, tiled=True
        ).astype(jnp.float32),
        lax.psum_scatter(
            grad_kvup.astype(jnp.bfloat16), "fsdp", scatter_dimension=0, tiled=True
        ).astype(jnp.float32),
        lax.psum_scatter(
            grad_out.astype(jnp.bfloat16), "fsdp", scatter_dimension=1, tiled=True
        ).astype(jnp.float32),
        lax.psum_scatter(
            grad_gateup.astype(jnp.bfloat16), "fsdp", scatter_dimension=1, tiled=True
        ).astype(jnp.float32),
        lax.psum_scatter(
            grad_down.astype(jnp.bfloat16), "fsdp", scatter_dimension=1, tiled=True
        ).astype(jnp.float32),
        lax.psum_scatter(
            grad_latent.astype(jnp.bfloat16), "fsdp", scatter_dimension=0, tiled=True
        ).astype(jnp.float32),
        lax.psum_scatter(
            norm_grads.astype(jnp.bfloat16), "fsdp", scatter_dimension=0, tiled=True
        ).astype(jnp.float32),
    )
    owned = (
        lax.psum_scatter(
            outer_sums[0].astype(jnp.bfloat16), "ctx", scatter_dimension=1, tiled=True
        ).astype(jnp.float32),
        lax.psum_scatter(
            outer_sums[1].astype(jnp.bfloat16), "ctx", scatter_dimension=1, tiled=True
        ).astype(jnp.float32),
        lax.psum_scatter(
            outer_sums[2].astype(jnp.bfloat16), "ctx", scatter_dimension=0, tiled=True
        ).astype(jnp.float32),
        lax.psum_scatter(
            outer_sums[3].astype(jnp.bfloat16), "ctx", scatter_dimension=0, tiled=True
        ).astype(jnp.float32),
        lax.psum_scatter(
            outer_sums[4].astype(jnp.bfloat16), "ctx", scatter_dimension=1, tiled=True
        ).astype(jnp.float32),
        lax.psum_scatter(
            outer_sums[5].astype(jnp.bfloat16), "ctx", scatter_dimension=1, tiled=True
        ).astype(jnp.float32),
        lax.psum_scatter(
            outer_sums[6].astype(jnp.bfloat16), "ctx", scatter_dimension=1, tiled=True
        ).astype(jnp.float32),
        lax.psum_scatter(
            outer_sums[7].astype(jnp.bfloat16), "ctx", scatter_dimension=0, tiled=True
        ).astype(jnp.float32),
        lax.psum_scatter(
            outer_sums[8].astype(jnp.bfloat16), "ctx", scatter_dimension=0, tiled=True
        ).astype(jnp.float32),
    )
    local_grads = (
        owned[0],
        owned[1],
        owned[2],
        owned[3],
        owned[4],
        owned[5],
        owned[6],
        owned[8][0],
        owned[7],
    )
    entry_counts = (
        D * QR,
        D * (KVR + ROPE),
        QR * H * (NOPE + ROPE),
        KVR * H * (NOPE + VD),
        H * VD * D,
        2 * D * FF,
        FF * D,
        2 * D,
        QR + KVR,
    )
    copies = (1.0, 1.0, 1.0, 1.0, 1.0, 1.0, 1.0, float(fold_count), float(lax.axis_size("tp")))
    local_squares = jnp.stack(
        [
            jnp.sum(local_grads[param_index] * local_grads[param_index]) / copies[param_index]
            for param_index in range(9)
        ]
    )
    total_squares = lax.psum(local_squares, ("fsdp", "ctx", "tp"))
    new_params = []
    new_firsts = []
    new_seconds = []
    for param_index in range(9):
        decay_rate = WEIGHT_DECAY if param_index < 7 else 0.0
        limit = CLIP_RMS * entry_counts[param_index] ** 0.5
        clipped = local_grads[param_index] * (
            limit / jnp.maximum(jnp.sqrt(total_squares[param_index]), limit)
        )
        updated, first_new, second_new = adamw_update(
            params[param_index], clipped, firsts[param_index], seconds[param_index], decay_rate
        )
        new_params.append(updated)
        new_firsts.append(first_new)
        new_seconds.append(second_new)
    return (
        layer_out,
        grad_input,
        local_grads[0],
        local_grads[1],
        local_grads[2],
        local_grads[3],
        local_grads[4],
        local_grads[5],
        local_grads[6],
        local_grads[7],
        local_grads[8],
        new_params[0],
        new_params[1],
        new_params[2],
        new_params[3],
        new_params[4],
        new_params[5],
        new_params[6],
        new_firsts[0],
        new_firsts[1],
        new_firsts[2],
        new_firsts[3],
        new_firsts[4],
        new_firsts[5],
        new_firsts[6],
        new_firsts[7],
        new_firsts[8],
        new_seconds[0],
        new_seconds[1],
        new_seconds[2],
        new_seconds[3],
        new_seconds[4],
        new_seconds[5],
        new_seconds[6],
        new_seconds[7],
        new_seconds[8],
    )


def solution(mesh):
    placed = (
        P(("fsdp", "ctx"), "tp"),
        P(("fsdp", "ctx"), None),
        P("fsdp", None),
        P("tp", ("fsdp", "ctx")),
        P("tp", ("fsdp", "ctx")),
        P(("fsdp", "ctx"), "tp"),
        P(("fsdp", "ctx"), "tp"),
        P("tp", ("fsdp", "ctx")),
        P(None, ("fsdp", "ctx"), "tp"),
        P("tp", ("fsdp", "ctx")),
        P(None, "tp"),
        P(("fsdp", "ctx")),
        P("tp", ("fsdp", "ctx")),
        P("tp", ("fsdp", "ctx")),
        P(("fsdp", "ctx"), "tp"),
        P(("fsdp", "ctx"), "tp"),
        P("tp", ("fsdp", "ctx")),
        P(None, ("fsdp", "ctx"), "tp"),
        P("tp", ("fsdp", "ctx")),
        P(None, "tp"),
        P(("fsdp", "ctx")),
        P("tp", ("fsdp", "ctx")),
        P("tp", ("fsdp", "ctx")),
        P(("fsdp", "ctx"), "tp"),
        P(("fsdp", "ctx"), "tp"),
        P("tp", ("fsdp", "ctx")),
        P(None, ("fsdp", "ctx"), "tp"),
        P("tp", ("fsdp", "ctx")),
        P(None, "tp"),
        P(("fsdp", "ctx")),
    )
    return jax.shard_map(
        local,
        mesh=mesh,
        in_specs=placed,
        out_specs=(
            P(("fsdp", "ctx"), "tp"),
            P(("fsdp", "ctx"), "tp"),
            P("tp", ("fsdp", "ctx")),
            P("tp", ("fsdp", "ctx")),
            P(("fsdp", "ctx"), "tp"),
            P(("fsdp", "ctx"), "tp"),
            P("tp", ("fsdp", "ctx")),
            P(None, ("fsdp", "ctx"), "tp"),
            P("tp", ("fsdp", "ctx")),
            P(None, "tp"),
            P(("fsdp", "ctx")),
            P("tp", ("fsdp", "ctx")),
            P("tp", ("fsdp", "ctx")),
            P(("fsdp", "ctx"), "tp"),
            P(("fsdp", "ctx"), "tp"),
            P("tp", ("fsdp", "ctx")),
            P(None, ("fsdp", "ctx"), "tp"),
            P("tp", ("fsdp", "ctx")),
            P("tp", ("fsdp", "ctx")),
            P("tp", ("fsdp", "ctx")),
            P(("fsdp", "ctx"), "tp"),
            P(("fsdp", "ctx"), "tp"),
            P("tp", ("fsdp", "ctx")),
            P(None, ("fsdp", "ctx"), "tp"),
            P("tp", ("fsdp", "ctx")),
            P(None, "tp"),
            P(("fsdp", "ctx")),
            P("tp", ("fsdp", "ctx")),
            P("tp", ("fsdp", "ctx")),
            P(("fsdp", "ctx"), "tp"),
            P(("fsdp", "ctx"), "tp"),
            P("tp", ("fsdp", "ctx")),
            P(None, ("fsdp", "ctx"), "tp"),
            P("tp", ("fsdp", "ctx")),
            P(None, "tp"),
            P(("fsdp", "ctx")),
        ),
        check_vma=False,
    )
```

profile of v0, /device:TPU:0, one launch (start us, length us, event | category | flops | bytes accessed | tf_op | source)
XLA Modules:
  0.0 1964.1 jit_solution(14916175286734529038)
XLA Ops:
  73.3 65.5 %all-reduce.14.cloned.1.call-done = bf16[1024,1056]{0,1:T(8,128)(2,1)} async-done(((bf16[1024,1056]{0,1:T(8,128)(2,1)}), bf16[1024,1056]{0,1:T(8,128)(2,1)}) %all-reduce.14.cloned.1.call-update) | async-done | bytes 2162704 | tf_op jit(solution)/shard_map/psum | solution.py:295
  178.0 116.0 %while.31 = (s32[]{:T(128)}, bf16[2,512,10,64]{1,3,2,0:T(8,128)(2,1)S(1)}, f32[2,10,512]{2,1,0:T(8,128)S(1)}, s32[2,512]{1,0:T(2,128)S(1)}, s32[2,512]{1,0:T(2,1...) while((s32[]{:T(128)}, ...), condition=%wide.region_8.9_spmd.clone.clone, body=%wide.region_5.8_spmd.clone.clone.sunk | while | flops 3485799424 | bytes 148975792 | solution.py:141
  180.1 19.2 fusion.167
  199.4 19.3 fusion.168
  218.7 17.3 fusion.169
  237.9 19.2 fusion.167
  257.2 19.3 fusion.168
  276.5 17.3 fusion.169
  313.8 93.0 %reduce-scatter.48.cloned.1.call-done = bf16[640,1024]{1,0:T(8,128)(2,1)} async-done(((bf16[2560,1024]{1,0:T(8,128)(2,1)}), bf16[640,1024]{1,0:T(8,128)(2,1)}) %reduce-scatter.48.cloned.1.call-update) | async-done | bytes 1310736
  428.7 89.7 %all-gather.13.cloned.1.call-done = bf16[1024,2560]{1,0:T(8,128)(2,1)} async-done(((bf16[1024,640]{1,0:T(8,128)(2,1)}), bf16[1024,2560]{1,0:T(8,128)(2,1)}) %all-gather.13.cloned.1.call-update) | async-done | bytes 5242896 | tf_op jit(solution)/shard_map/all_gather | solution.py:336
  518.4 91.9 %all-gather.15.cloned.1.call-done = bf16[2,2560,1600]{2,1,0:T(8,128)(2,1)} async-done(((bf16[2,320,1600]{2,1,0:T(8,128)(2,1)}), bf16[2,2560,1600]{2,1,0:T(8,128)(2,1)}) %all-gather.15.cloned.1.call-update) | async-done | bytes 16384016 | tf_op jit(solution)/shard_map/all_gather | solution.py:210
  639.8 27.9 %all-gather.17.cloned.1.call-done = bf16[1600,2560]{0,1:T(8,128)(2,1)} async-done(((bf16[1600,320]{0,1:T(8,128)(2,1)}), bf16[1600,2560]{0,1:T(8,128)(2,1)}) %all-gather.17.cloned.1.call-update) | async-done | bytes 8192016 | tf_op jit(solution)/shard_map/all_gather | solution.py:211
  667.7 22.0 %multiply_convert_fusion.2 = (bf16[1024,1600]{0,1:T(8,128)(2,1)}, bf16[1024,1600]{0,1:T(8,128)(2,1)}, bf16[1024,1600]{0,1:T(8,128)(2,1)}) fusion(f32[1024,1600]{0,1:T(8,128)} %fusion.48, f32[1024,1600]{0,1:T(8,128)} %fusion.50, bf16[1600,2560]{0,1:T(8,128)(2,1)} %all-gather.17.cloned.1.call-done, f32[1024]{0:T(1024)S(1)} %fusion.89, ...), kind=kOutput, calls=%fused_computation.74 | convolution fusion | flops 8425308160 | bytes 36376576 | tf_op jit(solution)/shard_map/dot_general | solution.py:82
  734.0 86.2 %reduce-scatter.52.cloned.1.call-done = bf16[640,1024]{1,0:T(8,128)(2,1)} async-done(((bf16[2560,1024]{1,0:T(8,128)(2,1)}), bf16[640,1024]{1,0:T(8,128)(2,1)}) %reduce-scatter.52.cloned.1.call-update) | async-done | bytes 1310736
  840.4 96.5 %all-gather.19.cloned.1.call-done = bf16[1024,2560]{1,0:T(8,128)(2,1)} async-done(((bf16[1024,640]{1,0:T(8,128)(2,1)}), bf16[1024,2560]{1,0:T(8,128)(2,1)}) %all-gather.19.cloned.1.call-update) | async-done | bytes 5242896 | tf_op jit(solution)/shard_map/all_gather | solution.py:370
  949.8 271.6 %while.32 = (s32[]{:T(128)}, f32[2048,10,96]{0,2,1:T(8,128)}, f32[2048,10,64]{0,2,1:T(8,128)}, f32[2,512,10,96]{1,0,3,2:T(2,128)}, bf16[2,512,10,96]{1,3,2,0:T(8...) while((s32[]{:T(128)}, f32[2048,10,96]{0,2,1:T(8,128)}, ...), condition=%wide.region_18.19_spmd.clone.clone.clone, body=%wide.region_16.18_spmd.clone.clone.clone.sunk | while | flops 8851559424 | bytes 266772752 | solution.py:199
  953.2 18.4 fusion.180
  971.6 20.4 %bitcast_add_fusion.5 = f32[2048,10,64]{0,2,1:T(8,128)} fusion(f32[2048,10,64]{0,2,1:T(8,128)} %get-tuple-element.939, f32[10,512,2048]{2,1,0:T(8,128)} %fusion.180, f32[10,512]{1,0:T(8,128)S(1)} %dynamic-slice_bitcast_fusion.3, pred[512,2048]{1,0:T(8,128)(4,1)S(1)} %compare_and_fusion.5, pred[]{:T(512)S(6)} %compare.5, ...), kind=kOutput, calls=%fused_computation.32.clone.1 | convolution fusion | flops 1386741760 | bytes 54153220 | tf_op jit(solution)/shard_map/while/body/eval_jaxpr/hqk,qhd->khd/dot_general | solution.py:78
  992.0 27.8 %multiply_convert_fusion.14 = bf16[10,512,2048]{2,1,0:T(8,128)(2,1)} fusion(f32[10,512,2048]{2,1,0:T(8,128)} %fusion.180, f32[10,512]{1,0:T(8,128)S(1)} %bitcast.240, f32[10,512]{1,0:T(8,128)S(1)} %dynamic-slice_bitcast_fusion.3, pred[512,2048]{1,0:T(8,128)(4,1)S(1)} %compare_and_fusion.5, bf16[2048,10,64]{0,2,1:T(8,128)(2,1)} %get-tuple-element.963, ...), kind=kOutput, calls=%fused_computation.26.clone.1 | convolution fusion | flops 1415577600 | bytes 67280896 | tf_op jit(solution)/shard_map/while/body/eval_jaxpr/qhd,khd->hqk/dot_general | solution.py:78
  1047.9 35.7 %dynamic_update_slice.26 = f32[2,512,10,96]{1,0,3,2:T(2,128)} dynamic-update-slice(f32[2,512,10,96]{1,0,3,2:T(2,128)} %get-tuple-element.940, f32[1,512,10,96]{1,0,3,2:T(1,128)S(1)} %copy.220, s32[]{:T(128)S(6)} %copy.238, s32[]{:T(128)} %constant.76.clone.1..sunk, s32[]{:T(128)} %constant.76.clone.1..sunk, s32[]{:T(128)} %constant.76.clone.1..sunk) | dynamic-update-slice | bytes 3932164 | tf_op jit(solution)/shard_map/while/body/jit(dynamic_update_index_in_dim)/dynamic_update_slice | solution.py:199
  1086.9 18.4 fusion.180
  1105.3 21.9 %bitcast_add_fusion.5 = f32[2048,10,64]{0,2,1:T(8,128)} fusion(f32[2048,10,64]{0,2,1:T(8,128)} %get-tuple-element.939, f32[10,512,2048]{2,1,0:T(8,128)} %fusion.180, f32[10,512]{1,0:T(8,128)S(1)} %dynamic-slice_bitcast_fusion.3, pred[512,2048]{1,0:T(8,128)(4,1)S(1)} %compare_and_fusion.5, pred[]{:T(512)S(6)} %compare.5, ...), kind=kOutput, calls=%fused_computation.32.clone.1 | convolution fusion | flops 1386741760 | bytes 54153220 | tf_op jit(solution)/shard_map/while/body/eval_jaxpr/hqk,qhd->khd/dot_general | solution.py:78
  1127.2 27.8 %multiply_convert_fusion.14 = bf16[10,512,2048]{2,1,0:T(8,128)(2,1)} fusion(f32[10,512,2048]{2,1,0:T(8,128)} %fusion.180, f32[10,512]{1,0:T(8,128)S(1)} %bitcast.240, f32[10,512]{1,0:T(8,128)S(1)} %dynamic-slice_bitcast_fusion.3, pred[512,2048]{1,0:T(8,128)(4,1)S(1)} %compare_and_fusion.5, bf16[2048,10,64]{0,2,1:T(8,128)(2,1)} %get-tuple-element.963, ...), kind=kOutput, calls=%fused_computation.26.clone.1 | convolution fusion | flops 1415577600 | bytes 67280896 | tf_op jit(solution)/shard_map/while/body/eval_jaxpr/qhd,khd->hqk/dot_general | solution.py:78
  1185.3 35.7 %dynamic_update_slice.26 = f32[2,512,10,96]{1,0,3,2:T(2,128)} dynamic-update-slice(f32[2,512,10,96]{1,0,3,2:T(2,128)} %get-tuple-element.940, f32[1,512,10,96]{1,0,3,2:T(1,128)S(1)} %copy.220, s32[]{:T(128)S(6)} %copy.238, s32[]{:T(128)} %constant.76.clone.1..sunk, s32[]{:T(128)} %constant.76.clone.1..sunk, s32[]{:T(128)} %constant.76.clone.1..sunk) | dynamic-update-slice | bytes 3932164 | tf_op jit(solution)/shard_map/while/body/jit(dynamic_update_index_in_dim)/dynamic_update_slice | solution.py:199
  1287.3 51.3 %all-reduce.16.cloned.1.call-done = bf16[1024,1056]{0,1:T(8,128)(2,1)} async-done(((bf16[1024,1056]{0,1:T(8,128)(2,1)}), bf16[1024,1056]{0,1:T(8,128)(2,1)}) %all-reduce.16.cloned.1.call-update) | async-done | bytes 2162704 | tf_op jit(solution)/shard_map/psum | solution.py:409
  1394.8 42.3 %copy.186 = bf16[2,2560,1600]{2,0,1:T(2,128)(2,1)} copy(bf16[2,2560,1600]{1,2,0:T(8,128)(2,1)} %pad_maximum_fusion) | data formatting | bytes 32768000
  1437.1 33.2 %reshape.429 = bf16[2560,3200]{1,0:T(8,128)(2,1)} reshape(bf16[2560,2,1600]{2,1,0:T(2,128)(2,1)} %bitcast.218) | data formatting | bytes 32768000
  1497.8 141.5 %reduce-scatter.58.cloned.1.call-done = bf16[640,3200]{1,0:T(8,128)(2,1)} async-done(((bf16[2560,3200]{1,0:T(8,128)(2,1)}), bf16[640,3200]{1,0:T(8,128)(2,1)}) %reduce-scatter.58.cloned.1.call-update) | async-done | bytes 4096016
  1669.1 66.1 %reduce-scatter.50.cloned.1.call-done = bf16[640,1024]{1,0:T(8,128)(2,1)} async-done(((bf16[2560,1024]{1,0:T(8,128)(2,1)}), bf16[640,1024]{1,0:T(8,128)(2,1)}) %reduce-scatter.50.cloned.1.call-update) | async-done | bytes 1310736
  1770.6 16.5 all-reduce.8
  1824.2 27.5 %all-reduce.18.cloned.1.call-done = bf16[2,640,1600]{2,0,1:T(2,128)(2,1)} async-done(((bf16[2,640,1600]{2,0,1:T(2,128)(2,1)}), bf16[2,640,1600]{2,0,1:T(2,128)(2,1)}) %all-reduce.18.cloned.1.call-update) | async-done | bytes 4096016
  1864.1 40.5 %psum.55 = f32[9]{0:T(128)S(1)} all-reduce(f32[9]{0:T(128)S(1)} %stack.69), channel_id=1, replica_groups=mesh['fsdp'=4,'ctx'=2,'tp'=4] {'fsdp','ctx','tp'}, use_global_device_ids=true, to_apply=%region_56.57 | all-reduce | flops 9 | bytes 72 | tf_op jit(solution)/shard_map/psum | solution.py:520
  (462 shorter events, 624.0 us)
Async XLA Ops:
  8.1 130.7 %all-reduce.14.cloned.1.call-start = ((), (), s32[]{:S(2)}) async-start(), calls=%async_computation.15 | async-start | bytes 4325376 | tf_op jit(solution)/shard_map/psum | solution.py:295
  52.3 95.9 %all-gather.9.cloned.1.call-start = ((), (), s32[]{:S(2)}) async-start(), calls=%async_computation.16 | async-start | bytes 1769472 | tf_op jit(solution)/shard_map/all_gather | solution.py:207
  53.1 243.7 %all-gather.11.cloned.1.call-start = ((), (), s32[]{:S(2)}) async-start(), calls=%async_computation.17 | async-start | bytes 3686400 | tf_op jit(solution)/shard_map/all_gather | solution.py:209
  54.3 352.6 %reduce-scatter.48.cloned.1.call-start = ((), (), s32[]{:S(2)}) async-start(), calls=%async_computation.29 | async-start | bytes 6553600
  143.0 5.1 collective-permute-start.1
  145.6 25.0 %collective-permute-start = (bf16[1024,256]{0,1:T(8,128)(2,1)S(1)}, bf16[1024,256]{0,1:T(8,128)(2,1)}, u32[]{:S(2)}, u32[]{:S(2)}) collective-permute-start(bf16[1024,256]{0,1:T(8,128)(2,1)S(1)} %multiply_convert_fusion.10), channel_id=1, source_target_pairs={{0,4},{1,5},{2,6},{3,7},{8,12},{9,13},{10,14},{11,15},{16,20},{17,... | collective-permute-start | bytes 1572872 | tf_op jit(solution)/shard_map/ppermute | solution.py:32
  313.8 204.6 %all-gather.13.cloned.1.call-start = ((), (), s32[]{:S(2)}) async-start(), calls=%async_computation.18 | async-start | bytes 6553600 | tf_op jit(solution)/shard_map/all_gather | solution.py:336
  408.6 428.0 %copy-start.6 = (bf16[1024,640]{1,0:T(8,128)(2,1)}, bf16[1024,640]{1,0:T(8,128)(2,1)S(1)}, u32[]{:S(2)}) copy-start(bf16[1024,640]{1,0:T(8,128)(2,1)S(1)} %copy.177) | copy-start | bytes 3932164
  420.1 416.5 %copy-start.50 = (f32[1024]{0:T(1024)}, f32[1024]{0:T(1024)S(1)}, u32[]{:S(2)}) copy-start(f32[1024]{0:T(1024)S(1)} %get-tuple-element.707) | copy-start | bytes 12292
  420.1 416.5 %copy-start.55 = (f32[1024]{0:T(1024)}, f32[1024]{0:T(1024)S(1)}, u32[]{:S(2)}) copy-start(f32[1024]{0:T(1024)S(1)} %get-tuple-element.706) | copy-start | bytes 12292
  421.8 188.5 %all-gather.15.cloned.1.call-start = ((), (), s32[]{:S(2)}) async-start(), calls=%async_computation.19 | async-start | bytes 19169280 | tf_op jit(solution)/shard_map/all_gather | solution.py:210
  425.6 242.1 %all-gather.17.cloned.1.call-start = ((), (), s32[]{:S(2)}) async-start(), calls=%async_computation.20 | async-start | bytes 9584640 | tf_op jit(solution)/shard_map/all_gather | solution.py:211
  428.6 391.5 %reduce-scatter.52.cloned.1.call-start = ((), (), s32[]{:S(2)}) async-start(), calls=%async_computation.31 | async-start | bytes 6553600
  726.2 210.7 %all-gather.19.cloned.1.call-start = ((), (), s32[]{:S(2)}) async-start(), calls=%async_computation.21 | async-start | bytes 6553600 | tf_op jit(solution)/shard_map/all_gather | solution.py:370
  840.3 498.3 %all-reduce.16.cloned.1.call-start = ((), (), s32[]{:S(2)}) async-start(), calls=%async_computation.22 | async-start | bytes 4325376 | tf_op jit(solution)/shard_map/psum | solution.py:409
  1235.9 12.5 collective-permute-start.3
  1243.3 5.2 collective-permute-start.2
  1250.3 243.3 %reduce-scatter.44.cloned.1.call-start = ((), (), s32[]{:S(2)}) async-start(), calls=%async_computation.27 | async-start | bytes 819200 | tf_op jit(solution)/shard_map/reduce_scatter | solution.py:443
  1255.4 238.9 %reduce-scatter.60.cloned.1.call-start = ((), (), s32[]{:S(2)}) async-start(), calls=%async_computation.35 | async-start | bytes 10649600
  1281.7 214.0 %reduce-scatter.40.cloned.1.call-start = ((), (), s32[]{:S(2)}) async-start(), calls=%async_computation.25 | async-start | bytes 1966080 | tf_op jit(solution)/shard_map/reduce_scatter | solution.py:440
  1287.2 209.1 %reduce-scatter.36.cloned.1.call-start = ((), (), s32[]{:S(2)}) async-start(), calls=%async_computation.23 | async-start | bytes 1228800 | tf_op jit(solution)/shard_map/reduce_scatter | solution.py:434
  1349.9 147.1 %reduce-scatter.54.cloned.1.call-start = ((), (), s32[]{:S(2)}) async-start(), calls=%async_computation.32 | async-start | bytes 4096000
  1364.3 274.9 %reduce-scatter.58.cloned.1.call-start = ((), (), s32[]{:S(2)}) async-start(), calls=%async_computation.34 | async-start | bytes 20480000
  1470.3 264.8 %reduce-scatter.50.cloned.1.call-start = ((), (), s32[]{:S(2)}) async-start(), calls=%async_computation.30 | async-start | bytes 6553600
  1493.5 252.0 %reduce-scatter.46.cloned.1.call-start = ((), (), s32[]{:S(2)}) async-start(), calls=%async_computation.28 | async-start | bytes 245760 | tf_op jit(solution)/shard_map/reduce_scatter | solution.py:472
  1494.2 264.1 %reduce-scatter.62.cloned.1.call-start = ((), (), s32[]{:S(2)}) async-start(), calls=%async_computation.36 | async-start | bytes 3194880
  1494.8 313.1 %reduce-scatter.64.cloned.1.call-start = ((), (), s32[]{:S(2)}) async-start(), calls=%async_computation.38 | async-start | bytes 460800
  1495.6 321.9 %reduce-scatter.42.cloned.1.call-start = ((), (), s32[]{:S(2)}) async-start(), calls=%async_computation.26 | async-start | bytes 589824 | tf_op jit(solution)/shard_map/reduce_scatter | solution.py:469
  1496.2 323.6 %reduce-scatter.38.cloned.1.call-start = ((), (), s32[]{:S(2)}) async-start(), calls=%async_computation.24 | async-start | bytes 368640 | tf_op jit(solution)/shard_map/reduce_scatter | solution.py:463
  1497.0 325.1 %reduce-scatter.56.cloned.1.call-start = ((), (), s32[]{:S(2)}) async-start(), calls=%async_computation.33 | async-start | bytes 1228800
  1497.7 354.0 %all-reduce.18.cloned.1.call-start = ((), (), s32[]{:S(2)}) async-start(), calls=%async_computation.37 | async-start | bytes 8519680
  1811.5 4.2 collective-permute-start.4
  (90 other events, 2089.0 us)
Sparse Core Ops, SparseCore 0:
  52.4 86.3 all-reduce.13
  313.9 92.9 reduce-scatter.47
  421.9 96.4 all-gather.12
  520.9 89.3 all-gather.14
  612.8 54.9 all-gather.16
  726.4 93.7 reduce-scatter.51
  840.5 96.4 all-gather.18
  1250.4 88.1 all-reduce.15
Sparse Core Ops, SparseCore 1:
  55.4 23.6 all-gather.8
  81.5 32.7 all-gather.10
  1255.5 24.5 reduce-scatter.43
  1283.5 87.3 reduce-scatter.59
  1374.7 30.8 reduce-scatter.39
  1409.5 27.2 reduce-scatter.35
  1440.5 44.8 reduce-scatter.53
  1488.8 150.5 reduce-scatter.57
  1641.5 93.6 reduce-scatter.49
  1737.4 8.0 reduce-scatter.45
  1747.6 10.7 reduce-scatter.61
  1761.8 25.0 reduce-scatter.63
  1789.0 7.7 reduce-scatter.41
  1799.0 8.7 reduce-scatter.37
  1810.1 9.4 reduce-scatter.55
  1822.6 29.0 all-reduce.17
where the time goes:
time: 1980 us; the launch traced here: 1960 us
  waiting for transfers between devices  859 us (43%)
  matrix products  451 us (23%)
  local copies, waits for them, and re-layouts  296 us (15%)
  other arithmetic  169 us (9%)
  blocking collectives  149 us (8%)
  between operations  29.4 us (1%)
    unnamed x35, waiting for transfers between devices  428 us
    dot_general x14, matrix products, product(): jnp.einsum(spec, left_side, right_side, preferred_element_type=jnp.float32)  262 us
    unnamed x212, local copies, waits for them, and re-layouts  185 us
    all_gather x1, waiting for transfers between devices, local(): seed_full = lax.all_gather(attn_seed, 'tp', axis=1, tiled=True)  96.5 us
    all_gather x1, waiting for transfers between devices, collect_weights(): lax.all_gather(shards[5], ('fsdp', 'ctx'), axis=1, tiled=True)  91.9 us
    all_gather x1, waiting for transfers between devices, local(): normed_full = lax.all_gather(normed_two, 'tp', axis=1, tiled=True)  89.7 us
    dynamic_update_slice x4, local copies, waits for them, and re-layouts, attend_backward(): (key_sum, value_sum), d_queries = lax.scan(one_block, initial, pieces)  75.5 us
    dot_general x7, matrix products, contract_last(): lax.dot_general(left_side, right_side, (((1,), (1,)), ((), ())), preferre...  67.4 us
  transfers between devices with their start and end apart: 29, of which 13 were waited for; matrix products, arithmetic and copies ran while one was open for 23% of the time, Pallas kernels for 0%

commit v1 on v0

v1 whole, which is shorter than its diff:
```python
import functools

import jax
import jax.numpy as jnp
from jax import lax
from jax.experimental import pallas as pl
from jax.experimental.pallas import tpu as pltpu
from jax.sharding import PartitionSpec as P

D = 2560
H = 40
NOPE = 64
ROPE = 32
VD = 64
QR = 768
KVR = 256
FF = 6400
STEP = 3
HEAD = NOPE + ROPE
LAT = QR + KVR + ROPE

EPS_NORM = 1e-05
RESIDUAL_SCALE = 1.4 / 62**0.5
ROPE_BASE = 10000.0
MASK_VALUE = -1e30
BETA_ONE = 0.9
BETA_TWO = 0.95
ADAM_EPS = 1e-08
LEARN_RATE = 0.1
WEIGHT_DECAY = 0.1
CLIP_RMS = 0.0002
LOG2E = 1.4426950408889634
LN2 = 0.6931471805599453

BF = jnp.bfloat16
F32 = jnp.float32
MESH = pl.DeviceIdType.MESH
MIB = 1024 * 1024


def dot_nn(a, b):
    return lax.dot_general(a, b, (((1,), (0,)), ((), ())), preferred_element_type=F32)


def dot_nt(a, b):
    return lax.dot_general(a, b, (((1,), (1,)), ((), ())), preferred_element_type=F32)


def dot_tn(a, b):
    return lax.dot_general(a, b, (((0,), (0,)), ((), ())), preferred_element_type=F32)


def line_reduce_kernel(chunks, x_ref, o_ref, near, cross, part, in_send, in_recv, mid_send, mid_recv, out_send, out_recv):
    z = lax.axis_index("tp")
    rows = x_ref.shape[0] // chunks
    is_end = jnp.logical_or(z == 0, z == 3)
    is_mid = jnp.logical_not(is_end)
    partner = jnp.where(z == 0, 1, jnp.where(z == 3, 2, jnp.where(z == 1, 0, 3)))
    across = jnp.where(z == 1, 2, 1)

    barrier = pltpu.get_barrier_semaphore()
    pl.semaphore_signal(barrier, inc=1, device_id={"tp": partner}, device_id_type=MESH)

    @pl.when(is_mid)
    def _():
        pl.semaphore_signal(barrier, inc=1, device_id={"tp": across}, device_id_type=MESH)
        pl.semaphore_wait(barrier, 2)

    @pl.when(is_end)
    def _():
        pl.semaphore_wait(barrier, 1)

    def piece(k):
        return pl.ds(pl.multiple_of(k * rows, rows), rows)

    def to_mid(k):
        return pltpu.make_async_remote_copy(
            src_ref=x_ref.at[piece(k)], dst_ref=near.at[piece(k)], send_sem=in_send.at[k], recv_sem=in_recv.at[k],
            device_id={"tp": partner}, device_id_type=MESH,
        )

    def over(k):
        return pltpu.make_async_remote_copy(
            src_ref=part.at[piece(k)], dst_ref=cross.at[piece(k)], send_sem=mid_send.at[k], recv_sem=mid_recv.at[k],
            device_id={"tp": across}, device_id_type=MESH,
        )

    def to_end(k):
        return pltpu.make_async_remote_copy(
            src_ref=o_ref.at[piece(k)], dst_ref=o_ref.at[piece(k)], send_sem=out_send.at[k], recv_sem=out_recv.at[k],
            device_id={"tp": partner}, device_id_type=MESH,
        )

    @pl.when(is_end)
    def _():
        def begin(k, carry):
            to_mid(k).start()
            return carry

        def finish(k, carry):
            to_mid(k).wait_send()
            to_end(k).wait_recv()
            return carry

        lax.fori_loop(0, chunks, begin, 0)
        lax.fori_loop(0, chunks, finish, 0)

    @pl.when(is_mid)
    def _():
        def first(k):
            to_mid(k).wait_recv()
            part[piece(k)] = (x_ref[piece(k)].astype(F32) + near[piece(k)].astype(F32)).astype(BF)
            over(k).start()

        def second(k):
            over(k).wait_recv()
            o_ref[piece(k)] = (part[piece(k)].astype(F32) + cross[piece(k)].astype(F32)).astype(BF)
            to_end(k).start()

        first(0)

        def step(k, carry):
            first(k)
            second(k - 1)
            return carry

        lax.fori_loop(1, chunks, step, 0)
        second(chunks - 1)

        def finish(k, carry):
            over(k).wait_send()
            to_end(k).wait_send()
            return carry

        lax.fori_loop(0, chunks, finish, 0)


def line_reduce(x, chunks, collective_id):
    if lax.axis_size("tp") != 4:
        return lax.psum(x, "tp")
    rows, cols = x.shape
    dma = pltpu.SemaphoreType.DMA((chunks,))
    return pl.pallas_call(
        functools.partial(line_reduce_kernel, chunks),
        out_shape=jax.ShapeDtypeStruct((rows, cols), BF),
        in_specs=[pl.BlockSpec(memory_space=pltpu.VMEM)],
        out_specs=pl.BlockSpec(memory_space=pltpu.VMEM),
        scratch_shapes=[pltpu.VMEM((rows, cols), BF)] * 3 + [dma] * 6,
        compiler_params=pltpu.CompilerParams(
            collective_id=collective_id, has_side_effects=True, vmem_limit_bytes=40 * MIB
        ),
        cost_estimate=pl.CostEstimate(flops=rows * cols * 2, bytes_accessed=rows * cols * 40, transcendentals=0),
        name="line_reduce",
    )(x)


BQ = 512


def attend_forward_kernel(
    qn_ref, kn_ref, krx_ref, cos_ref, sin_ref, segq_ref, wq_ref, wk_ref, wv_ref, o_ref, lse_ref, q_ref, k_ref, v_ref
):
    i = pl.program_id(1)
    rows = qn_ref.shape[0]

    @pl.when(i == 0)
    def _():
        for r in range(rows // BQ):
            part = pl.ds(r * BQ, BQ)
            qf = dot_nt(wq_ref[0], qn_ref[part, :]) * (LOG2E * HEAD**-0.5)
            cos = cos_ref[:, part]
            sin = sin_ref[:, part]
            one, two = qf[NOPE : NOPE + 16], qf[NOPE + 16 : HEAD]
            q_ref[0, 0:NOPE, part] = qf[:NOPE].astype(BF)
            q_ref[0, NOPE : NOPE + 16, part] = (one * cos - two * sin).astype(BF)
            q_ref[0, NOPE + 16 : HEAD, part] = (two * cos + one * sin).astype(BF)
            q_ref[0, HEAD : HEAD + 16, part] = segq_ref[:, part]
            q_ref[0, HEAD + 16 : 128, part] = jnp.zeros((16, BQ), BF)
            k_ref[0, part, :] = (dot_nn(kn_ref[part, :], wk_ref[0]) + krx_ref[part, :].astype(F32)).astype(BF)
            vt = dot_nt(wv_ref[0], kn_ref[part, :])
            row = lax.broadcasted_iota(jnp.int32, vt.shape, 0)
            v_ref[0, :, part] = jnp.where(row == VD, 1.0, vt).astype(BF)

    here = pl.ds(pl.multiple_of(i * BQ, BQ), BQ)
    q = q_ref[0, :, here]

    def block(j, carried, masked):
        m, acc = carried
        there = pl.ds(pl.multiple_of(j * BQ, BQ), BQ)
        s = dot_nn(k_ref[0, there, :], q)
        if masked:
            krow = lax.broadcasted_iota(jnp.int32, s.shape, 0)
            qcol = lax.broadcasted_iota(jnp.int32, s.shape, 1)
            s = jnp.where(krow <= qcol, s, MASK_VALUE)
        top = jnp.maximum(m, jnp.max(s, axis=0, keepdims=True))
        p = jnp.exp2(s - top).astype(BF)
        acc = acc * jnp.exp2(m - top) + dot_nn(v_ref[0, :, there], p)
        return top, acc

    start = (jnp.full((1, BQ), -3e38, F32), jnp.zeros((80, BQ), F32))
    carried = lax.fori_loop(0, i, lambda j, c: block(j, c, False), start)
    m, acc = block(i, carried, True)
    total = acc[VD : VD + 1]
    o_ref[0, :, here] = (acc[:VD] / total).astype(BF)
    lse_ref[0, :, here] = m + jnp.log2(total)


def attend_forward(qn, kn, krx, cos, sin, segq, wq, wk, wv):
    heads = wq.shape[0]
    rows = qn.shape[0]
    whole = lambda a: pl.BlockSpec(a.shape, lambda h, i: (0,) * a.ndim)
    per_head = lambda a, b: pl.BlockSpec((1, a, b), lambda h, i: (h, 0, 0))
    return pl.pallas_call(
        attend_forward_kernel,
        grid=(heads, rows // BQ),
        in_specs=[whole(qn), whole(kn), whole(krx), whole(cos), whole(sin), whole(segq)]
        + [per_head(*w.shape[1:]) for w in (wq, wk, wv)],
        out_specs=[per_head(VD, rows), per_head(1, rows), per_head(128, rows), per_head(rows, 128), per_head(80, rows)],
        out_shape=[
            jax.ShapeDtypeStruct((heads, VD, rows), BF),
            jax.ShapeDtypeStruct((heads, 1, rows), F32),
            jax.ShapeDtypeStruct((heads, 128, rows), BF),
            jax.ShapeDtypeStruct((heads, rows, 128), BF),
            jax.ShapeDtypeStruct((heads, 80, rows), BF),
        ],
        compiler_params=pltpu.CompilerParams(vmem_limit_bytes=40 * MIB),
        cost_estimate=pl.CostEstimate(flops=heads * rows * rows * 320, bytes_accessed=30 * MIB, transcendentals=0),
        name="attend_forward",
    )(qn, kn, krx, cos, sin, segq, wq, wk, wv)


def attend_backward_kernel(q_ref, k_ref, v_ref, o_ref, do_ref, lse_ref, cos_ref, sin_ref, dq_ref, de_ref, dkr_ref, dq_acc, delta):
    h, j = pl.program_id(0), pl.program_id(1)
    rows = k_ref.shape[1]
    blocks = rows // BQ

    @pl.when(j == 0)
    def _():
        dq_acc[...] = jnp.zeros_like(dq_acc)
        delta[...] = jnp.sum(o_ref[0].astype(F32) * do_ref[0].astype(F32), axis=0, keepdims=True)

    there = pl.ds(pl.multiple_of(j * BQ, BQ), BQ)
    k = k_ref[0, there, :]
    kt = k.astype(F32).T.astype(BF)
    v = v_ref[0, 0:VD, there].astype(F32).T.astype(BF)

    def block(i, carried, masked):
        dk, dv = carried
        here = pl.ds(pl.multiple_of(i * BQ, BQ), BQ)
        q = q_ref[0, :, here]
        do = do_ref[0, :, here]
        s = dot_nn(k, q)
        if masked:
            krow = lax.broadcasted_iota(jnp.int32, s.shape, 0)
            qcol = lax.broadcasted_iota(jnp.int32, s.shape, 1)
            s = jnp.where(krow <= qcol, s, MASK_VALUE)
        p = jnp.exp2(s - lse_ref[0, :, here])
        dp = dot_nn(v, do)
        ds = (p * (dp - delta[:, here])).astype(BF)
        dv = dv + dot_nt(p.astype(BF), do)
        dk = dk + dot_nt(ds, q)
        dq_acc[:, here] = dq_acc[:, here] + dot_nn(kt, ds)
        return dk, dv

    start = (jnp.zeros((BQ, 128), F32), jnp.zeros((BQ, VD), F32))
    carried = block(j, start, True)
    dk, dv = lax.fori_loop(j + 1, blocks, lambda i, c: block(i, c, False), carried)
    dk = dk * LN2
    de_ref[there, 0:NOPE] = dk[:, :NOPE].astype(BF)
    de_ref[there, NOPE:128] = dv.astype(BF)

    @pl.when(h == 0)
    def _():
        dkr_ref[there, :] = dk

    @pl.when(h > 0)
    def _():
        dkr_ref[there, :] = dkr_ref[there, :] + dk

    @pl.when(j == blocks - 1)
    def _():
        dq = dq_acc[...] * HEAD**-0.5
        cos, sin = cos_ref[...], sin_ref[...]
        one, two = dq[NOPE : NOPE + 16], dq[NOPE + 16 : HEAD]
        dq_ref[0:NOPE, :] = dq[:NOPE].astype(BF)
        dq_ref[NOPE : NOPE + 16, :] = (one * cos + two * sin).astype(BF)
        dq_ref[NOPE + 16 : HEAD, :] = (two * cos - one * sin).astype(BF)


def attend_backward(q, k, v, o, do, lse, cos, sin):
    heads = q.shape[0]
    rows = k.shape[1]
    whole = lambda a: pl.BlockSpec(a.shape, lambda h, i: (0,) * a.ndim)
    per_head = lambda a: pl.BlockSpec((1,) + a.shape[1:], lambda h, i: (h, 0, 0))
    return pl.pallas_call(
        attend_backward_kernel,
        grid=(heads, rows // BQ),
        in_specs=[per_head(a) for a in (q, k, v, o, do, lse)] + [whole(cos), whole(sin)],
        out_specs=[
            pl.BlockSpec((HEAD, rows), lambda h, i: (h, 0)),
            pl.BlockSpec((rows, 128), lambda h, i: (0, h)),
            pl.BlockSpec((rows, 128), lambda h, i: (0, 0)),
        ],
        out_shape=[
            jax.ShapeDtypeStruct((heads * HEAD, rows), BF),
            jax.ShapeDtypeStruct((rows, heads * 128), BF),
            jax.ShapeDtypeStruct((rows, 128), F32),
        ],
        scratch_shapes=[pltpu.VMEM((128, rows), F32), pltpu.VMEM((1, rows), F32)],
        compiler_params=pltpu.CompilerParams(vmem_limit_bytes=40 * MIB),
        cost_estimate=pl.CostEstimate(flops=heads * rows * rows * 900, bytes_accessed=30 * MIB, transcendentals=0),
        name="attend_backward",
    )(q, k, v, o, do, lse, cos, sin)


LINE = 32
MLP_ROWS = 256
TILES = ((0, 384), (384, 384), (768, 384), (1152, 448))


def line_places(z):
    is_end = jnp.logical_or(z == 0, z == 3)
    partner = jnp.where(z == 0, 1, jnp.where(z == 3, 2, jnp.where(z == 1, 0, 3)))
    return is_end, jnp.logical_not(is_end), partner, jnp.where(z == 1, 2, 1)


def line_barrier(is_mid, is_end, partner, across):
    barrier = pltpu.get_barrier_semaphore()
    pl.semaphore_signal(barrier, inc=1, device_id={"tp": partner}, device_id_type=MESH)

    @pl.when(is_mid)
    def _():
        pl.semaphore_signal(barrier, inc=1, device_id={"tp": across}, device_id_type=MESH)
        pl.semaphore_wait(barrier, 2)

    @pl.when(is_end)
    def _():
        pl.semaphore_wait(barrier, 1)


def line_copies(source, near, cross, total, sems, partner, across):
    in_send, in_recv, mid_send, mid_recv, out_send, out_recv = sems

    def piece(k):
        return pl.ds(pl.multiple_of(k * LINE, LINE), LINE)

    def copy(src, dst, send, recv, k, to):
        return pltpu.make_async_remote_copy(
            src_ref=src.at[piece(k)], dst_ref=dst.at[piece(k)], send_sem=send.at[k], recv_sem=recv.at[k],
            device_id={"tp": to}, device_id_type=MESH,
        )

    to_mid = lambda k: copy(source, near, in_send, in_recv, k, partner)
    over = lambda k: copy(near, cross, mid_send, mid_recv, k, across)
    to_end = lambda k: copy(total, total, out_send, out_recv, k, partner)

    def first(k):
        to_mid(k).wait_recv()
        near[piece(k)] = (source[piece(k)].astype(F32) + near[piece(k)].astype(F32)).astype(BF)
        over(k).start()

    def second(k):
        over(k).wait_recv()
        total[piece(k)] = (near[piece(k)].astype(F32) + cross[piece(k)].astype(F32)).astype(BF)
        to_end(k).start()

    return to_mid, over, to_end, first, second


def each(count, body):
    def step(k, carry):
        body(k)
        return carry

    lax.fori_loop(0, count, step, 0)


def block_kernel(
    att_ref, x_ref, out_ref, gain_ref, seed_any, gu_any, down_any,
    hid_any, dn_any, mo_any, n2t_any, act_any, dg_any, du_any,
    xb, near, cross, total, gu, down, n2, n2t, seed, act, dg, du,
    load_sem, seed_sem, hid_sem, dn_sem, mo_sem, n2t_sem, act_sem, dg_sem, du_sem, *sems,
):
    z = lax.axis_index("tp")
    is_end, is_mid, partner, across = line_places(z)
    to_mid, over, to_end, first, second = line_copies(xb, near, cross, total, sems, partner, across)
    count = xb.shape[0] // LINE
    group = MLP_ROWS // LINE
    groups = count // group
    width = x_ref.shape[1]

    def rows_of(m):
        return pl.ds(pl.multiple_of(m * MLP_ROWS, MLP_ROWS), MLP_ROWS)

    load_gu = pltpu.make_async_copy(gu_any, gu, load_sem.at[0])
    load_down = pltpu.make_async_copy(down_any, down, load_sem.at[1])
    load_seed = lambda m: pltpu.make_async_copy(seed_any.at[rows_of(m)], seed, seed_sem.at[m])
    save_hid = lambda m: pltpu.make_async_copy(total.at[rows_of(m)], hid_any.at[rows_of(m)], hid_sem.at[m])
    save_dn = lambda m: pltpu.make_async_copy(xb.at[rows_of(m)], dn_any.at[rows_of(m)], dn_sem.at[m])
    save_mo = lambda m: pltpu.make_async_copy(cross.at[rows_of(m)], mo_any.at[rows_of(m)], mo_sem.at[m])
    save_n2t = lambda m: pltpu.make_async_copy(n2t, n2t_any.at[:, rows_of(m)], n2t_sem.at[m])
    save_act = lambda m: pltpu.make_async_copy(act, act_any.at[rows_of(m)], act_sem.at[m])
    save_dg = lambda m: pltpu.make_async_copy(dg, dg_any.at[rows_of(m)], dg_sem.at[m])
    save_du = lambda m: pltpu.make_async_copy(du, du_any.at[rows_of(m)], du_sem.at[m])

    load_seed(0).start()
    load_gu.start()
    load_down.start()
    line_barrier(is_mid, is_end, partner, across)

    mine = pl.ds(pl.multiple_of(z * width, 128), width)
    per = 128

    def project(p):
        rows = pl.ds(pl.multiple_of(p * per, per), per)
        part = dot_nt(att_ref[rows, :], out_ref[...]) * RESIDUAL_SCALE
        xb[rows, :] = part.astype(BF)
        xb[rows, mine] = (xb[rows, mine].astype(F32) + x_ref[rows, :].astype(F32)).astype(BF)

        @pl.when(is_end)
        def _():
            for n in range(per // LINE):
                to_mid(p * (per // LINE) + n).start()

    each(xb.shape[0] // per, project)

    @pl.when(is_mid)
    def _():
        first(0)

        def both(k):
            first(k + 1)
            second(k)

        each(group, both)

    def mlp(m):
        rows = rows_of(m)

        @pl.when(is_end)
        def _():
            def arrive(n):
                to_mid(m * group + n).wait_send()
                to_end(m * group + n).wait_recv()

            each(group, arrive)

        def serve(n):
            k = (m + 1) * group + 1 + n

            @pl.when(jnp.logical_and(is_mid, k < count))
            def _():
                first(k)

            @pl.when(jnp.logical_and(is_mid, k <= count))
            def _():
                second(k - 1)

        save_hid(m).start()

        @pl.when(m > 0)
        def _():
            save_n2t(m - 1).wait()
            save_act(m - 1).wait()
            save_dg(m - 1).wait()
            save_du(m - 1).wait()

        def normalize(r):
            here = pl.ds(pl.multiple_of(r * 32, 32), 32)
            h = total[pl.ds(pl.multiple_of(m * MLP_ROWS + r * 32, 32), 32), :].astype(F32)
            factor = lax.rsqrt(jnp.mean(h * h, axis=1, keepdims=True) + EPS_NORM)
            n2[here, :] = (h * factor * gain_ref[...]).astype(BF)

        each(MLP_ROWS // 32, normalize)

        def turn(c):
            cols = pl.ds(pl.multiple_of(c * 256, 256), 256)
            n2t[cols, :] = n2[:, cols].astype(F32).T.astype(BF)

        each(D // 256, turn)
        save_n2t(m).start()
        load_seed(m).wait()

        @pl.when(m == 0)
        def _():
            load_gu.wait()
            load_down.wait()

        for t, (at, size) in enumerate(TILES):
            cols = pl.ds(at, size)
            g = dot_nn(n2[...], gu[0, :, cols])
            u = dot_nn(n2[...], gu[1, :, cols])
            d = dot_nn(seed[...], down[:, cols])
            sig = jax.nn.sigmoid(g)
            act[:, cols] = (g * sig * u).astype(BF)
            dg[:, cols] = (d * u * sig * (1.0 + g * (1.0 - sig))).astype(BF)
            du[:, cols] = (d * g * sig).astype(BF)
            serve(t)
        save_act(m).start()
        save_dg(m).start()
        save_du(m).start()

        @pl.when(m + 1 < groups)
        def _():
            load_seed(m + 1).start()

        for n in range(4):
            cols = pl.ds(n * 640, 640)
            xb[rows, cols] = (dot_nt(dg[...], gu[0, cols, :]) + dot_nt(du[...], gu[1, cols, :])).astype(BF)
            cross[rows, cols] = dot_nt(act[...], down[cols, :]).astype(BF)
            serve(4 + n)
        save_dn(m).start()
        save_mo(m).start()

    each(groups, mlp)

    def finish(m):
        save_hid(m).wait()
        save_dn(m).wait()
        save_mo(m).wait()

    each(groups, finish)
    save_n2t(groups - 1).wait()
    save_act(groups - 1).wait()
    save_dg(groups - 1).wait()
    save_du(groups - 1).wait()

    @pl.when(is_mid)
    def _():
        def sent(k):
            over(k).wait_send()
            to_end(k).wait_send()

        each(count, sent)


def block_forward(att, x, out_t, gain, seed, gate_up, down_t):
    rows = att.shape[0]
    hidden_units = down_t.shape[1]
    count, groups = rows // LINE, rows // MLP_ROWS
    vmem = pl.BlockSpec(memory_space=pltpu.VMEM)
    anywhere = pl.BlockSpec(memory_space=pl.ANY)
    wide = jax.ShapeDtypeStruct((rows, D), BF)
    units = jax.ShapeDtypeStruct((rows, hidden_units), BF)
    dma = pltpu.SemaphoreType.DMA
    return pl.pallas_call(
        block_kernel,
        out_shape=[wide, wide, wide, jax.ShapeDtypeStruct((D, rows), BF), units, units, units],
        in_specs=[vmem] * 4 + [anywhere] * 3,
        out_specs=[anywhere] * 7,
        scratch_shapes=[pltpu.VMEM((rows, D), BF)] * 4
        + [
            pltpu.VMEM(gate_up.shape, BF),
            pltpu.VMEM(down_t.shape, BF),
            pltpu.VMEM((MLP_ROWS, D), BF),
            pltpu.VMEM((D, MLP_ROWS), BF),
            pltpu.VMEM((MLP_ROWS, D), BF),
        ]
        + [pltpu.VMEM((MLP_ROWS, hidden_units), BF)] * 3
        + [dma((2,))]
        + [dma((groups,))] * 8
        + [dma((count,))] * 6,
        compiler_params=pltpu.CompilerParams(collective_id=3, has_side_effects=True, vmem_limit_bytes=63 * MIB),
        cost_estimate=pl.CostEstimate(flops=rows * D * hidden_units * 12, bytes_accessed=400 * MIB, transcendentals=0),
        name="block_forward",
    )(att, x, out_t, gain, seed, gate_up, down_t)


def swap_cores(v):
    return lax.ppermute(v, "ctx", [(0, 1), (1, 0)])


def in_core_order(mine, other, core, axis):
    return jnp.where(
        core == 0, jnp.concatenate([mine, other], axis=axis), jnp.concatenate([other, mine], axis=axis)
    )


def gather_shards(v):
    return lax.all_gather(v, ("fsdp", "ctx"), axis=0, tiled=True)


X_SWAP = [(0, 1), (1, 0), (2, 3), (3, 2)]
Y_SWAP = [(0, 2), (2, 0), (1, 3), (3, 1)]


def take(v, which, axis):
    return lax.dynamic_index_in_dim(v, which, axis, keepdims=False)


def add_up(a, b):
    return (a.astype(F32) + b.astype(F32)).astype(BF)


def keep_half(v, axis, which, name, pairs):
    other = lax.ppermute(take(v, 1 - which, axis), name, pairs)
    return add_up(take(v, which, axis), other)


def scatter_fsdp(v):
    if lax.axis_size("fsdp") != 4:
        return lax.psum_scatter(v, "fsdp", scatter_dimension=0, tiled=False)
    place = lax.axis_index("fsdp")
    y, x = place // 2, place % 2
    _, rows, cols = v.shape
    v = v.reshape(2, 2, 2, rows // 2, cols)
    first = keep_half(v[:, :, 0], 1, x, "fsdp", X_SWAP)
    second = keep_half(v[:, :, 1], 0, y, "fsdp", Y_SWAP)
    first = keep_half(first, 0, y, "fsdp", Y_SWAP)
    second = keep_half(second, 0, x, "fsdp", X_SWAP)
    return jnp.concatenate([first, second], axis=0)


def scatter_grads(v):
    fsdp, ctx = lax.axis_size("fsdp"), lax.axis_size("ctx")
    rows, cols = v.shape
    v = v.reshape(fsdp, ctx, rows // (fsdp * ctx), cols)
    return scatter_fsdp(keep_half(v, 1, lax.axis_index("ctx"), "ctx", [(0, 1), (1, 0)]))


def split_two(v):
    high = v.astype(BF)
    return high, (v - high.astype(F32)).astype(BF)


def adamw_update(parameter, gradient, first_moment, second_moment, decay_rate):
    first_new = BETA_ONE * first_moment + (1.0 - BETA_ONE) * gradient
    second_new = BETA_TWO * second_moment + (1.0 - BETA_TWO) * gradient * gradient
    first_hat = first_new / (1.0 - BETA_ONE**STEP)
    second_hat = second_new / (1.0 - BETA_TWO**STEP)
    updated = parameter - LEARN_RATE * (
        first_hat / (jnp.sqrt(second_hat) + ADAM_EPS) + decay_rate * parameter
    )
    return (updated, first_new, second_new)


def norm_backward(incoming, values, factor, gain):
    scaled = incoming * gain
    gain_grad = jnp.sum(incoming * values * factor, axis=0)
    result = factor * scaled - values * factor**3 * jnp.mean(scaled * values, axis=1, keepdims=True)
    return (result, gain_grad)


def local(*args):
    tokens, cotangent, lengths = args[:3]
    params, firsts, seconds = args[3:12], args[12:21], args[21:30]
    w_qdown, w_kvdown, w_qup, w_kvup, w_out, w_gateup, w_down, g_norms, g_latent = params
    n_tp, n_ctx, n_fsdp = lax.axis_size("tp"), lax.axis_size("ctx"), lax.axis_size("fsdp")
    tp, core = lax.axis_index("tp"), lax.axis_index("ctx")
    rows, width = tokens.shape
    slot = rows * n_ctx
    heads_all = H // n_tp
    by_head = heads_all % n_ctx == 0
    heads = heads_all // n_ctx if by_head else heads_all

    down_t = jnp.concatenate(
        [gather_shards(w_qdown.T.astype(BF)), gather_shards(w_kvdown.T.astype(BF))], axis=0
    )
    q_up = gather_shards(w_qup.astype(BF))
    kv_up = gather_shards(w_kvup.astype(BF))
    gain_lat = lax.all_gather(g_latent.astype(BF), ("fsdp", "ctx"), axis=0, tiled=True).astype(F32)
    out_t = gather_shards(w_out.T.astype(BF))
    gate_up = lax.all_gather(w_gateup.astype(BF), ("fsdp", "ctx"), axis=1, tiled=True)
    ff_down_t = gather_shards(w_down.T.astype(BF))
    if by_head:
        q_up_here = lax.dynamic_slice_in_dim(q_up, core * heads * HEAD, heads * HEAD, 1)
        kv_up_here = lax.dynamic_slice_in_dim(kv_up, core * heads * 128, heads * 128, 1)
    else:
        q_up_here, kv_up_here = q_up, kv_up
    wq = q_up_here.T.reshape(heads, HEAD, QR)
    kv3 = kv_up_here.reshape(KVR, heads, 128)
    wk = jnp.pad(jnp.transpose(kv3[:, :, :NOPE], (1, 0, 2)), ((0, 0), (0, 0), (0, 128 - NOPE)))
    wv = jnp.pad(jnp.transpose(kv3[:, :, NOPE:], (1, 2, 0)), ((0, 0), (0, 80 - VD), (0, 0)))

    gains_norm = g_norms.astype(BF)
    gain_attn = gains_norm[0].astype(F32)
    gain_query, gain_kv = gain_lat[:QR], gain_lat[QR:]

    seq_length = lengths[0, 0]
    index = jnp.arange(slot, dtype=jnp.int32)
    segment = (index >= seq_length).astype(jnp.int32)
    position = (index - segment * seq_length).astype(F32)
    frequency = ROPE_BASE ** (-2.0 * jnp.arange(ROPE // 2, dtype=F32) / ROPE)
    angles = frequency[:, None] * position[None, :]
    cos_t, sin_t = jnp.cos(angles), jnp.sin(angles)
    own_cos = lax.dynamic_slice_in_dim(cos_t, core * rows, rows, 1).T
    own_sin = lax.dynamic_slice_in_dim(sin_t, core * rows, rows, 1).T
    own_segment = lax.dynamic_slice_in_dim(segment, core * rows, rows, 0)
    live = (own_segment == 0).astype(F32)[:, None]
    seg_f = segment.astype(F32)
    seg_q = jnp.concatenate([seg_f[None], 1.0 - seg_f[None], jnp.zeros((14, slot), F32)], axis=0).astype(BF)
    seg_k = (MASK_VALUE * jnp.concatenate([1.0 - seg_f[:, None], seg_f[:, None]], axis=1)).astype(BF)

    inputs = tokens.astype(F32)
    scaled_in = (inputs * gain_attn).astype(BF)
    lat_part = dot_nt(scaled_in, down_t)
    squares_high, squares_low = split_two(jnp.sum(inputs * inputs, axis=1))
    column = jnp.arange(2 * n_tp)
    stats = jnp.where(
        column[None] == 2 * tp, squares_high[:, None], jnp.where(column[None] == 2 * tp + 1, squares_low[:, None], 0)
    ).astype(BF)
    lat_wide = 1152
    payload = jnp.concatenate(
        [lat_part.astype(BF), stats, jnp.zeros((rows, lat_wide - LAT - 2 * n_tp), BF)], axis=1
    )
    gain_rows = jnp.where((jnp.arange(64) == tp)[:, None], gains_norm[1][None], 0).astype(BF)
    gain_rows = jnp.pad(gain_rows, ((0, 0), (0, lat_wide - width)))
    reduced = line_reduce(jnp.concatenate([payload, gain_rows], axis=0), 17, 0)
    gain_mlp = reduced[rows : rows + n_tp, :width].reshape(n_tp * width).astype(F32)
    lat_sum = reduced[:rows].astype(F32)
    factor_one = lax.rsqrt(jnp.sum(lat_sum[:, LAT : LAT + 2 * n_tp], axis=1) / D + EPS_NORM)[:, None]
    latents = lat_sum[:, :LAT] * factor_one
    query_latent = latents[:, :QR]
    kv_latent = latents[:, QR : QR + KVR]
    rope_raw = latents[:, QR + KVR :]
    factor_query = lax.rsqrt(jnp.mean(query_latent * query_latent, axis=1, keepdims=True) + EPS_NORM)
    factor_kv = lax.rsqrt(jnp.mean(kv_latent * kv_latent, axis=1, keepdims=True) + EPS_NORM)
    query_normed = (query_latent * factor_query * gain_query).astype(BF)
    kv_normed = (kv_latent * factor_kv * gain_kv).astype(BF)
    r_one, r_two = rope_raw[:, : ROPE // 2], rope_raw[:, ROPE // 2 :]
    rope_key = jnp.concatenate(
        [r_one * own_cos - r_two * own_sin, r_two * own_cos + r_one * own_sin], axis=1
    ).astype(BF)
    normed_lat = jnp.concatenate([query_normed, kv_normed, rope_key], axis=1)
    lat_both = in_core_order(normed_lat, swap_cores(normed_lat), core, 0)
    qn, kn, kr = lat_both[:, :QR], lat_both[:, QR : QR + KVR], lat_both[:, QR + KVR :]
    krx = jnp.concatenate(
        [jnp.zeros((slot, NOPE), BF), kr, seg_k, jnp.zeros((slot, 128 - HEAD - 2), BF)], axis=1
    )

    att_heads, lse, q_t, k_rows, v_t = attend_forward(qn, kn, krx, cos_t, sin_t, seg_q, wq, wk, wv)
    att_flat = att_heads.reshape(heads * VD, slot)
    own_cols = lambda v: lax.dynamic_slice_in_dim(v, core * rows, rows, 1)
    if by_head:
        other = swap_cores(lax.dynamic_slice_in_dim(att_flat, (1 - core) * rows, rows, 1))
        att_t = in_core_order(own_cols(att_flat), other, core, 0)
    else:
        att_t = own_cols(att_flat)

    feature_owner = jnp.arange(D) // width
    dy = cotangent.astype(F32) * live
    mlp_seed = (RESIDUAL_SCALE * dy).astype(BF)
    if n_tp == 4:
        hidden, d_normed_part, mlp_part, normed_two_t, activation, d_gate, d_up = block_forward(
            att_t.T, tokens, out_t, gain_mlp[None], mlp_seed, gate_up, ff_down_t
        )
        hidden_f = hidden.astype(F32)
        factor_two = lax.rsqrt(jnp.mean(hidden_f * hidden_f, axis=1, keepdims=True) + EPS_NORM)
    else:
        h_part = RESIDUAL_SCALE * dot_nt(att_t.T, out_t)
        h_part = h_part + jnp.where(
            (feature_owner == tp)[None], jnp.concatenate([inputs] * n_tp, axis=1), 0.0
        )
        hidden = lax.psum(h_part.astype(BF), "tp")
        hidden_f = hidden.astype(F32)
        factor_two = lax.rsqrt(jnp.mean(hidden_f * hidden_f, axis=1, keepdims=True) + EPS_NORM)
        normed_two = (hidden_f * factor_two * gain_mlp).astype(BF)
        normed_two_t = normed_two.T
        gate_proj = dot_nn(normed_two, gate_up[0])
        up_proj = dot_nn(normed_two, gate_up[1])
        sigmoid_gate = jax.nn.sigmoid(gate_proj)
        activation = (gate_proj * sigmoid_gate * up_proj).astype(BF)
        mlp_part = dot_nt(activation, ff_down_t).astype(BF)
        d_activation = dot_nn(mlp_seed, ff_down_t)
        d_gate = (
            d_activation * up_proj * sigmoid_gate * (1.0 + gate_proj * (1.0 - sigmoid_gate))
        ).astype(BF)
        d_up = (d_activation * gate_proj * sigmoid_gate).astype(BF)
        d_normed_part = (dot_nt(d_gate, gate_up[0]) + dot_nt(d_up, gate_up[1])).astype(BF)
    mlp_out = lax.psum_scatter(mlp_part, "tp", scatter_dimension=1, tiled=True).astype(F32)
    grads = (
        dot_nn(mlp_seed.T, activation).astype(BF),
        dot_nn(normed_two_t, d_gate).astype(BF),
        dot_nn(normed_two_t, d_up).astype(BF),
    )
    d_normed_part, grads = lax.optimization_barrier((d_normed_part, grads))
    d_normed = line_reduce(d_normed_part, 32, 1).astype(F32)
    own_features = lambda v: lax.dynamic_slice_in_dim(v, tp * width, width, 1)
    layer_out = (own_features(hidden).astype(F32) + RESIDUAL_SCALE * mlp_out).astype(BF)

    grad_down, grad_gate, grad_up = (scatter_grads(g) for g in grads)

    row_inner = jnp.sum(d_normed * gain_mlp * hidden_f, axis=1, keepdims=True) / D
    d_hidden_full = dy + factor_two * d_normed * gain_mlp - hidden_f * (factor_two**3 * row_inner)
    attn_seed = (RESIDUAL_SCALE * d_hidden_full).astype(BF)
    own_dn, own_h = own_features(d_normed), own_features(hidden).astype(F32)
    d_hidden = (
        own_features(cotangent).astype(F32) * live
        + factor_two * own_dn * own_features(gain_mlp[None])
        - own_h * (factor_two**3 * row_inner)
    )
    grad_gain_mlp = jnp.sum(own_dn * own_h * factor_two, axis=0)
    d_att_t = lax.dot_general(out_t, attn_seed, (((0,), (1,)), ((), ())), preferred_element_type=F32).astype(BF)
    grad_out = scatter_grads(dot_tn(attn_seed, att_t.T).astype(BF))

    if by_head:
        pick = lambda v, which: lax.dynamic_slice_in_dim(v, which * heads * VD, heads * VD, 0)
        d_att = in_core_order(pick(d_att_t, core), swap_cores(pick(d_att_t, 1 - core)), core, 1)
    else:
        d_att = lax.dynamic_update_slice(jnp.zeros((heads * VD, slot), BF), d_att_t, (0, core * rows))
    dq_t, d_e, d_kr = attend_backward(
        q_t, k_rows, v_t, att_heads, d_att.reshape(heads, VD, slot), lse, cos_t, sin_t
    )

    d_qn = lax.dot_general(dq_t, q_up_here, (((0,), (1,)), ((), ())), preferred_element_type=F32)
    d_kn = dot_nt(d_e, kv_up_here)
    d_lat_part = jnp.concatenate([d_qn, d_kn, d_kr[:, NOPE:HEAD]], axis=1)
    own_rows = lambda v, which: lax.dynamic_slice_in_dim(v, which * rows, rows, 0)
    from_other = swap_cores(own_rows(d_lat_part, 1 - core).astype(BF)).astype(F32)
    d_lat_sum = (own_rows(d_lat_part, core) + from_other).astype(BF)
    d_lat = line_reduce(jnp.pad(d_lat_sum, ((0, 0), (0, lat_wide - LAT))), 16, 2).astype(F32)
    d_rope = d_lat[:, QR + KVR : LAT]
    k_one, k_two = d_rope[:, : ROPE // 2], d_rope[:, ROPE // 2 :]
    d_rope_raw = jnp.concatenate([k_one * own_cos + k_two * own_sin, k_two * own_cos - k_one * own_sin], axis=1)
    d_query_latent, grad_gain_query = norm_backward(d_lat[:, :QR], query_latent, factor_query, gain_query)
    d_kv_latent, grad_gain_kv = norm_backward(d_lat[:, QR : QR + KVR], kv_latent, factor_kv, gain_kv)
    d_latents = jnp.concatenate([d_query_latent, d_kv_latent, d_rope_raw], axis=1)
    in_inner = jnp.sum(d_latents * latents, axis=1, keepdims=True) / D
    d_latents = (d_latents * factor_one).astype(BF)
    grad_both = dot_tn(d_latents, scaled_in).astype(BF)
    grad_qdown = scatter_grads(grad_both[:QR])
    grad_kvdown = scatter_grads(grad_both[QR:])
    d_in = dot_nn(d_latents, down_t)
    grad_gain_attn = jnp.sum(d_in * inputs, axis=0)
    grad_input = (d_hidden + d_in * gain_attn - inputs * (factor_one**2 * in_inner)).astype(BF)

    grad_qup = dot_nt(qn.T, dq_t).astype(BF)
    grad_kvup = dot_tn(kn, d_e).astype(BF)

    def scatter_up(g):
        if not by_head:
            return scatter_grads(g)
        n_rows, n_cols = g.shape
        g = g.reshape(n_fsdp, n_ctx, n_rows // (n_fsdp * n_ctx), n_cols)
        mine = lax.dynamic_index_in_dim(g, core, 1, keepdims=False)
        other = swap_cores(lax.dynamic_index_in_dim(g, 1 - core, 1, keepdims=False))
        return scatter_fsdp(in_core_order(mine, other, core, 2))

    grad_qup, grad_kvup = scatter_up(grad_qup), scatter_up(grad_kvup)

    owned = [
        grad_qdown.astype(F32).T,
        grad_kvdown.astype(F32).T,
        grad_qup.astype(F32),
        grad_kvup.astype(F32),
        grad_out.astype(F32).T,
        jnp.stack([grad_gate, grad_up]).astype(F32),
        grad_down.astype(F32).T,
    ]
    both_gains = jnp.stack([grad_gain_attn, grad_gain_mlp])
    placed_gains = jnp.where((feature_owner == tp)[None], jnp.concatenate([both_gains] * n_tp, axis=1), 0.0)
    latent_gains = jnp.concatenate([grad_gain_query, grad_gain_kv]) * (tp == 0)
    squares = jnp.stack([jnp.sum(g * g) for g in owned])
    small = lax.psum(
        jnp.concatenate([placed_gains.reshape(-1), latent_gains, squares]), ("fsdp", "ctx", "tp")
    )
    all_gains = small[: 2 * D].reshape(2, D)
    all_latent = small[2 * D : 2 * D + QR + KVR]
    share = g_latent.shape[0]
    place = lax.axis_index("fsdp") * n_ctx + core
    owned.append(own_features(all_gains))
    owned.append(lax.dynamic_slice_in_dim(all_latent, place * share, share, 0))
    totals = [small[2 * D + QR + KVR + n] for n in range(7)]
    totals += [jnp.sum(all_gains * all_gains), jnp.sum(all_latent * all_latent)]
    entry_counts = (
        D * QR,
        D * (KVR + ROPE),
        QR * H * HEAD,
        KVR * H * (NOPE + VD),
        H * VD * D,
        2 * D * FF,
        FF * D,
        2 * D,
        QR + KVR,
    )
    new_params, new_firsts, new_seconds = [], [], []
    for n in range(9):
        limit = CLIP_RMS * entry_counts[n] ** 0.5
        clipped = owned[n] * (limit / jnp.maximum(jnp.sqrt(totals[n]), limit))
        updated, first_new, second_new = adamw_update(
            params[n], clipped, firsts[n], seconds[n], WEIGHT_DECAY if n < 7 else 0.0
        )
        new_params.append(updated)
        new_firsts.append(first_new)
        new_seconds.append(second_new)
    return (layer_out, grad_input, *owned, *new_params[:7], *new_firsts, *new_seconds)


def solution(mesh):
    sharded = ("fsdp", "ctx")
    weights = (
        P("tp", sharded),
        P("tp", sharded),
        P(sharded, "tp"),
        P(sharded, "tp"),
        P("tp", sharded),
        P(None, sharded, "tp"),
        P("tp", sharded),
    )
    gains = (P(None, "tp"), P(sharded))
    tokens = P(sharded, "tp")
    return jax.shard_map(
        local,
        mesh=mesh,
        in_specs=(tokens, P(sharded, None), P("fsdp", None)) + (weights + gains) * 3,
        out_specs=(tokens, tokens) + weights + gains + weights + (weights + gains) * 2,
        check_vma=False,
    )
```

time: 1980 us -> 1140 us (0.58)
  waiting for transfers between devices: 859 us -> 138 us
  Pallas kernels: 0 us -> 508 us
  matrix products: 451 us -> 72.5 us
  local copies, waits for them, and re-layouts: 296 us -> 144 us
  blocking collectives: 149 us -> 82.2 us
  other arithmetic: 169 us -> 128 us
  starting transfers between devices: 10.1 us -> 34.1 us
    pallas_call x0 -> x6, Pallas kernels: none -> 508 us  [the longest x3 250 us: line_reduce(): pl.pallas_call(functools.partial(line_reduce_kernel, chunks), out_shape=j...]
    unnamed x35 -> x6, waiting for transfers between devices: 428 us -> 0.1 us
    dot_general x35 -> x12, matrix products: 451 us -> 72.5 us  [the longest x4 49 us: dot_nn(): lax.dot_general(a, b, (((1,), (0,)), ((), ())), preferred_element_type=F32)]
    all_gather x6 -> x4, waiting for transfers between devices: 306 us -> 0.01 us  [the longest x3 0.01 us: gather_shards(): return lax.all_gather(v, ('fsdp', 'ctx'), axis=0, tiled=True)]
    unnamed x212 -> x261, local copies, waits for them, and re-layouts: 185 us -> 28.8 us
    ppermute x4 -> x44, waiting for transfers between devices: 0.01 us -> 138 us  [the longest x38 136 us: keep_half(): other = lax.ppermute(take(v, 1 - which, axis), name, pairs)]
    psum x2 -> x0, waiting for transfers between devices: 117 us -> none  [the longest x1 65.5 us: local(): lax.psum(jnp.dot(normed_one, down_both, preferred_element_type=jnp.float3...]
    dynamic_update_slice x4 -> x0, local copies, waits for them, and re-layouts: 75.5 us -> none  [attend_backward(): (key_sum, value_sum), d_queries = lax.scan(one_block, initial, pieces)]
  transfers between devices with their start and end apart: 29 -> 49, of which waited for: 13 -> 30; matrix products, arithmetic and copies ran while one was open for 23% -> 20% of each run, Pallas kernels for 0% -> 19%
where the time goes in v1:
time: 1140 us; the launch traced here: 1130 us
  Pallas kernels  508 us (45%)
  local copies, waits for them, and re-layouts  144 us (13%)
  waiting for transfers between devices  138 us (12%)
  other arithmetic  128 us (11%)
  blocking collectives  82.2 us (7%)
  matrix products  72.5 us (6%)
  starting transfers between devices  34.1 us (3%)
  between operations  23.5 us (2%)
    pallas_call x3, Pallas kernels, line_reduce(): pl.pallas_call(functools.partial(line_reduce_kernel, chunks), out_shape=j...  250 us
    pallas_call x1, Pallas kernels, block_forward(): pl.pallas_call(block_kernel, out_shape=[wide, wide, wide, jax.ShapeDtypeS...  173 us
    ppermute x38, waiting for transfers between devices, keep_half(): other = lax.ppermute(take(v, 1 - which, axis), name, pairs)  136 us
    dot_general x4, matrix products, dot_nn(): lax.dot_general(a, b, (((1,), (0,)), ((), ())), preferred_element_type=F32)  49 us
    pallas_call x1, Pallas kernels, attend_backward(): pl.pallas_call(attend_backward_kernel, grid=(heads, rows // BQ), in_specs...  47.8 us
    psum x1, blocking collectives, local(): lax.psum(jnp.concatenate([placed_gains.reshape(-1), latent_gains, squares...  37.7 us
    pallas_call x1, Pallas kernels, attend_forward(): pl.pallas_call(attend_forward_kernel, grid=(heads, rows // BQ), in_specs=...  37.5 us
    optimization_barrier x3, local copies, waits for them, and re-layouts, local(): d_normed_part, grads = lax.optimization_barrier((d_normed_part, grads))  36.3 us
  transfers between devices with their start and end apart: 49, of which 30 were waited for; matrix products, arithmetic and copies ran while one was open for 20% of the time, Pallas kernels for 19%

profile of v1, /device:TPU:0, one launch (start us, length us, event | category | flops | bytes accessed | tf_op | source)
XLA Modules:
  0.0 1130.7 jit_solution(8554413573161454700)
XLA Ops:
  16.3 10.2 all-gather.1
  27.1 11.3 all-gather
  38.5 10.1 all_gather.24
  64.5 68.6 %line_reduce.3 = bf16[1088,1152]{1,0:T(8,128)(2,1)S(1)} custom-call(bf16[1088,1152]{1,0:T(8,128)(2,1)S(1)} %fusion.21.x_ref), custom_call_target="tpu_custom_call" | custom-call | flops 2506752 | bytes 50135040 | tf_op jit(solution)/shard_map/line_reduce/pallas_call | solution.py:143
  160.9 12.9 %all_gather.28 = bf16[256,1280]{1,0:T(8,128)(2,1)S(1)} all-gather(bf16[32,1280]{1,0:T(8,128)(2,1)S(1)} %convert_element_type.754), channel_id=1, replica_groups=mesh['fsdp'=4,'ctx'=2,'tp'=4] {'fsdp','ctx'}, dimensions={0}, use_global_device_ids=true | all-gather | bytes 737280 | tf_op jit(solution)/shard_map/all_gather | solution.py:580
  204.1 37.5 %attend_forward.1 = (bf16[5,64,2048]{2,1,0:T(8,128)(2,1)S(1)}, f32[5,1,2048]{2,1,0:T(1,128)S(1)}, bf16[5,128,2048]{2,1,0:T(8,128)(2,1)S(1)}, bf16[5,2048,128]{2,1,0:T(8,128)(2,1)S(1)}, bf16[5,80,2048]{2,1,0:T(8,128)(2,1)S(1)}) custom-call(bf16[2048,768]{1,0:T(8,128)(2,1)S(1)} %slice.214.qn_ref, bf16[2048,256]{1,0:T(8,128)(2,1)S(1)} %copy-done.2, ...), custom_call_target="tpu_custom_call" | custom-call | flops 6710886400 | bytes 31457280 | tf_op jit(solution)/shard_map/attend_forward/pallas_call | solution.py:213
  242.2 8.3 multiply_convert_fusion.seed_any
  254.2 172.9 %block_forward.1 = (bf16[1024,2560]{1,0:T(8,128)(2,1)}, bf16[1024,2560]{1,0:T(8,128)(2,1)}, bf16[1024,2560]{1,0:T(8,128)(2,1)}, bf16[2560,1024]{1,0:T(8,128)(2,1...) custom-call(bf16[1024,640]{1,0:T(8,128)(2,1)} %fusion.67.att_ref, ...), custom_call_target="tpu_custom_call" | custom-call | flops 50331648000 | bytes 419430400 | tf_op jit(solution)/shard_map/block_forward/pallas_call | solution.py:546
  427.1 13.9 %convolution_convert_fusion = bf16[2560,1600]{0,1:T(8,128)(2,1)} fusion(bf16[2560,1024]{1,0:T(8,128)(2,1)} %get-tuple-element.60, bf16[1024,1600]{1,0:T(8,128)(2,1)} %get-tuple-element.62), kind=kOutput, calls=%fused_computation.3 | convolution fusion | flops 8392704000 | bytes 16711680 | tf_op jit(solution)/shard_map/dot_general | solution.py:42
  441.0 13.9 %convolution_convert_fusion.1 = bf16[2560,1600]{0,1:T(8,128)(2,1)} fusion(bf16[2560,1024]{1,0:T(8,128)(2,1)} %get-tuple-element.60, bf16[1024,1600]{1,0:T(8,128)(2,1)} %get-tuple-element.61), kind=kOutput, calls=%fused_computation.4 | convolution fusion | flops 8392704000 | bytes 16711680 | tf_op jit(solution)/shard_map/dot_general | solution.py:42
  455.0 11.7 %convolution_convert_fusion.2 = bf16[2560,1600]{0,1:T(8,128)(2,1)} fusion(bf16[1024,2560]{1,0:T(8,128)(2,1)S(1)} %bitcast.408, bf16[1024,1600]{1,0:T(8,128)(2,1)S(1)} %copy-done.103), kind=kOutput, calls=%fused_computation.5 | convolution fusion | flops 8392704000 | bytes 16711680 | tf_op jit(solution)/shard_map/dot_general | solution.py:42
  466.7 119.7 %line_reduce.4 = bf16[1024,2560]{1,0:T(8,128)(2,1)S(1)} custom-call(bf16[1024,2560]{1,0:T(8,128)(2,1)S(1)} %bitcast.377), custom_call_target="tpu_custom_call" | custom-call | flops 5242880 | bytes 104857600 | tf_op jit(solution)/shard_map/line_reduce/pallas_call | solution.py:143
  586.4 5.4 convert_element_type.774
  598.9 6.4 convolution_convert_fusion.3
  609.1 8.0 copy.211
  617.1 12.2 %copy.207 = bf16[2560,1600]{1,0:T(8,128)(2,1)} copy(bf16[2560,1600]{0,1:T(8,128)(2,1)} %convolution_convert_fusion.2) | data formatting | bytes 16384000 | tf_op jit(solution)/shard_map/optimization_barrier | solution.py:776
  634.4 12.0 %copy.202 = bf16[2560,1600]{1,0:T(8,128)(2,1)} copy(bf16[2560,1600]{0,1:T(8,128)(2,1)} %convolution_convert_fusion.1) | data formatting | bytes 16384000 | tf_op jit(solution)/shard_map/optimization_barrier | solution.py:776
  650.9 12.1 %copy.204 = bf16[2560,1600]{1,0:T(8,128)(2,1)} copy(bf16[2560,1600]{0,1:T(8,128)(2,1)} %convolution_convert_fusion) | data formatting | bytes 16384000 | tf_op jit(solution)/shard_map/optimization_barrier | solution.py:776
  672.3 47.8 %attend_backward.1 = (bf16[480,2048]{1,0:T(8,128)(2,1)S(1)}, bf16[2048,640]{1,0:T(8,128)(2,1)S(1)}, f32[2048,128]{1,0:T(8,128)S(1)}) custom-call(bf16[5,128,2048]{2,1,0:T(8,128)(2,1)S(1)} %copy-done.11, bf16[5,2048,128]{2,1,0:T(8,128)(2,1)} %copy-done.12, bf16[5,80,2048]{2,1,0:T(8,128)(2,1)S(1)} %copy-done.14, bf16[5,64,2048]{2,1,0:T(8,128)(2,1)S(1)} %copy-done.1, ...), custom_call_target="tpu_custom_call" | custom-call | flops 18874368000 | bytes 31457280 | tf_op jit(solution)/shard_map/attend_backward/pallas_call | solution.py:295
  729.7 6.2 pad_maximum_fusion
  795.3 5.2 collective-permute-done.26
  814.0 61.9 %line_reduce.5 = bf16[1024,1152]{1,0:T(8,128)(2,1)S(1)} custom-call(bf16[1024,1152]{1,0:T(8,128)(2,1)S(1)} %pad.19.x_ref), custom_call_target="tpu_custom_call" | custom-call | flops 2359296 | bytes 47185920 | tf_op jit(solution)/shard_map/line_reduce/pallas_call | solution.py:143
  882.0 5.7 concatenate.128
  946.9 12.9 %collective-permute-done.40 = bf16[2,160,1600]{2,1,0:T(8,128)(2,1)} collective-permute-done((bf16[2,160,1600]{2,1,0:T(8,128)(2,1)}, bf16[2,160,1600]{2,1,0:T(8,128)(2,1)}, u32[]{:S(2)}, u32[]{:S(2)}) %collective-permute-start.40) | collective-permute-done | bytes 1024032 | tf_op jit(solution)/shard_map/ppermute | solution.py:596
  965.0 17.5 %collective-permute-done.30 = bf16[2,160,1600]{2,1,0:T(8,128)(2,1)S(1)} collective-permute-done((bf16[2,160,1600]{2,1,0:T(8,128)(2,1)S(1)}, bf16[2,160,1600]{2,1,0:T(8,128)(2,1)S(1)}, u32[]{:S(2)}, u32[]{:S(2)}) %collective-permute-start.30) | collective-permute-done | bytes 1024032 | tf_op jit(solution)/shard_map/ppermute | solution.py:596
  985.5 19.8 %collective-permute-done.35 = bf16[2,160,1600]{2,1,0:T(8,128)(2,1)S(1)} collective-permute-done((bf16[2,160,1600]{2,1,0:T(8,128)(2,1)S(1)}, bf16[2,160,1600]{2,1,0:T(8,128)(2,1)S(1)}, u32[]{:S(2)}, u32[]{:S(2)}) %collective-permute-start.35) | collective-permute-done | bytes 1024032 | tf_op jit(solution)/shard_map/ppermute | solution.py:596
  1008.3 10.1 collective-permute-done.41
  1020.0 7.9 collective-permute-done.31
  1040.3 9.5 fusion.17
  1054.5 37.7 %psum.7 = f32[6151]{0:T(1024)S(1)} all-reduce(f32[6151]{0:T(1024)S(1)} %concatenate.147), channel_id=1, replica_groups=mesh['fsdp'=4,'ctx'=2,'tp'=4] {'fsdp','ctx','tp'}, use_global_device_ids=true, to_apply=%region_21.22 | all-reduce | flops 6151 | bytes 49208 | tf_op jit(solution)/shard_map/psum | solution.py:854
  1103.0 6.8 multiply_subtract_fusion.2
  1109.9 8.1 multiply_subtract_fusion
  (595 shorter events, 303.0 us)
Async XLA Ops:
  7.2 186.1 %all-gather.7.cloned.1.call-start = ((), (), s32[]{:S(2)}) async-start(), calls=%async_computation.1 | async-start | bytes 1769472 | tf_op jit(solution)/shard_map/all_gather | solution.py:580
  9.1 245.1 %all-gather.9.cloned.1.call-start = ((), (), s32[]{:S(2)}) async-start(), calls=%async_computation.2 | async-start | bytes 3686400 | tf_op jit(solution)/shard_map/all_gather | solution.py:580
  11.2 243.1 %all-gather.13.cloned.1.call-start = ((), (), s32[]{:S(2)}) async-start(), calls=%async_computation.4 | async-start | bytes 9584640 | tf_op jit(solution)/shard_map/all_gather | solution.py:580
  12.4 241.9 %all-gather.11.cloned.1.call-start = ((), (), s32[]{:S(2)}) async-start(), calls=%async_computation.3 | async-start | bytes 19169280 | tf_op jit(solution)/shard_map/all_gather | solution.py:663
  16.2 1021.5 %reduce-scatter.4.cloned.1.call-start = ((), (), s32[]{:S(2)}) async-start(), calls=%async_computation.5 | async-start | bytes 6553600
  154.6 25.8 %collective-permute-start = (bf16[1024,1056]{0,1:T(8,128)(2,1)}, bf16[1024,1056]{0,1:T(8,128)(2,1)}, u32[]{:S(2)}, u32[]{:S(2)}) collective-permute-start(bf16[1024,1056]{0,1:T(8,128)(2,1)} %copy.174), channel_id=1, source_target_pairs={{0,4},{4,0},{1,5},{5,1},{2,6},{6,2},{3,7},{7,3},{8,12},{12,8},{9,1... | collective-permute-start | bytes 6488072 | tf_op jit(solution)/shard_map/ppermute | solution.py:570
  241.8 9.1 collective-permute-start.1
  609.0 61.9 %collective-permute-start.2 = (bf16[320,1024]{1,0:T(8,128)(2,1)S(1)}, bf16[320,1024]{1,0:T(8,128)(2,1)S(1)}, u32[]{:S(2)}, u32[]{:S(2)}) collective-permute-start(bf16[320,1024]{1,0:T(8,128)(2,1)S(1)} %get-tuple-element.140), channel_id=1, source_target_pairs={{0,4},{4,0},{1,5},{5,1},{2,6},{6,2},{3,7},{7,3},{8,12},{12,8},{9,1... | collective-permute-start | bytes 1966088 | tf_op jit(solution)/shard_map/ppermute | solution.py:570
  633.9 293.0 %collective-permute-start.39 = (bf16[4,320,1600]{2,1,0:T(8,128)(2,1)}, bf16[4,320,1600]{2,1,0:T(8,128)(2,1)}, u32[]{:S(2)}, u32[]{:S(2)}) collective-permute-start(bf16[4,320,1600]{2,1,0:T(8,128)(2,1)} %dynamic-slice_bitcast_fusion), channel_id=1, source_target_pairs={{0,4},{4,0},{1,5},{5,1},{2,6},{6,2},{3,7},{7,3},{8,12},{12,8},{9,1... | collective-permute-start | bytes 12288008 | tf_op jit(solution)/shard_map/ppermute | solution.py:596
  650.9 284.8 %collective-permute-start.29 = (bf16[4,320,1600]{2,1,0:T(8,128)(2,1)}, bf16[4,320,1600]{2,1,0:T(8,128)(2,1)}, u32[]{:S(2)}, u32[]{:S(2)}) collective-permute-start(bf16[4,320,1600]{2,1,0:T(8,128)(2,1)} %dynamic-slice_bitcast_fusion.2), channel_id=1, source_target_pairs={{0,4},{4,0},{1,5},{5,1},{2,6},{6,2},{3,7},{7,3},{8,12},{12,8},{9,1... | collective-permute-start | bytes 12288008 | tf_op jit(solution)/shard_map/ppermute | solution.py:596
  665.7 115.6 %collective-permute-start.24 = (bf16[4,320,640]{2,1,0:T(8,128)(2,1)}, bf16[4,320,640]{2,1,0:T(8,128)(2,1)}, u32[]{:S(2)}, u32[]{:S(2)}) collective-permute-start(bf16[4,320,640]{2,1,0:T(8,128)(2,1)} %dynamic-slice_bitcast_fusion.3), channel_id=1, source_target_pairs={{0,4},{4,0},{1,5},{5,1},{2,6},{6,2},{3,7},{7,3},{8,12},{12,8},{9,1... | collective-permute-start | bytes 4915208 | tf_op jit(solution)/shard_map/ppermute | solution.py:596
  724.9 17.4 %collective-permute-start.19 = (bf16[4,32,640]{2,1,0:T(8,128)(2,1)S(1)}, bf16[4,32,640]{2,1,0:T(8,128)(2,1)}, u32[]{:S(2)}, u32[]{:S(2)}) collective-permute-start(bf16[4,32,640]{2,1,0:T(8,128)(2,1)S(1)} %get-tuple-element.152), channel_id=1, source_target_pairs={{0,4},{4,0},{1,5},{5,1},{2,6},{6,2},{3,7},{7,3},{8,12},{12,8},{9,1... | collective-permute-start | bytes 491528 | tf_op jit(solution)/shard_map/ppermute | solution.py:570
  741.4 66.6 %collective-permute-start.3 = (bf16[1024,1056]{0,1:T(8,128)(2,1)}, bf16[1024,1056]{0,1:T(8,128)(2,1)}, u32[]{:S(2)}, u32[]{:S(2)}) collective-permute-start(bf16[1024,1056]{0,1:T(8,128)(2,1)} %copy.190), channel_id=1, source_target_pairs={{0,4},{4,0},{1,5},{5,1},{2,6},{6,2},{3,7},{7,3},{8,12},{12,8},{9,1... | collective-permute-start | bytes 6488072 | tf_op jit(solution)/shard_map/ppermute | solution.py:570
  762.8 7.0 collective-permute-start.15
  769.8 6.1 collective-permute-start.17
  783.4 9.4 collective-permute-start.25
  786.3 8.0 collective-permute-start.27
  792.8 149.5 %collective-permute-start.34 = (bf16[4,320,1600]{2,1,0:T(8,128)(2,1)}, bf16[4,320,1600]{2,1,0:T(8,128)(2,1)}, u32[]{:S(2)}, u32[]{:S(2)}) collective-permute-start(bf16[4,320,1600]{2,1,0:T(8,128)(2,1)} %dynamic-slice_bitcast_fusion.1), channel_id=1, source_target_pairs={{0,4},{4,0},{1,5},{5,1},{2,6},{6,2},{3,7},{7,3},{8,12},{12,8},{9,1... | collective-permute-start | bytes 12288008 | tf_op jit(solution)/shard_map/ppermute | solution.py:596
  794.3 6.3 collective-permute-start.26
  896.2 17.9 %collective-permute-start.4 = (bf16[4,96,640]{2,1,0:T(8,128)(2,1)S(1)}, bf16[4,96,640]{2,1,0:T(8,128)(2,1)S(1)}, u32[]{:S(2)}, u32[]{:S(2)}) collective-permute-start(bf16[4,96,640]{2,1,0:T(8,128)(2,1)S(1)} %dynamic-slice_bitcast_fusion.18), channel_id=1, source_target_pairs={{0,4},{4,0},{1,5},{5,1},{2,6},{6,2},{3,7},{7,3},{8,12},{12,8},{9,1... | collective-permute-start | bytes 1474568 | tf_op jit(solution)/shard_map/ppermute | solution.py:596
  933.0 26.8 %collective-permute-start.40 = (bf16[2,160,1600]{2,1,0:T(8,128)(2,1)}, bf16[2,160,1600]{2,1,0:T(8,128)(2,1)}, u32[]{:S(2)}, u32[]{:S(2)}) collective-permute-start(bf16[2,160,1600]{2,1,0:T(8,128)(2,1)} %dynamic-slice_bitcast_fusion.5), channel_id=1, source_target_pairs={{0,8},{8,0},{16,24},{24,16},{1,9},{9,1},{17,25},{25,17},{2,10},{10... | collective-permute-start | bytes 3072008 | tf_op jit(solution)/shard_map/ppermute | solution.py:596
  934.6 27.8 %collective-permute-start.42 = (bf16[2,160,1600]{2,1,0:T(8,128)(2,1)}, bf16[2,160,1600]{2,1,0:T(8,128)(2,1)}, u32[]{:S(2)}, u32[]{:S(2)}) collective-permute-start(bf16[2,160,1600]{2,1,0:T(8,128)(2,1)} %dynamic-slice_bitcast_fusion.4), channel_id=1, source_target_pairs={{0,16},{16,0},{8,24},{24,8},{1,17},{17,1},{9,25},{25,9},{2,18},{18... | collective-permute-start | bytes 3072008 | tf_op jit(solution)/shard_map/ppermute | solution.py:596
  939.6 42.8 %collective-permute-start.30 = (bf16[2,160,1600]{2,1,0:T(8,128)(2,1)S(1)}, bf16[2,160,1600]{2,1,0:T(8,128)(2,1)S(1)}, u32[]{:S(2)}, u32[]{:S(2)}) collective-permute-start(bf16[2,160,1600]{2,1,0:T(8,128)(2,1)S(1)} %dynamic-slice_bitcast_fusion.9), channel_id=1, source_target_pairs={{0,8},{8,0},{16,24},{24,16},{1,9},{9,1},{17,25},{25,17},{2,10},{10... | collective-permute-start | bytes 3072008 | tf_op jit(solution)/shard_map/ppermute | solution.py:596
  941.3 42.8 %collective-permute-start.32 = (bf16[2,160,1600]{2,1,0:T(8,128)(2,1)S(1)}, bf16[2,160,1600]{2,1,0:T(8,128)(2,1)S(1)}, u32[]{:S(2)}, u32[]{:S(2)}) collective-permute-start(bf16[2,160,1600]{2,1,0:T(8,128)(2,1)S(1)} %dynamic-slice_bitcast_fusion.8), channel_id=1, source_target_pairs={{0,16},{16,0},{8,24},{24,8},{1,17},{17,1},{9,25},{25,9},{2,18},{18... | collective-permute-start | bytes 3072008 | tf_op jit(solution)/shard_map/ppermute | solution.py:596
  946.1 59.2 %collective-permute-start.35 = (bf16[2,160,1600]{2,1,0:T(8,128)(2,1)S(1)}, bf16[2,160,1600]{2,1,0:T(8,128)(2,1)S(1)}, u32[]{:S(2)}, u32[]{:S(2)}) collective-permute-start(bf16[2,160,1600]{2,1,0:T(8,128)(2,1)S(1)} %dynamic-slice_bitcast_fusion.7), channel_id=1, source_target_pairs={{0,8},{8,0},{16,24},{24,16},{1,9},{9,1},{17,25},{25,17},{2,10},{10... | collective-permute-start | bytes 3072008 | tf_op jit(solution)/shard_map/ppermute | solution.py:596
  959.7 47.2 %collective-permute-start.37 = (bf16[2,160,1600]{2,1,0:T(8,128)(2,1)S(1)}, bf16[2,160,1600]{2,1,0:T(8,128)(2,1)S(1)}, u32[]{:S(2)}, u32[]{:S(2)}) collective-permute-start(bf16[2,160,1600]{2,1,0:T(8,128)(2,1)S(1)} %dynamic-slice_bitcast_fusion.6), channel_id=1, source_target_pairs={{0,16},{16,0},{8,24},{24,8},{1,17},{17,1},{9,25},{25,9},{2,18},{18... | collective-permute-start | bytes 3072008 | tf_op jit(solution)/shard_map/ppermute | solution.py:596
  962.4 56.0 %collective-permute-start.41 = (bf16[160,1600]{1,0:T(8,128)(2,1)S(1)}, bf16[160,1600]{1,0:T(8,128)(2,1)S(1)}, u32[]{:S(2)}, u32[]{:S(2)}) collective-permute-start(bf16[160,1600]{1,0:T(8,128)(2,1)S(1)} %dynamic-slice_bitcast_fusion.13), channel_id=1, source_target_pairs={{0,16},{16,0},{8,24},{24,8},{1,17},{17,1},{9,25},{25,9},{2,18},{18... | collective-permute-start | bytes 1536008 | tf_op jit(solution)/shard_map/ppermute | solution.py:596
  982.4 37.4 %collective-permute-start.43 = (bf16[160,1600]{1,0:T(8,128)(2,1)S(1)}, bf16[160,1600]{1,0:T(8,128)(2,1)S(1)}, u32[]{:S(2)}, u32[]{:S(2)}) collective-permute-start(bf16[160,1600]{1,0:T(8,128)(2,1)S(1)} %dynamic-slice_bitcast_fusion.12), channel_id=1, source_target_pairs={{0,8},{8,0},{16,24},{24,16},{1,9},{9,1},{17,25},{25,17},{2,10},{10... | collective-permute-start | bytes 1536008 | tf_op jit(solution)/shard_map/ppermute | solution.py:596
  984.1 43.9 %collective-permute-start.31 = (bf16[160,1600]{1,0:T(8,128)(2,1)S(1)}, bf16[160,1600]{1,0:T(8,128)(2,1)S(1)}, u32[]{:S(2)}, u32[]{:S(2)}) collective-permute-start(bf16[160,1600]{1,0:T(8,128)(2,1)S(1)} %dynamic-slice_bitcast_fusion.17), channel_id=1, source_target_pairs={{0,16},{16,0},{8,24},{24,8},{1,17},{17,1},{9,25},{25,9},{2,18},{18... | collective-permute-start | bytes 1536008 | tf_op jit(solution)/shard_map/ppermute | solution.py:596
  1005.3 22.9 %collective-permute-start.33 = (bf16[160,1600]{1,0:T(8,128)(2,1)S(1)}, bf16[160,1600]{1,0:T(8,128)(2,1)S(1)}, u32[]{:S(2)}, u32[]{:S(2)}) collective-permute-start(bf16[160,1600]{1,0:T(8,128)(2,1)S(1)} %dynamic-slice_bitcast_fusion.16), channel_id=1, source_target_pairs={{0,8},{8,0},{16,24},{24,16},{1,9},{9,1},{17,25},{25,17},{2,10},{10... | collective-permute-start | bytes 1536008 | tf_op jit(solution)/shard_map/ppermute | solution.py:596
  1006.9 26.7 %collective-permute-start.36 = (bf16[160,1600]{1,0:T(8,128)(2,1)S(1)}, bf16[160,1600]{1,0:T(8,128)(2,1)S(1)}, u32[]{:S(2)}, u32[]{:S(2)}) collective-permute-start(bf16[160,1600]{1,0:T(8,128)(2,1)S(1)} %dynamic-slice_bitcast_fusion.15), channel_id=1, source_target_pairs={{0,16},{16,0},{8,24},{24,8},{1,17},{17,1},{9,25},{25,9},{2,18},{18... | collective-permute-start | bytes 1536008 | tf_op jit(solution)/shard_map/ppermute | solution.py:596
  1018.3 15.5 %collective-permute-start.38 = (bf16[160,1600]{1,0:T(8,128)(2,1)S(1)}, bf16[160,1600]{1,0:T(8,128)(2,1)S(1)}, u32[]{:S(2)}, u32[]{:S(2)}) collective-permute-start(bf16[160,1600]{1,0:T(8,128)(2,1)S(1)} %dynamic-slice_bitcast_fusion.14), channel_id=1, source_target_pairs={{0,8},{8,0},{16,24},{24,16},{1,9},{9,1},{17,25},{25,17},{2,10},{10... | collective-permute-start | bytes 1536008 | tf_op jit(solution)/shard_map/ppermute | solution.py:596
  (143 other events, 2610.6 us)
Sparse Core Ops, SparseCore 0:
  10.5 29.4 all-gather.6
  42.5 32.8 all-gather.8
  77.9 54.9 all-gather.12
  135.2 93.5 all-gather.10
  617.2 92.0 reduce-scatter.3

commit v2 on v1

--- a/solution.py
+++ b/solution.py
@@ -376,7 +376,7 @@
 
 
 def block_kernel(
-    att_ref, x_ref, out_ref, gain_ref, seed_any, gu_any, down_any,
+    att_ref, x_ref, out_ref, gain_ref, live_ref, seed_any, gu_any, down_any,
     hid_any, dn_any, mo_any, n2t_any, act_any, dg_any, du_any,
     xb, near, cross, total, gu, down, n2, n2t, seed, act, dg, du,
     load_sem, seed_sem, hid_sem, dn_sem, mo_sem, n2t_sem, act_sem, dg_sem, du_sem, *sems,
@@ -480,6 +480,13 @@
         each(D // 256, turn)
         save_n2t(m).start()
         load_seed(m).wait()
+
+        def weigh(r):
+            here = pl.ds(pl.multiple_of(r * 32, 32), 32)
+            live = live_ref[pl.ds(pl.multiple_of(m * MLP_ROWS + r * 32, 32), 32), :]
+            seed[here, :] = (seed[here, :].astype(F32) * (live * RESIDUAL_SCALE)).astype(BF)
+
+        each(MLP_ROWS // 32, weigh)
 
         @pl.when(m == 0)
         def _():
@@ -534,7 +541,7 @@
         each(count, sent)
 
 
-def block_forward(att, x, out_t, gain, seed, gate_up, down_t):
+def block_forward(att, x, out_t, gain, live, seed, gate_up, down_t):
     rows = att.shape[0]
     hidden_units = down_t.shape[1]
     count, groups = rows // LINE, rows // MLP_ROWS
@@ -546,7 +553,7 @@
     return pl.pallas_call(
         block_kernel,
         out_shape=[wide, wide, wide, jax.ShapeDtypeStruct((D, rows), BF), units, units, units],
-        in_specs=[vmem] * 4 + [anywhere] * 3,
+        in_specs=[vmem] * 5 + [anywhere] * 3,
         out_specs=[anywhere] * 7,
         scratch_shapes=[pltpu.VMEM((rows, D), BF)] * 4
         + [
@@ -563,7 +570,318 @@
         compiler_params=pltpu.CompilerParams(collective_id=3, has_side_effects=True, vmem_limit_bytes=63 * MIB),
         cost_estimate=pl.CostEstimate(flops=rows * D * hidden_units * 12, bytes_accessed=400 * MIB, transcendentals=0),
         name="block_forward",
-    )(att, x, out_t, gain, seed, gate_up, down_t)
+    )(att, x, out_t, gain, live, seed, gate_up, down_t)
+
+
+LAG = 3
+LOAD = 128
+
+
+def grad_kernel(
+    live_ref, gain_ref, dnp_any, hid_any, cot_any, n2t_any, dg_any, du_any, act_any,
+    sa_any, dh_any, gain_out, grad_any,
+    near, cross, total, cin, stage, xin, yin2, yin, xin2, lhs, rhs, hbuf, cbuf, sbuf, dbuf, prep,
+    total_sem, lhs_sem, rhs_sem, h_sem, c_sem, sa_sem, dh_sem, prep_sem, out_sem,
+    core_send, core_recv, x_send, x_recv, y2_send, y2_recv, y_send, y_recv, x2_send, x2_recv, *sems,
+):
+    z, core, place = lax.axis_index("tp"), lax.axis_index("ctx"), lax.axis_index("fsdp")
+    y, x = place // 2, place % 2
+    is_end, is_mid, partner, across = line_places(z)
+    to_mid, over, to_end, _, _ = line_copies(dnp_any, near, cross, total, sems, partner, across)
+    count = total.shape[0] // LINE
+    width = dh_any.shape[1]
+    half = yin.shape[1]
+    block = 2 * half
+    mine = pl.ds(pl.multiple_of(z * width, 128), width)
+    to_core, to_x, to_y = {"ctx": 1 - core}, {"fsdp": y * 2 + 1 - x}, {"fsdp": (1 - y) * 2 + x}
+
+    def piece(k):
+        return pl.ds(pl.multiple_of(k * LINE, LINE), LINE)
+
+    def remote(src, dst, send, recv, to):
+        return pltpu.make_async_remote_copy(
+            src_ref=src, dst_ref=dst, send_sem=send, recv_sem=recv, device_id=to, device_id_type=MESH
+        )
+
+    local = pltpu.make_async_copy
+    load_total = local(dnp_any, total, total_sem)
+    load_lhs = local(n2t_any, lhs, lhs_sem)
+    right = (dg_any, du_any, act_any)
+    load_rhs = lambda i: local(right[i], rhs.at[i % 2], rhs_sem.at[i])
+    rows_of = lambda g: pl.ds(pl.multiple_of(g * LOAD, LOAD), LOAD)
+    load_h = lambda g: local(hid_any.at[rows_of(g)], hbuf.at[g % 2], h_sem.at[g])
+    load_c = lambda g: local(cot_any.at[rows_of(g)], cbuf.at[g % 2], c_sem.at[g])
+    save_sa = lambda e: local(sbuf.at[e % 2], sa_any.at[piece(e)], sa_sem.at[e])
+    save_dh = lambda e: local(dbuf.at[e % 2], dh_any.at[piece(e)], dh_sem.at[e])
+
+    load_lhs.start()
+    load_rhs(0).start()
+    load_rhs(1).start()
+    load_h(0).start()
+    load_c(0).start()
+
+    @pl.when(is_mid)
+    def _():
+        load_total.start()
+
+    barrier = pltpu.get_barrier_semaphore()
+    for to in (to_core, to_x, to_y, {"tp": partner}):
+        pl.semaphore_signal(barrier, inc=1, device_id=to, device_id_type=MESH)
+
+    @pl.when(is_mid)
+    def _():
+        pl.semaphore_signal(barrier, inc=1, device_id={"tp": across}, device_id_type=MESH)
+        pl.semaphore_wait(barrier, 5)
+
+    @pl.when(is_end)
+    def _():
+        pl.semaphore_wait(barrier, 4)
+        each(count, lambda k: to_mid(k).start())
+
+    gain_out[...] = jnp.zeros_like(gain_out)
+
+    @pl.when(is_mid)
+    def _():
+        load_total.wait()
+
+    def finish_rows(e):
+        per = LOAD // LINE
+        g = e // per
+
+        @pl.when(e % per == 0)
+        def _():
+            load_h(g).wait()
+            load_c(g).wait()
+
+            @pl.when(g + 1 < count // per)
+            def _():
+                load_h(g + 1).start()
+                load_c(g + 1).start()
+
+        @pl.when(e >= 2)
+        def _():
+            save_sa(e - 2).wait()
+            save_dh(e - 2).wait()
+
+        here = pl.ds(pl.multiple_of((e % per) * LINE, LINE), LINE)
+        live = live_ref[piece(e), :]
+
+        def grads_of(dn, h, dy, gain, factor, inner):
+            return dy * live + factor * (dn * gain) - h * (factor * factor * factor * inner)
+
+        dn = total[piece(e), :].astype(F32)
+        h = hbuf[g % 2, here, :].astype(F32)
+        factor = lax.rsqrt(jnp.mean(h * h, axis=1, keepdims=True) + EPS_NORM)
+        inner = jnp.mean(dn * gain_ref[...] * h, axis=1, keepdims=True)
+        dy = cbuf[g % 2, here, :].astype(F32)
+        sbuf[e % 2] = (RESIDUAL_SCALE * grads_of(dn, h, dy, gain_ref[...], factor, inner)).astype(BF)
+        own_dn = total[piece(e), mine].astype(F32)
+        own_h = hbuf[g % 2, here, mine].astype(F32)
+        own_dy = cbuf[g % 2, here, mine].astype(F32)
+        dbuf[e % 2] = grads_of(own_dn, own_h, own_dy, gain_ref[:, mine], factor, inner)
+        gain_out[...] += jnp.sum(own_dn * own_h * factor, axis=0, keepdims=True)
+        save_sa(e).start()
+        save_dh(e).start()
+
+    def serve(n):
+        @pl.when(jnp.logical_and(is_mid, n < count))
+        def _():
+            to_mid(n).wait_recv()
+            near[piece(n)] = (total[piece(n)].astype(F32) + near[piece(n)].astype(F32)).astype(BF)
+            over(n).start()
+
+        @pl.when(jnp.logical_and(is_mid, jnp.logical_and(n >= 1, n <= count)))
+        def _():
+            over(n - 1).wait_recv()
+            total[piece(n - 1)] = (near[piece(n - 1)].astype(F32) + cross[piece(n - 1)].astype(F32)).astype(BF)
+            to_end(n - 1).start()
+            finish_rows(n - 1)
+
+        @pl.when(jnp.logical_and(is_end, jnp.logical_and(n >= LAG, n < count + LAG)))
+        def _():
+            to_mid(n - LAG).wait_send()
+            to_end(n - LAG).wait_recv()
+            finish_rows(n - LAG)
+
+    def flip(v, by):
+        return v + by - 2 * v * by
+
+    def spot(j):
+        down, over_x = 1 - j // 2, 1 - j % 2
+        return down, over_x, flip(y, down), flip(x, over_x)
+
+    def tile(i, f, parity):
+        rows = pl.ds(pl.multiple_of((2 * f + parity) * block, 16), block)
+        return dot_nn(lhs[rows, :], rhs[i % 2])
+
+    upper, lower = pl.ds(0, half), pl.ds(half, half)
+    core_copy = lambda i, j, f: remote(stage.at[j % 2], cin.at[i, f], core_send.at[i, j], core_recv.at[i, f], to_core)
+    x_copy = lambda i, f, yy: remote(cin.at[i, f, upper], xin.at[i, yy], x_send.at[i, yy], x_recv.at[i, yy], to_x)
+    y2_copy = lambda i, f, xx: remote(cin.at[i, f, lower], yin2.at[i, xx], y2_send.at[i, xx], y2_recv.at[i, xx], to_y)
+    y_copy = lambda i: remote(xin.at[i, 1 - y], yin.at[i], y_send.at[i], y_recv.at[i], to_y)
+    x2_copy = lambda i: remote(yin2.at[i, 1 - x], xin2.at[i], x2_send.at[i], x2_recv.at[i], to_x)
+    save_upper = lambda i: local(yin.at[i], grad_any.at[i, upper], out_sem.at[i, 0])
+    save_lower = lambda i: local(xin2.at[i], grad_any.at[i, lower], out_sem.at[i, 1])
+
+    def plus(a, b):
+        return (a.astype(F32) + b.astype(F32)).astype(BF)
+
+    def products(i, n0):
+        def for_other(j):
+            _, _, yy, xx = spot(j)
+            f = yy * 2 + xx
+
+            @pl.when(j >= 2)
+            def _():
+                core_copy(i, j - 2, f).wait_send()
+
+            stage[j % 2] = tile(i, f, 1 - core).astype(BF)
+            core_copy(i, j, f).start()
+            serve(n0 + j)
+
+        each(4, for_other)
+
+        def for_own(j):
+            down, over_x, yy, xx = spot(j)
+            f = yy * 2 + xx
+            own = tile(i, f, core)
+            core_copy(i, j, f).wait_recv()
+            cin[i, f] = (own + cin[i, f].astype(F32)).astype(BF)
+
+            @pl.when(over_x == 1)
+            def _():
+                x_copy(i, f, yy).start()
+
+            @pl.when(down == 1)
+            def _():
+                y2_copy(i, f, xx).start()
+
+            serve(n0 + 4 + j)
+
+        each(4, for_own)
+        for j in (2, 3):
+            core_copy(i, j, 0).wait_send()
+
+    def first_stage(i):
+        x_copy(i, 0, 1 - y).wait_recv()
+        xin[i, 1 - y] = plus(xin[i, 1 - y], cin[i, (1 - y) * 2 + x, upper])
+        y_copy(i).start()
+        y2_copy(i, 0, 1 - x).wait_recv()
+        yin2[i, 1 - x] = plus(yin2[i, 1 - x], cin[i, y * 2 + 1 - x, lower])
+        x2_copy(i).start()
+        x_copy(i, 0, y).wait_recv()
+        xin[i, y] = plus(xin[i, y], cin[i, y * 2 + x, upper])
+        y2_copy(i, 0, x).wait_recv()
+        yin2[i, x] = plus(yin2[i, x], cin[i, y * 2 + x, lower])
+
+    def second_stage(i):
+        y_copy(i).wait_recv()
+        yin[i] = plus(yin[i], xin[i, y])
+        save_upper(i).start()
+        x2_copy(i).wait_recv()
+        xin2[i] = plus(xin2[i], yin2[i, x])
+        save_lower(i).start()
+
+    load_lhs.wait()
+    load_rhs(0).wait()
+    products(0, 0)
+    load_rhs(2).start()
+    load_rhs(1).wait()
+    products(1, 8)
+
+    cols_of = lambda c: pl.ds(pl.multiple_of(c * 256, 256), 256)
+    load_prep = lambda c: local(cot_any.at[:, cols_of(c)], prep.at[c % 2], prep_sem.at[c])
+    load_prep(0).start()
+    groups = D // 256
+
+    def turn(c):
+        load_prep(c).wait()
+
+        @pl.when(c + 1 < groups)
+        def _():
+            load_prep(c + 1).start()
+
+        seed = prep[c % 2].astype(F32) * (live_ref[...] * RESIDUAL_SCALE)
+        lhs[cols_of(c), :] = seed.T.astype(BF)
+        serve(16 + c)
+
+    each(groups, turn)
+    first_stage(0)
+    load_rhs(2).wait()
+    products(2, 16 + groups)
+    first_stage(1)
+    second_stage(0)
+    for n in range(24 + groups, count + LAG):
+        serve(n)
+    first_stage(2)
+    second_stage(1)
+    second_stage(2)
+    for i in range(3):
+        for v in range(2):
+            x_copy(i, 0, v).wait_send()
+            y2_copy(i, 0, v).wait_send()
+        y_copy(i).wait_send()
+        x2_copy(i).wait_send()
+        save_upper(i).wait()
+        save_lower(i).wait()
+    for e in (count - 2, count - 1):
+        save_sa(e).wait()
+        save_dh(e).wait()
+
+    @pl.when(is_mid)
+    def _():
+        def sent(k):
+            over(k).wait_send()
+            to_end(k).wait_send()
+
+        each(count, sent)
+
+
+def grad_reduce(live, gain, d_normed_part, hidden, cotangent, normed_t, d_gate, d_up, activation):
+    rows = hidden.shape[0]
+    units = d_gate.shape[1]
+    width = D // lax.axis_size("tp")
+    shard = D // (lax.axis_size("fsdp") * lax.axis_size("ctx"))
+    count = rows // LINE
+    vmem = pl.BlockSpec(memory_space=pltpu.VMEM)
+    anywhere = pl.BlockSpec(memory_space=pl.ANY)
+    dma = pltpu.SemaphoreType.DMA
+    scratch = lambda *shape: pltpu.VMEM(shape, BF)
+    return pl.pallas_call(
+        grad_kernel,
+        out_shape=[
+            jax.ShapeDtypeStruct((rows, D), BF),
+            jax.ShapeDtypeStruct((rows, width), F32),
+            jax.ShapeDtypeStruct((1, width), F32),
+            jax.ShapeDtypeStruct((3, shard, units), BF),
+        ],
+        in_specs=[vmem] * 2 + [anywhere] * 7,
+        out_specs=[anywhere, anywhere, vmem, anywhere],
+        scratch_shapes=[scratch(rows, D)] * 3
+        + [
+            scratch(3, 4, shard, units),
+            scratch(2, shard, units),
+            scratch(3, 2, shard // 2, units),
+            scratch(3, 2, shard // 2, units),
+            scratch(3, shard // 2, units),
+            scratch(3, shard // 2, units),
+            scratch(D, rows),
+            scratch(2, rows, units),
+            scratch(2, LOAD, D),
+            scratch(2, LOAD, D),
+            scratch(2, LINE, D),
+            pltpu.VMEM((2, LINE, width), F32),
+            scratch(2, rows, 256),
+        ]
+        + [dma, dma, dma((3,)), dma((rows // LOAD,)), dma((rows // LOAD,)), dma((count,)), dma((count,)), dma((D // 256,)), dma((3, 2))]
+        + [dma((3, 4))] * 2
+        + [dma((3, 2))] * 4
+        + [dma((3,))] * 4
+        + [dma((count,))] * 6,
+        compiler_params=pltpu.CompilerParams(collective_id=4, has_side_effects=True, vmem_limit_bytes=63 * MIB),
+        cost_estimate=pl.CostEstimate(flops=rows * D * units * 6, bytes_accessed=400 * MIB, transcendentals=0),
+        name="grad_reduce",
+    )(live, gain, d_normed_part, hidden, cotangent, normed_t, d_gate, d_up, activation)
 
 
 def swap_cores(v):
@@ -738,15 +1056,19 @@
         att_t = own_cols(att_flat)
 
     feature_owner = jnp.arange(D) // width
-    dy = cotangent.astype(F32) * live
-    mlp_seed = (RESIDUAL_SCALE * dy).astype(BF)
-    if n_tp == 4:
+    own_features = lambda v: lax.dynamic_slice_in_dim(v, tp * width, width, 1)
+    if n_tp == 4 and n_fsdp == 4:
         hidden, d_normed_part, mlp_part, normed_two_t, activation, d_gate, d_up = block_forward(
-            att_t.T, tokens, out_t, gain_mlp[None], mlp_seed, gate_up, ff_down_t
+            att_t.T, tokens, out_t, gain_mlp[None], live, cotangent, gate_up, ff_down_t
         )
-        hidden_f = hidden.astype(F32)
-        factor_two = lax.rsqrt(jnp.mean(hidden_f * hidden_f, axis=1, keepdims=True) + EPS_NORM)
+        attn_seed, d_hidden, grad_gain_mlp, grads = grad_reduce(
+            live, gain_mlp[None], d_normed_part, hidden, cotangent, normed_two_t, d_gate, d_up, activation
+        )
+        grad_gain_mlp = grad_gain_mlp[0]
+        grad_gate, grad_up, grad_down = grads[0], grads[1], grads[2]
     else:
+        dy = cotangent.astype(F32) * live
+        mlp_seed = (RESIDUAL_SCALE * dy).astype(BF)
         h_part = RESIDUAL_SCALE * dot_nt(att_t.T, out_t)
         h_part = h_part + jnp.where(
             (feature_owner == tp)[None], jnp.concatenate([inputs] * n_tp, axis=1), 0.0
@@ -755,7 +1077,6 @@
         hidden_f = hidden.astype(F32)
         factor_two = lax.rsqrt(jnp.mean(hidden_f * hidden_f, axis=1, keepdims=True) + EPS_NORM)
         normed_two = (hidden_f * factor_two * gain_mlp).astype(BF)
-        normed_two_t = normed_two.T
         gate_proj = dot_nn(normed_two, gate_up[0])
         up_proj = dot_nn(normed_two, gate_up[1])
         sigmoid_gate = jax.nn.sigmoid(gate_proj)
@@ -767,29 +1088,18 @@
         ).astype(BF)
         d_up = (d_activation * gate_proj * sigmoid_gate).astype(BF)
         d_normed_part = (dot_nt(d_gate, gate_up[0]) + dot_nt(d_up, gate_up[1])).astype(BF)
+        grad_down = scatter_grads(dot_tn(mlp_seed, activation).astype(BF))
+        grad_gate = scatter_grads(dot_tn(normed_two, d_gate).astype(BF))
+        grad_up = scatter_grads(dot_tn(normed_two, d_up).astype(BF))
+        d_normed = lax.psum(d_normed_part, "tp").astype(F32)
+        row_inner = jnp.mean(d_normed * gain_mlp * hidden_f, axis=1, keepdims=True)
+        d_hidden_full = dy + factor_two * d_normed * gain_mlp - hidden_f * (factor_two**3 * row_inner)
+        attn_seed = (RESIDUAL_SCALE * d_hidden_full).astype(BF)
+        d_hidden = own_features(d_hidden_full)
+        grad_gain_mlp = jnp.sum(own_features(d_normed * hidden_f) * factor_two, axis=0)
+    mlp_part, attn_seed = lax.optimization_barrier((mlp_part, attn_seed))
     mlp_out = lax.psum_scatter(mlp_part, "tp", scatter_dimension=1, tiled=True).astype(F32)
-    grads = (
-        dot_nn(mlp_seed.T, activation).astype(BF),
-        dot_nn(normed_two_t, d_gate).astype(BF),
-        dot_nn(normed_two_t, d_up).astype(BF),
-    )
-    d_normed_part, grads = lax.optimization_barrier((d_normed_part, grads))
-    d_normed = line_reduce(d_normed_part, 32, 1).astype(F32)
-    own_features = lambda v: lax.dynamic_slice_in_dim(v, tp * width, width, 1)
     layer_out = (own_features(hidden).astype(F32) + RESIDUAL_SCALE * mlp_out).astype(BF)
-
-    grad_down, grad_gate, grad_up = (scatter_grads(g) for g in grads)
-
-    row_inner = jnp.sum(d_normed * gain_mlp * hidden_f, axis=1, keepdims=True) / D
-    d_hidden_full = dy + factor_two * d_normed * gain_mlp - hidden_f * (factor_two**3 * row_inner)
-    attn_seed = (RESIDUAL_SCALE * d_hidden_full).astype(BF)
-    own_dn, own_h = own_features(d_normed), own_features(hidden).astype(F32)
-    d_hidden = (
-        own_features(cotangent).astype(F32) * live
-        + factor_two * own_dn * own_features(gain_mlp[None])
-        - own_h * (factor_two**3 * row_inner)
-    )
-    grad_gain_mlp = jnp.sum(own_dn * own_h * factor_two, axis=0)
     d_att_t = lax.dot_general(out_t, attn_seed, (((0,), (1,)), ((), ())), preferred_element_type=F32).astype(BF)
     grad_out = scatter_grads(dot_tn(attn_seed, att_t.T).astype(BF))
 

time: 1140 us -> 953 us (0.84)
  waiting for transfers between devices: 138 us -> 35.5 us
  Pallas kernels: 508 us -> 555 us
  matrix products: 72.5 us -> 28.1 us
  local copies, waits for them, and re-layouts: 144 us -> 99.7 us
  other arithmetic: 128 us -> 98.9 us
    pallas_call x0 -> x1, Pallas kernels: none -> 163 us  [grad_reduce(): pl.pallas_call(grad_kernel, out_shape=[jax.ShapeDtypeStruct((rows, D), BF...]
    pallas_call x3 -> x2, Pallas kernels: 250 us -> 132 us  [line_reduce(): pl.pallas_call(functools.partial(line_reduce_kernel, chunks), out_shape=j...]
    ppermute x38 -> x23, waiting for transfers between devices: 136 us -> 35.4 us  [keep_half(): other = lax.ppermute(take(v, 1 - which, axis), name, pairs)]
    dot_general x4 -> x1, matrix products: 49 us -> 3.46 us  [dot_nn(): lax.dot_general(a, b, (((1,), (0,)), ((), ())), preferred_element_type=F32)]
    optimization_barrier x3 -> x0, local copies, waits for them, and re-layouts: 36.3 us -> none  [local(): d_normed_part, grads = lax.optimization_barrier((d_normed_part, grads))]
    squeeze x36 -> x21, local copies, waits for them, and re-layouts: 19.7 us -> 1.76 us  [take(): return lax.dynamic_index_in_dim(v, which, axis, keepdims=False)]
    convert_element_type x38 -> x23, other arithmetic: 19.2 us -> 2.82 us  [add_up(): return (a.astype(F32) + b.astype(F32)).astype(BF)]
    convert_element_type x5 -> x1, other arithmetic: 18.2 us -> 2.79 us  [local(): (own_features(hidden).astype(F32) + RESIDUAL_SCALE * mlp_out).astype(BF)]
  transfers between devices with their start and end apart: 49 -> 34, of which waited for: 30 -> 17; matrix products, arithmetic and copies ran while one was open for 20% -> 19% of each run, Pallas kernels for 19% -> 23%
where the time goes in v2:
time: 953 us; the launch traced here: 946 us
  Pallas kernels  555 us (58%)
  local copies, waits for them, and re-layouts  99.7 us (10%)
  other arithmetic  98.9 us (10%)
  blocking collectives  82.5 us (9%)
  waiting for transfers between devices  35.5 us (4%)
  matrix products  28.1 us (3%)
  starting transfers between devices  23.4 us (2%)
  between operations  22.9 us (2%)
    pallas_call x1, Pallas kernels, block_forward(): pl.pallas_call(block_kernel, out_shape=[wide, wide, wide, jax.ShapeDtypeS...  175 us
    pallas_call x1, Pallas kernels, grad_reduce(): pl.pallas_call(grad_kernel, out_shape=[jax.ShapeDtypeStruct((rows, D), BF...  163 us
    pallas_call x2, Pallas kernels, line_reduce(): pl.pallas_call(functools.partial(line_reduce_kernel, chunks), out_shape=j...  132 us
    pallas_call x1, Pallas kernels, attend_backward(): pl.pallas_call(attend_backward_kernel, grid=(heads, rows // BQ), in_specs...  47.6 us
    unnamed x209, local copies, waits for them, and re-layouts  38.4 us
    psum x1, blocking collectives, local(): lax.psum(jnp.concatenate([placed_gains.reshape(-1), latent_gains, squares...  37.9 us
    pallas_call x1, Pallas kernels, attend_forward(): pl.pallas_call(attend_forward_kernel, grid=(heads, rows // BQ), in_specs=...  37.6 us
    ppermute x23, waiting for transfers between devices, keep_half(): other = lax.ppermute(take(v, 1 - which, axis), name, pairs)  35.4 us
  transfers between devices with their start and end apart: 34, of which 17 were waited for; matrix products, arithmetic and copies ran while one was open for 19% of the time, Pallas kernels for 23%

profile of v2, /device:TPU:0, one launch (start us, length us, event | category | flops | bytes accessed | tf_op | source)
XLA Modules:
  0.0 946.3 jit_solution(1351043628053979719)
XLA Ops:
  12.4 3.8 convert_element_type.547
  16.3 10.2 %all-gather.1 = bf16[8,1,128]{2,1,0:T(2,128)(2,1)S(1)} all-gather(bf16[1,1,128]{2,1,0:T(2,128)(2,1)S(1)} %convert_bitcast_fusion.9), channel_id=1, replica_groups=mesh['fsdp'=4,'ctx'=2,'tp'=4] {'fsdp','ctx'}, dimensions={0}, use_global_device_ids=true | all-gather | bytes 2304 | tf_op jit(solution)/shard_map/all_gather | solution.py:979
  27.1 11.3 %all-gather = bf16[8,36,640]{2,1,0:T(8,128)(2,1)S(1)} all-gather(bf16[1,36,640]{2,1,0:T(8,128)(2,1)S(1)} %convert_bitcast_fusion.7), channel_id=1, replica_groups=mesh['fsdp'=4,'ctx'=2,'tp'=4] {'fsdp','ctx'}, dimensions={0}, use_global_device_ids=true | all-gather | bytes 414720 | tf_op jit(solution)/shard_map/all_gather | solution.py:898
  38.5 10.1 %all_gather.24 = bf16[768,640]{1,0:T(8,128)(2,1)S(1)} all-gather(bf16[96,640]{1,0:T(8,128)(2,1)S(1)} %convert_bitcast_fusion.5), channel_id=1, replica_groups=mesh['fsdp'=4,'ctx'=2,'tp'=4] {'fsdp','ctx'}, dimensions={0}, use_global_device_ids=true | all-gather | bytes 1105920 | tf_op jit(solution)/shard_map/all_gather | solution.py:898
  58.7 3.5 concatenate.104
  64.5 68.5 %line_reduce.2 = bf16[1088,1152]{1,0:T(8,128)(2,1)S(1)} custom-call(bf16[1088,1152]{1,0:T(8,128)(2,1)S(1)} %fusion.8.x_ref), custom_call_target="tpu_custom_call" | custom-call | flops 2506752 | bytes 50135040 | tf_op jit(solution)/shard_map/line_reduce/pallas_call | solution.py:143
  137.4 3.7 multiply_cosine_fusion
  145.6 4.6 concatenate.106
  150.3 4.2 copy.159
  160.8 13.0 %all_gather.28 = bf16[256,1280]{1,0:T(8,128)(2,1)S(1)} all-gather(bf16[32,1280]{1,0:T(8,128)(2,1)S(1)} %convert_element_type.541), channel_id=1, replica_groups=mesh['fsdp'=4,'ctx'=2,'tp'=4] {'fsdp','ctx'}, dimensions={0}, use_global_device_ids=true | all-gather | bytes 737280 | tf_op jit(solution)/shard_map/all_gather | solution.py:898
  176.6 4.1 copy.160
  180.8 5.5 maximum_select_fusion
  204.3 37.6 %attend_forward.1 = (bf16[5,64,2048]{2,1,0:T(8,128)(2,1)S(1)}, f32[5,1,2048]{2,1,0:T(1,128)S(1)}, bf16[5,128,2048]{2,1,0:T(8,128)(2,1)S(1)}, bf16[5,2048,128]{2,1,0:T(8,128)(2,1)S(1)}, bf16[5,80,2048]{2,1,0:T(8,128)(2,1)S(1)}) custom-call(bf16[2048,768]{1,0:T(8,128)(2,1)S(1)} %copy-done, bf16[2048,256]{1,0:T(8,128)(2,1)S(1)} %slice.198.kn_ref, ...), custom_call_target="tpu_custom_call" | custom-call | flops 6710886400 | bytes 31457280 | tf_op jit(solution)/shard_map/attend_forward/pallas_call | solution.py:213
  256.5 175.4 %block_forward.1 = (bf16[1024,2560]{1,0:T(8,128)(2,1)}, bf16[1024,2560]{1,0:T(8,128)(2,1)}, bf16[1024,2560]{1,0:T(8,128)(2,1)}, bf16[2560,1024]{1,0:T(8,128)(2,1...) custom-call(bf16[1024,640]{1,0:T(8,128)(2,1)} %fusion.42.att_ref, ...), custom_call_target="tpu_custom_call" | custom-call | flops 50331648000 | bytes 419430400 | tf_op jit(solution)/shard_map/block_forward/pallas_call | solution.py:553
  431.9 163.2 %grad_reduce.1 = (bf16[1024,2560]{1,0:T(8,128)(2,1)}, f32[1024,640]{1,0:T(8,128)}, f32[1,640]{1,0:T(1,128)}, bf16[3,320,1600]{2,1,0:T(8,128)(2,1)}) custom-call(f32[1024,1]{1,0:T(8,128)} %copy.171.live_ref, f32[1,2560]{1,0:T(1,128)} %bitcast.309, bf16[1024,2560]{1,0:T(8,128)(2,1)} %get-tuple-element.60.dnp_any, ...), custom_call_target="tpu_custom_call" | custom-call | flops 25165824000 | bytes 419430400 | tf_op jit(solution)/shard_map/grad_reduce/pallas_call | solution.py:850
  595.2 7.6 convolution_convert_fusion
  602.8 3.6 convolution_convert_fusion.3
  608.4 8.3 copy.191
  616.8 3.8 multiply_reduce_fusion.5
  620.6 3.7 multiply_reduce_fusion.1
  626.0 47.6 %attend_backward.1 = (bf16[480,2048]{1,0:T(8,128)(2,1)S(1)}, bf16[2048,640]{1,0:T(8,128)(2,1)S(1)}, f32[2048,128]{1,0:T(8,128)S(1)}) custom-call(bf16[5,128,2048]{2,1,0:T(8,128)(2,1)S(1)} %copy-done.13, bf16[5,2048,128]{2,1,0:T(8,128)(2,1)} %copy-done.14, bf16[5,80,2048]{2,1,0:T(8,128)(2,1)S(1)} %copy-done.16, bf16[5,64,2048]{2,1,0:T(8,128)(2,1)S(1)} %copy-done.2, ...), custom_call_target="tpu_custom_call" | custom-call | flops 18874368000 | bytes 31457280 | tf_op jit(solution)/shard_map/attend_backward/pallas_call | solution.py:295
  683.2 6.4 pad_maximum_fusion
  724.8 5.8 collective-permute-done.25
  733.0 3.6 collective-permute-done.26
  745.8 63.1 %line_reduce.3 = bf16[1024,1152]{1,0:T(8,128)(2,1)S(1)} custom-call(bf16[1024,1152]{1,0:T(8,128)(2,1)S(1)} %pad.19.x_ref), custom_call_target="tpu_custom_call" | custom-call | flops 2359296 | bytes 47185920 | tf_op jit(solution)/shard_map/line_reduce/pallas_call | solution.py:143
  815.3 5.5 concatenate.119
  820.8 4.5 multiply_reduce_fusion
  829.7 3.5 fusion.7
  857.4 4.6 concatenate.135
  862.0 37.9 %psum.7 = f32[6151]{0:T(1024)S(1)} all-reduce(f32[6151]{0:T(1024)S(1)} %concatenate.135), channel_id=1, replica_groups=mesh['fsdp'=4,'ctx'=2,'tp'=4] {'fsdp','ctx','tp'}, use_global_device_ids=true, to_apply=%region_18.19 | all-reduce | flops 6151 | bytes 49208 | tf_op jit(solution)/shard_map/psum | solution.py:1164
  921.4 3.9 multiply_subtract_fusion.2
  927.0 7.9 multiply_subtract_fusion
  (460 shorter events, 183.6 us)
Async XLA Ops:
  7.2 183.7 %all-gather.7.cloned.1.call-start = ((), (), s32[]{:S(2)}) async-start(), calls=%async_computation.1 | async-start | bytes 1769472 | tf_op jit(solution)/shard_map/all_gather | solution.py:898
  9.1 247.4 %all-gather.9.cloned.1.call-start = ((), (), s32[]{:S(2)}) async-start(), calls=%async_computation.2 | async-start | bytes 3686400 | tf_op jit(solution)/shard_map/all_gather | solution.py:898
  11.2 245.4 %all-gather.13.cloned.1.call-start = ((), (), s32[]{:S(2)}) async-start(), calls=%async_computation.4 | async-start | bytes 9584640 | tf_op jit(solution)/shard_map/all_gather | solution.py:898
  12.4 244.2 %all-gather.11.cloned.1.call-start = ((), (), s32[]{:S(2)}) async-start(), calls=%async_computation.3 | async-start | bytes 19169280 | tf_op jit(solution)/shard_map/all_gather | solution.py:981
  16.2 918.8 %reduce-scatter.4.cloned.1.call-start = ((), (), s32[]{:S(2)}) async-start(), calls=%async_computation.5 | async-start | bytes 6553600
  154.5 22.1 %collective-permute-start = (bf16[1024,1056]{0,1:T(8,128)(2,1)}, bf16[1024,1056]{0,1:T(8,128)(2,1)}, u32[]{:S(2)}, u32[]{:S(2)}) collective-permute-start(bf16[1024,1056]{0,1:T(8,128)(2,1)} %copy.159), channel_id=1, source_target_pairs={{0,4},{4,0},{1,5},{5,1},{2,6},{6,2},{3,7},{7,3},{8,12},{12,8},{9,1... | collective-permute-start | bytes 6488072 | tf_op jit(solution)/shard_map/ppermute | solution.py:888
  248.1 4.0 collective-permute-start.1
  606.5 17.7 %collective-permute-start.2 = (bf16[320,1024]{1,0:T(8,128)(2,1)S(1)}, bf16[320,1024]{1,0:T(8,128)(2,1)S(1)}, u32[]{:S(2)}, u32[]{:S(2)}) collective-permute-start(bf16[320,1024]{1,0:T(8,128)(2,1)S(1)} %get-tuple-element.132), channel_id=1, source_target_pairs={{0,4},{4,0},{1,5},{5,1},{2,6},{6,2},{3,7},{7,3},{8,12},{12,8},{9,1... | collective-permute-start | bytes 1966088 | tf_op jit(solution)/shard_map/ppermute | solution.py:888
  607.9 111.2 %collective-permute-start.24 = (bf16[4,320,640]{2,1,0:T(8,128)(2,1)}, bf16[4,320,640]{2,1,0:T(8,128)(2,1)}, u32[]{:S(2)}, u32[]{:S(2)}) collective-permute-start(bf16[4,320,640]{2,1,0:T(8,128)(2,1)} %dynamic-slice_bitcast_fusion), channel_id=1, source_target_pairs={{0,4},{4,0},{1,5},{5,1},{2,6},{6,2},{3,7},{7,3},{8,12},{12,8},{9,1... | collective-permute-start | bytes 4915208 | tf_op jit(solution)/shard_map/ppermute | solution.py:914
  678.4 17.5 %collective-permute-start.19 = (bf16[4,32,640]{2,1,0:T(8,128)(2,1)S(1)}, bf16[4,32,640]{2,1,0:T(8,128)(2,1)}, u32[]{:S(2)}, u32[]{:S(2)}) collective-permute-start(bf16[4,32,640]{2,1,0:T(8,128)(2,1)S(1)} %get-tuple-element.144), channel_id=1, source_target_pairs={{0,4},{4,0},{1,5},{5,1},{2,6},{6,2},{3,7},{7,3},{8,12},{12,8},{9,1... | collective-permute-start | bytes 491528 | tf_op jit(solution)/shard_map/ppermute | solution.py:888
  694.8 45.1 %collective-permute-start.3 = (bf16[1024,1056]{0,1:T(8,128)(2,1)}, bf16[1024,1056]{0,1:T(8,128)(2,1)}, u32[]{:S(2)}, u32[]{:S(2)}) collective-permute-start(bf16[1024,1056]{0,1:T(8,128)(2,1)} %copy.177), channel_id=1, source_target_pairs={{0,4},{4,0},{1,5},{5,1},{2,6},{6,2},{3,7},{7,3},{8,12},{12,8},{9,1... | collective-permute-start | bytes 6488072 | tf_op jit(solution)/shard_map/ppermute | solution.py:888
  695.8 12.2 %collective-permute-start.14 = (bf16[4,96,480]{2,1,0:T(8,128)(2,1)S(1)}, bf16[4,96,480]{2,1,0:T(8,128)(2,1)S(1)}, u32[]{:S(2)}, u32[]{:S(2)}) collective-permute-start(bf16[4,96,480]{2,1,0:T(8,128)(2,1)S(1)} %get-tuple-element.138), channel_id=1, source_target_pairs={{0,4},{4,0},{1,5},{5,1},{2,6},{6,2},{3,7},{7,3},{8,12},{12,8},{9,1... | collective-permute-start | bytes 1105928 | tf_op jit(solution)/shard_map/ppermute | solution.py:888
  697.0 4.9 collective-permute-start.20
  697.4 6.5 collective-permute-start.22
  702.0 4.1 collective-permute-start.21
  703.9 4.1 collective-permute-start.23
  708.6 5.7 collective-permute-start.15
  710.3 6.8 collective-permute-start.17
  714.4 4.7 collective-permute-start.16
  717.1 4.9 collective-permute-start.18
  721.2 9.4 collective-permute-start.25
  722.1 10.1 %collective-permute-start.27 = (bf16[2,160,640]{2,1,0:T(8,128)(2,1)S(1)}, bf16[2,160,640]{2,1,0:T(8,128)(2,1)S(1)}, u32[]{:S(2)}, u32[]{:S(2)}) collective-permute-start(bf16[2,160,640]{2,1,0:T(8,128)(2,1)S(1)} %dynamic-slice_bitcast_fusion.4), channel_id=1, source_target_pairs={{0,16},{16,0},{8,24},{24,8},{1,17},{17,1},{9,25},{25,9},{2,18},{18... | collective-permute-start | bytes 1228808 | tf_op jit(solution)/shard_map/ppermute | solution.py:914
  730.8 5.8 collective-permute-start.26
  732.3 5.8 collective-permute-start.28
  833.5 12.2 %collective-permute-start.4 = (bf16[4,96,640]{2,1,0:T(8,128)(2,1)S(1)}, bf16[4,96,640]{2,1,0:T(8,128)(2,1)S(1)}, u32[]{:S(2)}, u32[]{:S(2)}) collective-permute-start(bf16[4,96,640]{2,1,0:T(8,128)(2,1)S(1)} %dynamic-slice_bitcast_fusion.3), channel_id=1, source_target_pairs={{0,4},{4,0},{1,5},{5,1},{2,6},{6,2},{3,7},{7,3},{8,12},{12,8},{9,1... | collective-permute-start | bytes 1474568 | tf_op jit(solution)/shard_map/ppermute | solution.py:914
  835.5 4.3 collective-permute-start.10
  837.4 4.1 collective-permute-start.12
  841.7 4.0 collective-permute-start.13
  846.0 4.9 collective-permute-start.5
  846.9 5.4 collective-permute-start.7
  851.0 4.3 collective-permute-start.6
  852.4 4.3 collective-permute-start.8
  (102 other events, 1572.9 us)
Sparse Core Ops, SparseCore 0:
  10.5 29.4 all-gather.6
  42.5 32.8 all-gather.8
  77.9 54.9 all-gather.12
  135.2 93.5 all-gather.10
  616.9 95.6 reduce-scatter.3

commit v3 on v2

--- a/solution.py
+++ b/solution.py
@@ -18,6 +18,7 @@
 STEP = 3
 HEAD = NOPE + ROPE
 LAT = QR + KVR + ROPE
+LAT_WIDE = 1152
 
 EPS_NORM = 1e-05
 RESIDUAL_SCALE = 1.4 / 62**0.5
@@ -50,124 +51,30 @@
     return lax.dot_general(a, b, (((0,), (0,)), ((), ())), preferred_element_type=F32)
 
 
-def line_reduce_kernel(chunks, x_ref, o_ref, near, cross, part, in_send, in_recv, mid_send, mid_recv, out_send, out_recv):
-    z = lax.axis_index("tp")
-    rows = x_ref.shape[0] // chunks
-    is_end = jnp.logical_or(z == 0, z == 3)
-    is_mid = jnp.logical_not(is_end)
-    partner = jnp.where(z == 0, 1, jnp.where(z == 3, 2, jnp.where(z == 1, 0, 3)))
-    across = jnp.where(z == 1, 2, 1)
-
-    barrier = pltpu.get_barrier_semaphore()
-    pl.semaphore_signal(barrier, inc=1, device_id={"tp": partner}, device_id_type=MESH)
-
-    @pl.when(is_mid)
-    def _():
-        pl.semaphore_signal(barrier, inc=1, device_id={"tp": across}, device_id_type=MESH)
-        pl.semaphore_wait(barrier, 2)
-
-    @pl.when(is_end)
-    def _():
-        pl.semaphore_wait(barrier, 1)
-
-    def piece(k):
-        return pl.ds(pl.multiple_of(k * rows, rows), rows)
-
-    def to_mid(k):
-        return pltpu.make_async_remote_copy(
-            src_ref=x_ref.at[piece(k)], dst_ref=near.at[piece(k)], send_sem=in_send.at[k], recv_sem=in_recv.at[k],
-            device_id={"tp": partner}, device_id_type=MESH,
-        )
-
-    def over(k):
-        return pltpu.make_async_remote_copy(
-            src_ref=part.at[piece(k)], dst_ref=cross.at[piece(k)], send_sem=mid_send.at[k], recv_sem=mid_recv.at[k],
-            device_id={"tp": across}, device_id_type=MESH,
-        )
-
-    def to_end(k):
-        return pltpu.make_async_remote_copy(
-            src_ref=o_ref.at[piece(k)], dst_ref=o_ref.at[piece(k)], send_sem=out_send.at[k], recv_sem=out_recv.at[k],
-            device_id={"tp": partner}, device_id_type=MESH,
-        )
-
-    @pl.when(is_end)
-    def _():
-        def begin(k, carry):
-            to_mid(k).start()
-            return carry
-
-        def finish(k, carry):
-            to_mid(k).wait_send()
-            to_end(k).wait_recv()
-            return carry
-
-        lax.fori_loop(0, chunks, begin, 0)
-        lax.fori_loop(0, chunks, finish, 0)
-
-    @pl.when(is_mid)
-    def _():
-        def first(k):
-            to_mid(k).wait_recv()
-            part[piece(k)] = (x_ref[piece(k)].astype(F32) + near[piece(k)].astype(F32)).astype(BF)
-            over(k).start()
-
-        def second(k):
-            over(k).wait_recv()
-            o_ref[piece(k)] = (part[piece(k)].astype(F32) + cross[piece(k)].astype(F32)).astype(BF)
-            to_end(k).start()
-
-        first(0)
-
-        def step(k, carry):
-            first(k)
-            second(k - 1)
-            return carry
-
-        lax.fori_loop(1, chunks, step, 0)
-        second(chunks - 1)
-
-        def finish(k, carry):
-            over(k).wait_send()
-            to_end(k).wait_send()
-            return carry
-
-        lax.fori_loop(0, chunks, finish, 0)
-
-
-def line_reduce(x, chunks, collective_id):
-    if lax.axis_size("tp") != 4:
-        return lax.psum(x, "tp")
-    rows, cols = x.shape
-    dma = pltpu.SemaphoreType.DMA((chunks,))
-    return pl.pallas_call(
-        functools.partial(line_reduce_kernel, chunks),
-        out_shape=jax.ShapeDtypeStruct((rows, cols), BF),
-        in_specs=[pl.BlockSpec(memory_space=pltpu.VMEM)],
-        out_specs=pl.BlockSpec(memory_space=pltpu.VMEM),
-        scratch_shapes=[pltpu.VMEM((rows, cols), BF)] * 3 + [dma] * 6,
-        compiler_params=pltpu.CompilerParams(
-            collective_id=collective_id, has_side_effects=True, vmem_limit_bytes=40 * MIB
-        ),
-        cost_estimate=pl.CostEstimate(flops=rows * cols * 2, bytes_accessed=rows * cols * 40, transcendentals=0),
-        name="line_reduce",
-    )(x)
-
-
 BQ = 512
 
 
 def attend_forward_kernel(
-    qn_ref, kn_ref, krx_ref, cos_ref, sin_ref, segq_ref, wq_ref, wk_ref, wv_ref, o_ref, lse_ref, q_ref, k_ref, v_ref
+    lat_ref, cos_ref, sin_ref, segq_ref, up_ref, o_ref, lse_ref, q_ref, k_ref, v_ref, stack_q, stack_kv, wq_t
 ):
     i = pl.program_id(1)
-    rows = qn_ref.shape[0]
+    rows = lat_ref.shape[0]
+    pieces = up_ref.shape[0]
+    nq, nk = QR // pieces, KVR // pieces
 
     @pl.when(i == 0)
     def _():
+        for p in range(pieces):
+            stack_q[p * nq : (p + 1) * nq, :] = up_ref[p, 0:nq, :].astype(F32)
+            stack_kv[p * nk : (p + 1) * nk, :] = up_ref[p, nq : nq + nk, :].astype(F32)
+        wq_t[...] = stack_q[...].T.astype(BF)
+        kv = stack_kv[...]
+        wk = jnp.where(lax.broadcasted_iota(jnp.int32, kv.shape, 1) < NOPE, kv, 0.0).astype(BF)
+        wv_t = kv.T[NOPE:128].astype(BF)
         for r in range(rows // BQ):
             part = pl.ds(r * BQ, BQ)
-            qf = dot_nt(wq_ref[0], qn_ref[part, :]) * (LOG2E * HEAD**-0.5)
+            kn = lat_ref[part, QR : QR + KVR]
+            qf = dot_nt(wq_t[...], lat_ref[part, 0:QR]) * (LOG2E * HEAD**-0.5)
             cos = cos_ref[:, part]
             sin = sin_ref[:, part]
             one, two = qf[NOPE : NOPE + 16], qf[NOPE + 16 : HEAD]
@@ -176,10 +83,10 @@
             q_ref[0, NOPE + 16 : HEAD, part] = (two * cos + one * sin).astype(BF)
             q_ref[0, HEAD : HEAD + 16, part] = segq_ref[:, part]
             q_ref[0, HEAD + 16 : 128, part] = jnp.zeros((16, BQ), BF)
-            k_ref[0, part, :] = (dot_nn(kn_ref[part, :], wk_ref[0]) + krx_ref[part, :].astype(F32)).astype(BF)
-            vt = dot_nt(wv_ref[0], kn_ref[part, :])
-            row = lax.broadcasted_iota(jnp.int32, vt.shape, 0)
-            v_ref[0, :, part] = jnp.where(row == VD, 1.0, vt).astype(BF)
+            k_ref[0, part, :] = (dot_nn(kn, wk) + lat_ref[part, QR + KVR : LAT_WIDE].astype(F32)).astype(BF)
+            v_ref[0, 0:VD, part] = dot_nt(wv_t, kn).astype(BF)
+            ones = lax.broadcasted_iota(jnp.int32, (16, BQ), 0) == 0
+            v_ref[0, VD : VD + 16, part] = ones.astype(F32).astype(BF)
 
     here = pl.ds(pl.multiple_of(i * BQ, BQ), BQ)
     q = q_ref[0, :, here]
@@ -205,16 +112,16 @@
     lse_ref[0, :, here] = m + jnp.log2(total)
 
 
-def attend_forward(qn, kn, krx, cos, sin, segq, wq, wk, wv):
-    heads = wq.shape[0]
-    rows = qn.shape[0]
+def attend_forward(lat, cos, sin, segq, up):
+    heads = up.shape[2] // 128
+    rows = lat.shape[0]
     whole = lambda a: pl.BlockSpec(a.shape, lambda h, i: (0,) * a.ndim)
     per_head = lambda a, b: pl.BlockSpec((1, a, b), lambda h, i: (h, 0, 0))
     return pl.pallas_call(
         attend_forward_kernel,
         grid=(heads, rows // BQ),
-        in_specs=[whole(qn), whole(kn), whole(krx), whole(cos), whole(sin), whole(segq)]
-        + [per_head(*w.shape[1:]) for w in (wq, wk, wv)],
+        in_specs=[whole(lat), whole(cos), whole(sin), whole(segq)]
+        + [pl.BlockSpec((up.shape[0], up.shape[1], 128), lambda h, i: (0, 0, h))],
         out_specs=[per_head(VD, rows), per_head(1, rows), per_head(128, rows), per_head(rows, 128), per_head(80, rows)],
         out_shape=[
             jax.ShapeDtypeStruct((heads, VD, rows), BF),
@@ -223,10 +130,11 @@
             jax.ShapeDtypeStruct((heads, rows, 128), BF),
             jax.ShapeDtypeStruct((heads, 80, rows), BF),
         ],
+        scratch_shapes=[pltpu.VMEM((QR, 128), F32), pltpu.VMEM((KVR, 128), F32), pltpu.VMEM((128, QR), BF)],
         compiler_params=pltpu.CompilerParams(vmem_limit_bytes=40 * MIB),
         cost_estimate=pl.CostEstimate(flops=heads * rows * rows * 320, bytes_accessed=30 * MIB, transcendentals=0),
         name="attend_forward",
-    )(qn, kn, krx, cos, sin, segq, wq, wk, wv)
+    )(lat, cos, sin, segq, up)
 
 
 def attend_backward_kernel(q_ref, k_ref, v_ref, o_ref, do_ref, lse_ref, cos_ref, sin_ref, dq_ref, de_ref, dkr_ref, dq_acc, delta):
@@ -279,12 +187,15 @@
 
     @pl.when(j == blocks - 1)
     def _():
-        dq = dq_acc[...] * HEAD**-0.5
-        cos, sin = cos_ref[...], sin_ref[...]
-        one, two = dq[NOPE : NOPE + 16], dq[NOPE + 16 : HEAD]
-        dq_ref[0:NOPE, :] = dq[:NOPE].astype(BF)
-        dq_ref[NOPE : NOPE + 16, :] = (one * cos + two * sin).astype(BF)
-        dq_ref[NOPE + 16 : HEAD, :] = (two * cos - one * sin).astype(BF)
+        for r in range(blocks):
+            part = pl.ds(r * BQ, BQ)
+            dq = dq_acc[:, part] * HEAD**-0.5
+            cos, sin = cos_ref[:, part], sin_ref[:, part]
+            one, two = dq[NOPE : NOPE + 16], dq[NOPE + 16 : HEAD]
+            dq = jnp.concatenate(
+                [dq[:NOPE], one * cos + two * sin, two * cos - one * sin, jnp.zeros((128 - HEAD, BQ), F32)], axis=0
+            )
+            dq_ref[part, :] = dq.T.astype(BF)
 
 
 def attend_backward(q, k, v, o, do, lse, cos, sin):
@@ -297,12 +208,12 @@
         grid=(heads, rows // BQ),
         in_specs=[per_head(a) for a in (q, k, v, o, do, lse)] + [whole(cos), whole(sin)],
         out_specs=[
-            pl.BlockSpec((HEAD, rows), lambda h, i: (h, 0)),
+            pl.BlockSpec((rows, 128), lambda h, i: (0, h)),
             pl.BlockSpec((rows, 128), lambda h, i: (0, h)),
             pl.BlockSpec((rows, 128), lambda h, i: (0, 0)),
         ],
         out_shape=[
-            jax.ShapeDtypeStruct((heads * HEAD, rows), BF),
+            jax.ShapeDtypeStruct((rows, heads * 128), BF),
             jax.ShapeDtypeStruct((rows, heads * 128), BF),
             jax.ShapeDtypeStruct((rows, 128), F32),
         ],
@@ -313,6 +224,233 @@
     )(q, k, v, o, do, lse, cos, sin)
 
 
+LAT_LINE = 64
+PIECE = 160
+
+
+def latent_kernel(
+    x_ref, gain_ref, gain2_ref, piece_ref, up_ref, sel_ref, freq_col, freq_lane, len_ref,
+    w_ref, total, lat_ref, cos_ref, sin_ref, segq_ref, upg_ref, tcos, tsin, gains,
+    gat, xb, near, cross, kvg,
+    w_send, w_recv, u_send, u_recv, c_send, c_recv, *sems,
+):
+    z, core, place = lax.axis_index("tp"), lax.axis_index("ctx"), lax.axis_index("fsdp")
+    is_end, is_mid, partner, across = line_places(z)
+    to_mid, over, to_end, first, second = line_copies(xb, near, cross, total, sems, partner, across, LAT_LINE)
+    count = xb.shape[0] // LAT_LINE
+    rows = x_ref.shape[0]
+    peers = gat.shape[0]
+    me = place * 2 + core
+
+    def remote(src, dst, send, recv, to):
+        return pltpu.make_async_remote_copy(
+            src_ref=src, dst_ref=dst, send_sem=send, recv_sem=recv, device_id=to, device_id_type=MESH
+        )
+
+    def peer(d):
+        to = lax.rem(me + d, peers)
+        return {"fsdp": to // 2, "ctx": lax.rem(to, 2)}
+
+    barrier = pltpu.get_barrier_semaphore()
+    for d in range(1, peers):
+        pl.semaphore_signal(barrier, inc=1, device_id=peer(d), device_id_type=MESH)
+    pl.semaphore_signal(barrier, inc=1, device_id={"tp": partner}, device_id_type=MESH)
+
+    @pl.when(is_mid)
+    def _():
+        pl.semaphore_signal(barrier, inc=1, device_id={"tp": across}, device_id_type=MESH)
+        pl.semaphore_wait(barrier, peers + 1)
+
+    @pl.when(is_end)
+    def _():
+        pl.semaphore_wait(barrier, peers)
+
+    def w_copy(d, source):
+        return remote(piece_ref, gat.at[source], w_send.at[d], w_recv.at[source], peer(d))
+
+    def u_copy(d, source):
+        return remote(up_ref.at[lax.rem(me + d, 2)], upg_ref.at[source], u_send.at[d], u_recv.at[source], peer(d))
+
+    for d in range(1, peers):
+        w_copy(d, me).start()
+    for d in range(1, peers):
+        u_copy(d, me).start()
+    gat[me] = piece_ref[...]
+    upg_ref[me] = up_ref[core]
+
+    length = len_ref[0, 0]
+    slot = cos_ref.shape[1]
+    index = lax.broadcasted_iota(jnp.int32, (1, slot), 1)
+    segment = (index >= length).astype(jnp.int32)
+    angle = freq_col[...] * (index - segment * length).astype(F32)
+    cos_ref[...] = jnp.cos(angle)
+    sin_ref[...] = jnp.sin(angle)
+    row16 = lax.broadcasted_iota(jnp.int32, (16, slot), 0)
+    seg_f = segment.astype(F32)
+    segq_ref[...] = jnp.where(row16 == 0, seg_f, jnp.where(row16 == 1, 1.0 - seg_f, 0.0)).astype(BF)
+    lane = lax.broadcasted_iota(jnp.int32, (1, 128), 1)
+    in_rope = jnp.logical_and(lane >= NOPE, lane < HEAD)
+
+    def own_index(e):
+        at = core * rows + e * LAT_LINE
+        return at + lax.broadcasted_iota(jnp.int32, (LAT_LINE, 1), 0)
+
+    def table(e):
+        here = pl.ds(pl.multiple_of(e * LAT_LINE, LAT_LINE), LAT_LINE)
+        at = own_index(e)
+        seg = (at >= length).astype(jnp.int32)
+        turn = (at - seg * length).astype(F32) * freq_lane[...]
+        tcos[here, :] = jnp.where(in_rope, jnp.cos(turn), 0.0)
+        tsin[here, :] = jnp.where(in_rope, jnp.sin(turn), 0.0)
+
+    each(rows // LAT_LINE, table)
+
+    for d in range(1, peers):
+        w_copy(d, lax.rem(me + peers - d, peers)).wait_recv()
+    for p in range(peers):
+        w_ref[p * 96 : (p + 1) * 96, :] = gat[p, 0:96, :]
+        kvg[p * 48 : (p + 1) * 48, :] = gat[p, 96:144, :]
+        gains[:, p * 128 : (p + 1) * 128] = gat[p, 144:160, 0:128].astype(F32)
+    w_ref[QR:LAT, :] = dot_nn(sel_ref[...], kvg[...]).astype(BF)
+    w_ref[LAT:LAT_WIDE, :] = jnp.zeros((LAT_WIDE - LAT, w_ref.shape[1]), BF)
+
+    wide_lane = lax.broadcasted_iota(jnp.int32, (1, LAT_WIDE), 1)
+    per = 128
+
+    def project(r):
+        here = pl.ds(pl.multiple_of(r * per, per), per)
+        x = x_ref[here, :].astype(F32)
+        square = jnp.sum(x * x, axis=1, keepdims=True)
+        high = square.astype(BF).astype(F32)
+        part = dot_nt((x * gain_ref[...]).astype(BF), w_ref[...])
+        part = jnp.where(wide_lane == LAT + 2 * z, high, jnp.where(wide_lane == LAT + 2 * z + 1, square - high, part))
+        xb[here, :] = part.astype(BF)
+
+        @pl.when(is_end)
+        def _():
+            for n in range(per // LAT_LINE):
+                to_mid(r * (per // LAT_LINE) + n).start()
+
+    each(rows // per, project)
+    gain_row = lax.broadcasted_iota(jnp.int32, (LAT_LINE, LAT_WIDE), 0) == z
+    xb[rows : rows + LAT_LINE, :] = jnp.where(gain_row, gain2_ref[...], 0.0).astype(BF)
+
+    @pl.when(is_end)
+    def _():
+        to_mid(count - 1).start()
+
+    def handover(e):
+        here = pl.ds(pl.multiple_of(core * rows + e * LAT_LINE, LAT_LINE), LAT_LINE)
+        return remote(lat_ref.at[here], lat_ref.at[here], c_send.at[e], c_recv.at[e], {"ctx": 1 - core})
+
+    stat_lane = jnp.logical_and(wide_lane >= LAT, wide_lane < LAT + 8)
+
+    def finish_rows(e):
+        @pl.when(e < rows // LAT_LINE)
+        def _():
+            here = pl.ds(pl.multiple_of(e * LAT_LINE, LAT_LINE), LAT_LINE)
+            there = pl.ds(pl.multiple_of(core * rows + e * LAT_LINE, LAT_LINE), LAT_LINE)
+            v = total[here, :].astype(F32)
+            square = jnp.sum(jnp.where(stat_lane, v, 0.0), axis=1, keepdims=True)
+            v = v * lax.rsqrt(square / D + EPS_NORM)
+            ql, kl, raw = v[:, :QR], v[:, QR : QR + KVR], v[:, QR + KVR :]
+            ql = ql * lax.rsqrt(jnp.mean(ql * ql, axis=1, keepdims=True) + EPS_NORM)
+            kl = kl * lax.rsqrt(jnp.mean(kl * kl, axis=1, keepdims=True) + EPS_NORM)
+            lat_ref[there, 0:QR] = (ql * gains[0:1, 0:QR]).astype(BF)
+            lat_ref[there, QR : QR + KVR] = (kl * gains[0:1, QR : QR + KVR]).astype(BF)
+            moved = pltpu.roll(jnp.where(lane < ROPE, raw, 0.0), NOPE, 1)
+            turned = jnp.where(lane < NOPE + 16, -pltpu.roll(moved, 128 - 16, 1), pltpu.roll(moved, 16, 1))
+            seg = (own_index(e) >= length).astype(F32)
+            mask = jnp.where(lane == HEAD, 1.0 - seg, jnp.where(lane == HEAD + 1, seg, 0.0)) * MASK_VALUE
+            lat_ref[there, QR + KVR : LAT_WIDE] = (moved * tcos[here, :] + turned * tsin[here, :] + mask).astype(BF)
+            handover(e).start()
+
+    def serve(n):
+        @pl.when(jnp.logical_and(is_mid, n < count))
+        def _():
+            first(n)
+
+        @pl.when(jnp.logical_and(is_mid, jnp.logical_and(n >= 1, n <= count)))
+        def _():
+            second(n - 1)
+            finish_rows(n - 1)
+
+        @pl.when(jnp.logical_and(is_end, n < count))
+        def _():
+            to_mid(n).wait_send()
+            to_end(n).wait_recv()
+            finish_rows(n)
+
+    each(count + 1, serve)
+
+    @pl.when(is_mid)
+    def _():
+        def sent(k):
+            over(k).wait_send()
+            to_end(k).wait_send()
+
+        each(count, sent)
+
+    for d in range(1, peers):
+        w_copy(d, me).wait_send()
+        u_copy(d, me).wait_send()
+        u_copy(d, lax.rem(me + peers - d, peers)).wait_recv()
+
+    def passed(e):
+        handover(e).wait_send()
+        here = pl.ds(pl.multiple_of((1 - core) * rows + e * LAT_LINE, LAT_LINE), LAT_LINE)
+        remote(lat_ref.at[here], lat_ref.at[here], c_send.at[e], c_recv.at[e], {"ctx": 1 - core}).wait_recv()
+
+    each(rows // LAT_LINE, passed)
+
+
+def spread(peers):
+    index = jnp.arange(KVR + ROPE)
+    return jnp.equal((index // 36 * 48 + index % 36)[:, None], jnp.arange(peers * 48)[None]).astype(BF)
+
+
+def latent_forward(x, gain, gain2, piece, up, length):
+    rows, width = x.shape
+    peers = lax.axis_size("fsdp") * lax.axis_size("ctx")
+    slot = rows * lax.axis_size("ctx")
+    wide = rows + LAT_LINE
+    count = wide // LAT_LINE
+    sel = spread(peers)
+    frequency = ROPE_BASE ** (-2.0 * jnp.arange(ROPE // 2, dtype=F32) / ROPE)
+    vmem = pl.BlockSpec(memory_space=pltpu.VMEM)
+    dma = pltpu.SemaphoreType.DMA
+    return pl.pallas_call(
+        latent_kernel,
+        out_shape=[
+            jax.ShapeDtypeStruct((LAT_WIDE, width), BF),
+            jax.ShapeDtypeStruct((wide, LAT_WIDE), BF),
+            jax.ShapeDtypeStruct((slot, LAT_WIDE), BF),
+            jax.ShapeDtypeStruct((ROPE // 2, slot), F32),
+            jax.ShapeDtypeStruct((ROPE // 2, slot), F32),
+            jax.ShapeDtypeStruct((16, slot), BF),
+            jax.ShapeDtypeStruct((peers,) + up.shape[1:], BF),
+            jax.ShapeDtypeStruct((rows, 128), F32),
+            jax.ShapeDtypeStruct((rows, 128), F32),
+            jax.ShapeDtypeStruct((16, QR + KVR), F32),
+        ],
+        in_specs=[vmem] * 8 + [pl.BlockSpec(memory_space=pltpu.SMEM)],
+        out_specs=[vmem] * 10,
+        scratch_shapes=[
+            pltpu.VMEM((peers, PIECE, width), BF),
+            pltpu.VMEM((wide, LAT_WIDE), BF),
+            pltpu.VMEM((wide, LAT_WIDE), BF),
+            pltpu.VMEM((wide, LAT_WIDE), BF),
+            pltpu.VMEM((peers * 48, width), BF),
+        ]
+        + [dma((peers,))] * 4
+        + [dma((rows // LAT_LINE,))] * 2
+        + [dma((count,))] * 6,
+        compiler_params=pltpu.CompilerParams(collective_id=0, has_side_effects=True, vmem_limit_bytes=48 * MIB),
+        cost_estimate=pl.CostEstimate(flops=rows * LAT_WIDE * width * 2, bytes_accessed=150 * MIB, transcendentals=0),
+        name="latent_forward",
+    )(x, gain, gain2, piece, up, sel, frequency[:, None], jnp.tile(frequency, 8)[None], length)
+
+
 LINE = 32
 MLP_ROWS = 256
 TILES = ((0, 384), (384, 384), (768, 384), (1152, 448))
@@ -338,11 +476,11 @@
         pl.semaphore_wait(barrier, 1)
 
 
-def line_copies(source, near, cross, total, sems, partner, across):
+def line_copies(source, near, cross, total, sems, partner, across, line=LINE):
     in_send, in_recv, mid_send, mid_recv, out_send, out_recv = sems
 
     def piece(k):
-        return pl.ds(pl.multiple_of(k * LINE, LINE), LINE)
+        return pl.ds(pl.multiple_of(k * line, line), line)
 
     def copy(src, dst, send, recv, k, to):
         return pltpu.make_async_remote_copy(
@@ -577,9 +715,14 @@
 LOAD = 128
 
 
+def total_square(v):
+    v = v.astype(F32)
+    return jnp.sum(jnp.sum(v * v, axis=0, keepdims=True), axis=1, keepdims=True)
+
+
 def grad_kernel(
     live_ref, gain_ref, dnp_any, hid_any, cot_any, n2t_any, dg_any, du_any, act_any,
-    sa_any, dh_any, gain_out, grad_any,
+    sa_any, dh_any, gain_out, grad_any, square_out,
     near, cross, total, cin, stage, xin, yin2, yin, xin2, lhs, rhs, hbuf, cbuf, sbuf, dbuf, prep,
     total_sem, lhs_sem, rhs_sem, h_sem, c_sem, sa_sem, dh_sem, prep_sem, out_sem,
     core_send, core_recv, x_send, x_recv, y2_send, y2_recv, y_send, y_recv, x2_send, x2_recv, *sems,
@@ -781,7 +924,10 @@
         x2_copy(i).wait_recv()
         xin2[i] = plus(xin2[i], yin2[i, x])
         save_lower(i).start()
-
+        square = total_square(yin[i]) + total_square(xin2[i])
+        square_out[i : i + 1, :] = jnp.broadcast_to(square, (1, 128))
+
+    square_out[...] = jnp.zeros_like(square_out)
     load_lhs.wait()
     load_rhs(0).wait()
     products(0, 0)
@@ -854,9 +1000,10 @@
             jax.ShapeDtypeStruct((rows, width), F32),
             jax.ShapeDtypeStruct((1, width), F32),
             jax.ShapeDtypeStruct((3, shard, units), BF),
+            jax.ShapeDtypeStruct((8, 128), F32),
         ],
         in_specs=[vmem] * 2 + [anywhere] * 7,
-        out_specs=[anywhere, anywhere, vmem, anywhere],
+        out_specs=[anywhere, anywhere, vmem, anywhere, vmem],
         scratch_shapes=[scratch(rows, D)] * 3
         + [
             scratch(3, 4, shard, units),
@@ -884,6 +1031,358 @@
     )(live, gain, d_normed_part, hidden, cotangent, normed_t, d_gate, d_up, activation)
 
 
+PACK = 576
+HALF = PACK // 2
+
+
+def torus(s1, xin, yin2, yin, xin2, sems, x, y, to_x, to_y):
+    x_send, x_recv, y2_send, y2_recv, y_send, y_recv, x2_send, x2_recv = sems
+    half = yin.shape[0]
+    upper, lower = pl.ds(0, half), pl.ds(half, half)
+
+    def remote(src, dst, send, recv, to):
+        return pltpu.make_async_remote_copy(
+            src_ref=src, dst_ref=dst, send_sem=send, recv_sem=recv, device_id=to, device_id_type=MESH
+        )
+
+    def plus(a, b):
+        return (a.astype(F32) + b.astype(F32)).astype(BF)
+
+    x_copy = lambda v: remote(s1.at[v * 2 + 1 - x, upper], xin.at[v], x_send.at[v], x_recv.at[v], to_x)
+    y2_copy = lambda v: remote(s1.at[(1 - y) * 2 + v, lower], yin2.at[v], y2_send.at[v], y2_recv.at[v], to_y)
+    y_copy = remote(xin.at[1 - y], yin, y_send.at[0], y_recv.at[0], to_y)
+    x2_copy = remote(yin2.at[1 - x], xin2, x2_send.at[0], x2_recv.at[0], to_x)
+
+    def begin():
+        x_copy(1 - y).start()
+        y2_copy(1 - x).start()
+        x_copy(y).start()
+        y2_copy(x).start()
+
+    def middle():
+        x_copy(1 - y).wait_recv()
+        xin[1 - y] = plus(xin[1 - y], s1[(1 - y) * 2 + x, upper])
+        y_copy.start()
+        y2_copy(1 - x).wait_recv()
+        yin2[1 - x] = plus(yin2[1 - x], s1[y * 2 + 1 - x, lower])
+        x2_copy.start()
+        x_copy(y).wait_recv()
+        xin[y] = plus(xin[y], s1[y * 2 + x, upper])
+        y2_copy(x).wait_recv()
+        yin2[x] = plus(yin2[x], s1[y * 2 + x, lower])
+
+    def last(out):
+        y_copy.wait_recv()
+        out[upper, :] = plus(yin[...], xin[y])
+        x2_copy.wait_recv()
+        out[lower, :] = plus(xin2[...], yin2[x])
+
+    def drain():
+        for v in range(2):
+            x_copy(v).wait_send()
+            y2_copy(v).wait_send()
+        y_copy.wait_send()
+        x2_copy.wait_send()
+
+    return begin, middle, last, drain
+
+
+def latent_back_kernel(
+    dq_ref, de_ref, dkr_ref, up_ref, sum_ref, w_ref, x_ref, gain_ref, dh_ref, tcos, tsin, gains, gout_ref, gq_ref, gkv_ref,
+    sel_ref, b2_ref, square_ref,
+    gin_ref, pack_out, wd_out, small_out, scalar_out,
+    uq, ukv, away, arrived, xb, near, cross, total, dl, dlt, xg, w_pack, small, small_in, scal_in,
+    s1, cin, xin, yin2, yin, xin2, s1w, cinw, xinw, yin2w, yinw, xin2w,
+    lat_send, lat_recv, out_send, out_recv, q_send, q_recv, kv_send, kv_recv, w_send, w_recv,
+    small_send, small_recv, scal_send, scal_recv, *sems,
+):
+    z, core, place = lax.axis_index("tp"), lax.axis_index("ctx"), lax.axis_index("fsdp")
+    y, x = place // 2, place % 2
+    is_end, is_mid, partner, across = line_places(z)
+    line_sems, pack_sems, w_sems = sems[:6], sems[6:14], sems[14:22]
+    to_mid, over, to_end, first, second = line_copies(xb, near, cross, total, line_sems, partner, across, LAT_LINE)
+    count = xb.shape[0] // LAT_LINE
+    rows = xb.shape[0]
+    peers = up_ref.shape[0]
+    me = place * 2 + core
+    to_core, to_x, to_y = {"ctx": 1 - core}, {"fsdp": y * 2 + 1 - x}, {"fsdp": (1 - y) * 2 + x}
+
+    def remote(src, dst, send, recv, to):
+        return pltpu.make_async_remote_copy(
+            src_ref=src, dst_ref=dst, send_sem=send, recv_sem=recv, device_id=to, device_id_type=MESH
+        )
+
+    def peer(d):
+        to = lax.rem(me + d, peers)
+        return {"fsdp": to // 2, "ctx": lax.rem(to, 2)}
+
+    barrier = pltpu.get_barrier_semaphore()
+    for d in range(1, peers):
+        pl.semaphore_signal(barrier, inc=1, device_id=peer(d), device_id_type=MESH)
+    for d in range(1, 4):
+        pl.semaphore_signal(barrier, inc=1, device_id={"tp": lax.rem(z + d, 4)}, device_id_type=MESH)
+    pl.semaphore_wait(barrier, peers + 2)
+
+    def piece(e):
+        return pl.ds(pl.multiple_of(e * LAT_LINE, LAT_LINE), LAT_LINE)
+
+    def span(f, parity, size):
+        return pl.ds(pl.multiple_of((2 * f + parity) * size, size), size)
+
+    slot_q, slot_kv = pl.ds(320 + 96 * core, 96), pl.ds(512 + 32 * core, 32)
+    other_q, other_kv = pl.ds(320 + 96 * (1 - core), 96), pl.ds(512 + 32 * (1 - core), 32)
+    out_copy = lambda f: remote(gout_ref.at[span(f, 1 - core, 320)], cin.at[f], out_send.at[f], out_recv.at[f], to_core)
+    q_copy = lambda f: remote(gq_ref.at[span(f, 1 - core, 96)], s1.at[f, slot_q], q_send.at[f], q_recv.at[f], to_core)
+    kv_copy = lambda f: remote(gkv_ref.at[span(f, 1 - core, 32)], s1.at[f, slot_kv], kv_send.at[f], kv_recv.at[f], to_core)
+    q_got = lambda f: remote(gq_ref.at[span(f, 1 - core, 96)], s1.at[f, other_q], q_send.at[f], q_recv.at[f], to_core)
+    kv_got = lambda f: remote(gkv_ref.at[span(f, 1 - core, 32)], s1.at[f, other_kv], kv_send.at[f], kv_recv.at[f], to_core)
+
+    for p in range(peers):
+        uq[p * 96 : (p + 1) * 96, :] = up_ref[p, 0:96, :]
+        ukv[p * 32 : (p + 1) * 32, :] = up_ref[p, 96:128, :]
+
+    lane = lax.broadcasted_iota(jnp.int32, (1, 128), 1)
+    hand = lambda e: remote(away.at[piece(e)], arrived.at[piece(e)], lat_send.at[e], lat_recv.at[e], to_core)
+
+    def share(at):
+        here = pl.ds(pl.multiple_of(at, LAT_LINE), LAT_LINE)
+        q = dot_nt(dq_ref[here, :], uq[...])
+        kv = dot_nt(de_ref[here, :], ukv[...])
+        rope = jnp.where(lane < ROPE, pltpu.roll(dkr_ref[here, :], NOPE, 1), 0.0)
+        return q, kv, rope
+
+    def send_away(e):
+        q, kv, rope = share((1 - core) * rows + e * LAT_LINE)
+        away[piece(e), 0:QR] = q.astype(BF)
+        away[piece(e), QR : QR + KVR] = kv.astype(BF)
+        away[piece(e), QR + KVR : LAT_WIDE] = rope.astype(BF)
+        hand(e).start()
+
+    each(count, send_away)
+    for f in range(4):
+        out_copy(f).start()
+        q_copy(f).start()
+        kv_copy(f).start()
+
+    def keep(e):
+        q, kv, rope = share(core * rows + e * LAT_LINE)
+        hand(e).wait_recv()
+        got = arrived[piece(e), :].astype(F32)
+        xb[piece(e), 0:QR] = (q + got[:, 0:QR]).astype(BF)
+        xb[piece(e), QR : QR + KVR] = (kv + got[:, QR : QR + KVR]).astype(BF)
+        xb[piece(e), QR + KVR : LAT_WIDE] = (rope + got[:, QR + KVR :]).astype(BF)
+
+        @pl.when(is_end)
+        def _():
+            to_mid(e).start()
+
+    each(count, keep)
+
+    small[...] = jnp.zeros_like(small)
+    small[2:3, 0 : b2_ref.shape[1]] = b2_ref[...]
+    stat_lane = lax.broadcasted_iota(jnp.int32, (1, LAT_WIDE), 1)
+    stat_lane = jnp.logical_and(stat_lane >= LAT, stat_lane < LAT + 8)
+    gain_q, gain_kv = gains[0:1, 0:QR], gains[0:1, QR : QR + KVR]
+
+    def through(d, v, gain):
+        factor = lax.rsqrt(jnp.mean(v * v, axis=1, keepdims=True) + EPS_NORM)
+        scaled = d * gain
+        gain_grad = jnp.sum(d * v * factor, axis=0, keepdims=True)
+        return factor * scaled - v * (factor * factor * factor * jnp.mean(scaled * v, axis=1, keepdims=True)), gain_grad
+
+    def finish_rows(e):
+        v = sum_ref[piece(e), :].astype(F32)
+        square = jnp.sum(jnp.where(stat_lane, v, 0.0), axis=1, keepdims=True)
+        factor = lax.rsqrt(square / D + EPS_NORM)
+        v = v * factor
+        d = total[piece(e), :].astype(F32)
+        ql, kl, raw = v[:, :QR], v[:, QR : QR + KVR], jnp.where(lane < ROPE, v[:, QR + KVR :], 0.0)
+        dql, grad_q = through(d[:, :QR], ql, gain_q)
+        dkl, grad_kv = through(d[:, QR : QR + KVR], kl, gain_kv)
+        moved = pltpu.roll(d[:, QR + KVR :], NOPE, 1)
+        turned = jnp.where(lane < NOPE + 16, pltpu.roll(moved, 128 - 16, 1), -pltpu.roll(moved, 16, 1))
+        rope = pltpu.roll(moved * tcos[piece(e), :] + turned * tsin[piece(e), :], NOPE, 1)
+        inner = (
+            jnp.sum(dql * ql, axis=1, keepdims=True)
+            + jnp.sum(dkl * kl, axis=1, keepdims=True)
+            + jnp.sum(rope * raw, axis=1, keepdims=True)
+        ) / D
+        small[0:1, 0:QR] += grad_q
+        small[0:1, QR : QR + KVR] += grad_kv
+        dl[piece(e), 0:QR] = (dql * factor).astype(BF)
+        dl[piece(e), QR : QR + KVR] = (dkl * factor).astype(BF)
+        dl[piece(e), QR + KVR : LAT_WIDE] = (rope * factor).astype(BF)
+        d_in = dot_nn(dl[piece(e), :], w_ref[...])
+        xin_rows = x_ref[piece(e), :].astype(F32)
+        gin_ref[piece(e), :] = (
+            dh_ref[piece(e), :] + d_in * gain_ref[...] - xin_rows * (factor * factor * inner)
+        ).astype(BF)
+        small[1:2, 0 : d_in.shape[1]] += jnp.sum(d_in * xin_rows, axis=0, keepdims=True)
+        xg[piece(e), :] = (xin_rows * gain_ref[...]).astype(BF)
+
+        @pl.when(e % 2 == 1)
+        def _():
+            pair = pl.ds(pl.multiple_of((e - 1) * LAT_LINE, 128), 128)
+            dlt[:, pair] = dl[pair, :].astype(F32).T.astype(BF)
+
+    def serve(n):
+        @pl.when(jnp.logical_and(is_mid, n < count))
+        def _():
+            first(n)
+
+        @pl.when(jnp.logical_and(is_mid, jnp.logical_and(n >= 1, n <= count)))
+        def _():
+            second(n - 1)
+            finish_rows(n - 1)
+
+        @pl.when(jnp.logical_and(is_end, jnp.logical_and(n >= 2, n < count + 2)))
+        def _():
+            to_mid(n - 2).wait_send()
+            to_end(n - 2).wait_recv()
+            finish_rows(n - 2)
+
+    begin, middle, last, drain = torus(s1, xin, yin2, yin, xin2, pack_sems, x, y, to_x, to_y)
+    begin_w, middle_w, last_w, drain_w = torus(s1w, xinw, yin2w, yinw, xin2w, w_sems, x, y, to_x, to_y)
+
+    serve(0)
+    for f in range(4):
+        out_copy(f).wait_recv()
+        s1[f, 0:320] = (gout_ref[span(f, core, 320), :].astype(F32) + cin[f].astype(F32)).astype(BF)
+        s1[f, slot_q] = gq_ref[span(f, core, 96), :]
+        s1[f, slot_kv] = gkv_ref[span(f, core, 32), :]
+        q_got(f).wait_recv()
+        kv_got(f).wait_recv()
+    begin()
+    each(6, lambda n: serve(n + 1))
+    middle()
+    each(4, lambda n: serve(n + 7))
+    last(pack_out)
+    each(count + 2 - 11, lambda n: serve(n + 11))
+
+    both = dot_nn(dlt[0:QR, :], xg[...])
+    for p in range(peers):
+        w_pack[p, 0:96, :] = both[p * 96 : (p + 1) * 96].astype(BF)
+    tail = dot_nn(dlt[QR:LAT, :], xg[...]).astype(BF)
+    wide = lax.dot_general(sel_ref[...], tail, (((0,), (0,)), ((), ())), preferred_element_type=F32)
+    for p in range(peers):
+        w_pack[p, 96:144, :] = wide[p * 48 : (p + 1) * 48].astype(BF)
+        w_pack[p, 144:160, :] = jnp.zeros((16, wide.shape[1]), BF)
+    w_copy = lambda f: remote(w_pack.at[2 * f + 1 - core], cinw.at[f], w_send.at[f], w_recv.at[f], to_core)
+    for f in range(4):
+        w_copy(f).start()
+    for f in range(4):
+        w_copy(f).wait_recv()
+        s1w[f] = (w_pack[2 * f + core].astype(F32) + cinw[f].astype(F32)).astype(BF)
+    begin_w()
+    middle_w()
+    last_w(wd_out)
+
+    squares = (
+        total_square(wd_out[0:96, :]),
+        total_square(wd_out[96:144, :]),
+        total_square(pack_out[320:512, :]),
+        total_square(pack_out[512:576, :]),
+        total_square(pack_out[0:320, :]),
+        square_ref[0:1, 0:1] + square_ref[1:2, 0:1],
+        square_ref[2:3, 0:1],
+    )
+    line = jnp.zeros((1, 128), F32)
+    for n, v in enumerate(squares):
+        line = jnp.where(lane == n, v, line)
+    small[3:4, 0:128] = line
+    small_copy = lambda d, source: remote(small, small_in.at[source], small_send.at[d], small_recv.at[source], peer(d))
+    for d in range(1, peers):
+        small_copy(d, me).start()
+    small_in[me] = small[...]
+    for d in range(1, peers):
+        small_copy(d, lax.rem(me + peers - d, peers)).wait_recv()
+    whole = small_in[0]
+    for p in range(1, peers):
+        whole = whole + small_in[p]
+    small_out[...] = whole
+    norms = total_square(whole[1:2]) + total_square(whole[2:3])
+    scal_in[z] = jnp.broadcast_to(jnp.where(lane == 7, norms, whole[3:4, 0:128]), (8, 128))
+    scal_copy = lambda d, source: remote(
+        scal_in.at[z], scal_in.at[source], scal_send.at[d], scal_recv.at[source], {"tp": lax.rem(z + d, 4)}
+    )
+    for d in range(1, 4):
+        scal_copy(d, z).start()
+    for d in range(1, 4):
+        scal_copy(d, lax.rem(z + 4 - d, 4)).wait_recv()
+    scalars = (scal_in[0] + scal_in[1]) + (scal_in[2] + scal_in[3])
+    scalar_out[...] = jnp.where(lane == 8, total_square(whole[0:1]), scalars)
+
+    for d in range(1, peers):
+        small_copy(d, me).wait_send()
+    for d in range(1, 4):
+        scal_copy(d, z).wait_send()
+    drain()
+    drain_w()
+    for f in range(4):
+        out_copy(f).wait_send()
+        q_copy(f).wait_send()
+        kv_copy(f).wait_send()
+        w_copy(f).wait_send()
+    each(count, lambda e: hand(e).wait_send())
+
+    @pl.when(is_mid)
+    def _():
+        def sent(k):
+            over(k).wait_send()
+            to_end(k).wait_send()
+
+        each(count, sent)
+
+
+def latent_backward(*args):
+    dq, up, x = args[0], args[3], args[6]
+    rows, width = x.shape
+    lanes = dq.shape[1]
+    peers = up.shape[0]
+    count = rows // LAT_LINE
+    vmem = pl.BlockSpec(memory_space=pltpu.VMEM)
+    dma = pltpu.SemaphoreType.DMA
+    scratch = lambda *shape: pltpu.VMEM(shape, BF)
+    halves = lambda half: [scratch(2, half, width), scratch(2, half, width), scratch(half, width), scratch(half, width)]
+    torus_sems = [dma((2,))] * 4 + [dma((1,))] * 4
+    return pl.pallas_call(
+        latent_back_kernel,
+        out_shape=[
+            jax.ShapeDtypeStruct((rows, width), BF),
+            jax.ShapeDtypeStruct((PACK, width), BF),
+            jax.ShapeDtypeStruct((PIECE, width), BF),
+            jax.ShapeDtypeStruct((8, QR + KVR), F32),
+            jax.ShapeDtypeStruct((8, 128), F32),
+        ],
+        in_specs=[vmem] * len(args),
+        out_specs=[vmem] * 5,
+        scratch_shapes=[scratch(QR, lanes), scratch(KVR, lanes)]
+        + [scratch(rows, LAT_WIDE)] * 7
+        + [
+            scratch(LAT_WIDE, rows),
+            scratch(rows, width),
+            scratch(peers, PIECE, width),
+            pltpu.VMEM((8, QR + KVR), F32),
+            pltpu.VMEM((peers, 8, QR + KVR), F32),
+            pltpu.VMEM((4, 8, 128), F32),
+            scratch(4, PACK, width),
+            scratch(4, 320, width),
+        ]
+        + halves(HALF)
+        + [scratch(4, PIECE, width), scratch(4, PIECE, width)]
+        + halves(PIECE // 2)
+        + [dma((count,))] * 2
+        + [dma((4,))] * 8
+        + [dma((peers,))] * 2
+        + [dma((4,))] * 2
+        + [dma((count,))] * 6
+        + torus_sems * 2,
+        compiler_params=pltpu.CompilerParams(collective_id=5, has_side_effects=True, vmem_limit_bytes=62 * MIB),
+        cost_estimate=pl.CostEstimate(flops=rows * LAT_WIDE * width * 6, bytes_accessed=200 * MIB, transcendentals=0),
+        name="latent_backward",
+    )(*args)
+
+
 def swap_cores(v):
     return lax.ppermute(v, "ctx", [(0, 1), (1, 0)])
 
@@ -971,82 +1470,82 @@
     by_head = heads_all % n_ctx == 0
     heads = heads_all // n_ctx if by_head else heads_all
 
-    down_t = jnp.concatenate(
-        [gather_shards(w_qdown.T.astype(BF)), gather_shards(w_kvdown.T.astype(BF))], axis=0
-    )
-    q_up = gather_shards(w_qup.astype(BF))
-    kv_up = gather_shards(w_kvup.astype(BF))
-    gain_lat = lax.all_gather(g_latent.astype(BF), ("fsdp", "ctx"), axis=0, tiled=True).astype(F32)
+    fused = n_tp == 4 and n_fsdp == 4 and n_ctx == 2
+    gains_norm = g_norms.astype(BF)
+    gain_attn = gains_norm[0].astype(F32)
+    inputs = tokens.astype(F32)
+    seq_length = lengths[0, 0]
+    own_index = core * rows + jnp.arange(rows, dtype=jnp.int32)
+    own_segment = (own_index >= seq_length).astype(jnp.int32)
+    live = (own_segment == 0).astype(F32)[:, None]
+
     out_t = gather_shards(w_out.T.astype(BF))
     gate_up = lax.all_gather(w_gateup.astype(BF), ("fsdp", "ctx"), axis=1, tiled=True)
     ff_down_t = gather_shards(w_down.T.astype(BF))
-    if by_head:
-        q_up_here = lax.dynamic_slice_in_dim(q_up, core * heads * HEAD, heads * HEAD, 1)
-        kv_up_here = lax.dynamic_slice_in_dim(kv_up, core * heads * 128, heads * 128, 1)
+    q_shard = jnp.pad(
+        w_qup.astype(BF).reshape(w_qup.shape[0], heads_all, HEAD), ((0, 0), (0, 0), (0, 128 - HEAD))
+    ).reshape(w_qup.shape[0], heads_all * 128)
+    up_shard = jnp.concatenate([q_shard, w_kvup.astype(BF)], axis=0)
+
+    if fused:
+        piece = jnp.concatenate(
+            [
+                w_qdown.T.astype(BF),
+                jnp.pad(w_kvdown.T.astype(BF), ((0, 12), (0, 0))),
+                jnp.broadcast_to(jnp.pad(g_latent.astype(BF), (0, width - g_latent.shape[0])), (16, width)),
+            ],
+            axis=0,
+        )
+        up_pair = jnp.stack([up_shard[:, : heads * 128], up_shard[:, heads * 128 :]])
+        gain_wide = jnp.pad(gains_norm[1].astype(F32), (0, LAT_WIDE - width))[None]
+        down_t, lat_sum, lat_all, cos_t, sin_t, seg_q, up, tcos, tsin, gains_lat = latent_forward(
+            tokens, gain_attn[None], gain_wide, piece, up_pair, lengths
+        )
+        gain_mlp = lat_sum[rows : rows + n_tp, :width].reshape(D).astype(F32)
     else:
-        q_up_here, kv_up_here = q_up, kv_up
-    wq = q_up_here.T.reshape(heads, HEAD, QR)
-    kv3 = kv_up_here.reshape(KVR, heads, 128)
-    wk = jnp.pad(jnp.transpose(kv3[:, :, :NOPE], (1, 0, 2)), ((0, 0), (0, 0), (0, 128 - NOPE)))
-    wv = jnp.pad(jnp.transpose(kv3[:, :, NOPE:], (1, 2, 0)), ((0, 0), (0, 80 - VD), (0, 0)))
-
-    gains_norm = g_norms.astype(BF)
-    gain_attn = gains_norm[0].astype(F32)
-    gain_query, gain_kv = gain_lat[:QR], gain_lat[QR:]
-
-    seq_length = lengths[0, 0]
-    index = jnp.arange(slot, dtype=jnp.int32)
-    segment = (index >= seq_length).astype(jnp.int32)
-    position = (index - segment * seq_length).astype(F32)
-    frequency = ROPE_BASE ** (-2.0 * jnp.arange(ROPE // 2, dtype=F32) / ROPE)
-    angles = frequency[:, None] * position[None, :]
-    cos_t, sin_t = jnp.cos(angles), jnp.sin(angles)
-    own_cos = lax.dynamic_slice_in_dim(cos_t, core * rows, rows, 1).T
-    own_sin = lax.dynamic_slice_in_dim(sin_t, core * rows, rows, 1).T
-    own_segment = lax.dynamic_slice_in_dim(segment, core * rows, rows, 0)
-    live = (own_segment == 0).astype(F32)[:, None]
-    seg_f = segment.astype(F32)
-    seg_q = jnp.concatenate([seg_f[None], 1.0 - seg_f[None], jnp.zeros((14, slot), F32)], axis=0).astype(BF)
-    seg_k = (MASK_VALUE * jnp.concatenate([1.0 - seg_f[:, None], seg_f[:, None]], axis=1)).astype(BF)
-
-    inputs = tokens.astype(F32)
-    scaled_in = (inputs * gain_attn).astype(BF)
-    lat_part = dot_nt(scaled_in, down_t)
-    squares_high, squares_low = split_two(jnp.sum(inputs * inputs, axis=1))
-    column = jnp.arange(2 * n_tp)
-    stats = jnp.where(
-        column[None] == 2 * tp, squares_high[:, None], jnp.where(column[None] == 2 * tp + 1, squares_low[:, None], 0)
-    ).astype(BF)
-    lat_wide = 1152
-    payload = jnp.concatenate(
-        [lat_part.astype(BF), stats, jnp.zeros((rows, lat_wide - LAT - 2 * n_tp), BF)], axis=1
-    )
-    gain_rows = jnp.where((jnp.arange(64) == tp)[:, None], gains_norm[1][None], 0).astype(BF)
-    gain_rows = jnp.pad(gain_rows, ((0, 0), (0, lat_wide - width)))
-    reduced = line_reduce(jnp.concatenate([payload, gain_rows], axis=0), 17, 0)
-    gain_mlp = reduced[rows : rows + n_tp, :width].reshape(n_tp * width).astype(F32)
-    lat_sum = reduced[:rows].astype(F32)
-    factor_one = lax.rsqrt(jnp.sum(lat_sum[:, LAT : LAT + 2 * n_tp], axis=1) / D + EPS_NORM)[:, None]
-    latents = lat_sum[:, :LAT] * factor_one
-    query_latent = latents[:, :QR]
-    kv_latent = latents[:, QR : QR + KVR]
-    rope_raw = latents[:, QR + KVR :]
-    factor_query = lax.rsqrt(jnp.mean(query_latent * query_latent, axis=1, keepdims=True) + EPS_NORM)
-    factor_kv = lax.rsqrt(jnp.mean(kv_latent * kv_latent, axis=1, keepdims=True) + EPS_NORM)
-    query_normed = (query_latent * factor_query * gain_query).astype(BF)
-    kv_normed = (kv_latent * factor_kv * gain_kv).astype(BF)
-    r_one, r_two = rope_raw[:, : ROPE // 2], rope_raw[:, ROPE // 2 :]
-    rope_key = jnp.concatenate(
-        [r_one * own_cos - r_two * own_sin, r_two * own_cos + r_one * own_sin], axis=1
-    ).astype(BF)
-    normed_lat = jnp.concatenate([query_normed, kv_normed, rope_key], axis=1)
-    lat_both = in_core_order(normed_lat, swap_cores(normed_lat), core, 0)
-    qn, kn, kr = lat_both[:, :QR], lat_both[:, QR : QR + KVR], lat_both[:, QR + KVR :]
-    krx = jnp.concatenate(
-        [jnp.zeros((slot, NOPE), BF), kr, seg_k, jnp.zeros((slot, 128 - HEAD - 2), BF)], axis=1
-    )
-
-    att_heads, lse, q_t, k_rows, v_t = attend_forward(qn, kn, krx, cos_t, sin_t, seg_q, wq, wk, wv)
+        index = jnp.arange(slot, dtype=jnp.int32)
+        segment = (index >= seq_length).astype(jnp.int32)
+        position = (index - segment * seq_length).astype(F32)
+        frequency = ROPE_BASE ** (-2.0 * jnp.arange(ROPE // 2, dtype=F32) / ROPE)
+        angles = frequency[:, None] * position[None, :]
+        cos_t, sin_t = jnp.cos(angles), jnp.sin(angles)
+        own_cos = lax.dynamic_slice_in_dim(cos_t, core * rows, rows, 1).T
+        own_sin = lax.dynamic_slice_in_dim(sin_t, core * rows, rows, 1).T
+        seg_f = segment.astype(F32)
+        seg_q = jnp.concatenate([seg_f[None], 1.0 - seg_f[None], jnp.zeros((14, slot), F32)], axis=0).astype(BF)
+        seg_k = (MASK_VALUE * jnp.concatenate([1.0 - seg_f[:, None], seg_f[:, None]], axis=1)).astype(BF)
+        down_t = jnp.concatenate(
+            [gather_shards(w_qdown.T.astype(BF)), gather_shards(w_kvdown.T.astype(BF)), jnp.zeros((LAT_WIDE - LAT, width), BF)]
+        )
+        gain_lat = lax.all_gather(g_latent.astype(BF), ("fsdp", "ctx"), axis=0, tiled=True).astype(F32)
+        gain_mlp = lax.all_gather(gains_norm[1], "tp", axis=0, tiled=True).astype(F32)
+        up = gather_shards(up_shard).reshape(n_fsdp * n_ctx, up_shard.shape[0], heads_all * 128)
+        if by_head:
+            up = lax.dynamic_slice_in_dim(up, core * heads * 128, heads * 128, 2)
+        scaled_in = (inputs * gain_attn).astype(BF)
+        lat_sum = lax.psum(dot_nt(scaled_in, down_t).astype(BF), "tp").astype(F32)
+        square_sum = lax.psum(jnp.sum(inputs * inputs, axis=1), "tp")
+    if not fused:
+        factor_one = lax.rsqrt(square_sum / D + EPS_NORM)[:, None]
+        latents = lat_sum[:, :LAT] * factor_one
+        query_latent = latents[:, :QR]
+        kv_latent = latents[:, QR : QR + KVR]
+        gain_query, gain_kv = gain_lat[:QR], gain_lat[QR:]
+        factor_query = lax.rsqrt(jnp.mean(query_latent * query_latent, axis=1, keepdims=True) + EPS_NORM)
+        factor_kv = lax.rsqrt(jnp.mean(kv_latent * kv_latent, axis=1, keepdims=True) + EPS_NORM)
+        rope_raw = latents[:, QR + KVR :]
+        query_normed = (query_latent * factor_query * gain_query).astype(BF)
+        kv_normed = (kv_latent * factor_kv * gain_kv).astype(BF)
+        r_one, r_two = rope_raw[:, : ROPE // 2], rope_raw[:, ROPE // 2 :]
+        rope_key = jnp.concatenate(
+            [r_one * own_cos - r_two * own_sin, r_two * own_cos + r_one * own_sin], axis=1
+        ).astype(BF)
+        normed_lat = jnp.concatenate([query_normed, kv_normed, jnp.zeros((rows, NOPE), BF), rope_key], axis=1)
+        lat_both = in_core_order(normed_lat, swap_cores(normed_lat), core, 0)
+        lat_all = jnp.concatenate([lat_both, seg_k, jnp.zeros((slot, 128 - HEAD - 2), BF)], axis=1)
+    qn, kn = lat_all[:, :QR], lat_all[:, QR : QR + KVR]
+
+    att_heads, lse, q_t, k_rows, v_t = attend_forward(lat_all, cos_t, sin_t, seg_q, up)
     att_flat = att_heads.reshape(heads * VD, slot)
     own_cols = lambda v: lax.dynamic_slice_in_dim(v, core * rows, rows, 1)
     if by_head:
@@ -1057,15 +1556,13 @@
 
     feature_owner = jnp.arange(D) // width
     own_features = lambda v: lax.dynamic_slice_in_dim(v, tp * width, width, 1)
-    if n_tp == 4 and n_fsdp == 4:
+    if fused:
         hidden, d_normed_part, mlp_part, normed_two_t, activation, d_gate, d_up = block_forward(
             att_t.T, tokens, out_t, gain_mlp[None], live, cotangent, gate_up, ff_down_t
         )
-        attn_seed, d_hidden, grad_gain_mlp, grads = grad_reduce(
+        attn_seed, d_hidden, grad_gain_mlp, grads, grad_squares = grad_reduce(
             live, gain_mlp[None], d_normed_part, hidden, cotangent, normed_two_t, d_gate, d_up, activation
         )
-        grad_gain_mlp = grad_gain_mlp[0]
-        grad_gate, grad_up, grad_down = grads[0], grads[1], grads[2]
     else:
         dy = cotangent.astype(F32) * live
         mlp_seed = (RESIDUAL_SCALE * dy).astype(BF)
@@ -1101,77 +1598,92 @@
     mlp_out = lax.psum_scatter(mlp_part, "tp", scatter_dimension=1, tiled=True).astype(F32)
     layer_out = (own_features(hidden).astype(F32) + RESIDUAL_SCALE * mlp_out).astype(BF)
     d_att_t = lax.dot_general(out_t, attn_seed, (((0,), (1,)), ((), ())), preferred_element_type=F32).astype(BF)
-    grad_out = scatter_grads(dot_tn(attn_seed, att_t.T).astype(BF))
+    grad_out = dot_tn(attn_seed, att_t.T).astype(BF)
 
     if by_head:
         pick = lambda v, which: lax.dynamic_slice_in_dim(v, which * heads * VD, heads * VD, 0)
         d_att = in_core_order(pick(d_att_t, core), swap_cores(pick(d_att_t, 1 - core)), core, 1)
     else:
         d_att = lax.dynamic_update_slice(jnp.zeros((heads * VD, slot), BF), d_att_t, (0, core * rows))
-    dq_t, d_e, d_kr = attend_backward(
+    d_q, d_e, d_kr = attend_backward(
         q_t, k_rows, v_t, att_heads, d_att.reshape(heads, VD, slot), lse, cos_t, sin_t
     )
-
-    d_qn = lax.dot_general(dq_t, q_up_here, (((0,), (1,)), ((), ())), preferred_element_type=F32)
-    d_kn = dot_nt(d_e, kv_up_here)
-    d_lat_part = jnp.concatenate([d_qn, d_kn, d_kr[:, NOPE:HEAD]], axis=1)
-    own_rows = lambda v, which: lax.dynamic_slice_in_dim(v, which * rows, rows, 0)
-    from_other = swap_cores(own_rows(d_lat_part, 1 - core).astype(BF)).astype(F32)
-    d_lat_sum = (own_rows(d_lat_part, core) + from_other).astype(BF)
-    d_lat = line_reduce(jnp.pad(d_lat_sum, ((0, 0), (0, lat_wide - LAT))), 16, 2).astype(F32)
-    d_rope = d_lat[:, QR + KVR : LAT]
-    k_one, k_two = d_rope[:, : ROPE // 2], d_rope[:, ROPE // 2 :]
-    d_rope_raw = jnp.concatenate([k_one * own_cos + k_two * own_sin, k_two * own_cos - k_one * own_sin], axis=1)
-    d_query_latent, grad_gain_query = norm_backward(d_lat[:, :QR], query_latent, factor_query, gain_query)
-    d_kv_latent, grad_gain_kv = norm_backward(d_lat[:, QR : QR + KVR], kv_latent, factor_kv, gain_kv)
-    d_latents = jnp.concatenate([d_query_latent, d_kv_latent, d_rope_raw], axis=1)
-    in_inner = jnp.sum(d_latents * latents, axis=1, keepdims=True) / D
-    d_latents = (d_latents * factor_one).astype(BF)
-    grad_both = dot_tn(d_latents, scaled_in).astype(BF)
-    grad_qdown = scatter_grads(grad_both[:QR])
-    grad_kvdown = scatter_grads(grad_both[QR:])
-    d_in = dot_nn(d_latents, down_t)
-    grad_gain_attn = jnp.sum(d_in * inputs, axis=0)
-    grad_input = (d_hidden + d_in * gain_attn - inputs * (factor_one**2 * in_inner)).astype(BF)
-
-    grad_qup = dot_nt(qn.T, dq_t).astype(BF)
+    grad_qup = dot_tn(qn, d_q).astype(BF)
     grad_kvup = dot_tn(kn, d_e).astype(BF)
 
-    def scatter_up(g):
-        if not by_head:
-            return scatter_grads(g)
-        n_rows, n_cols = g.shape
-        g = g.reshape(n_fsdp, n_ctx, n_rows // (n_fsdp * n_ctx), n_cols)
-        mine = lax.dynamic_index_in_dim(g, core, 1, keepdims=False)
-        other = swap_cores(lax.dynamic_index_in_dim(g, 1 - core, 1, keepdims=False))
-        return scatter_fsdp(in_core_order(mine, other, core, 2))
-
-    grad_qup, grad_kvup = scatter_up(grad_qup), scatter_up(grad_kvup)
-
-    owned = [
-        grad_qdown.astype(F32).T,
-        grad_kvdown.astype(F32).T,
-        grad_qup.astype(F32),
-        grad_kvup.astype(F32),
-        grad_out.astype(F32).T,
-        jnp.stack([grad_gate, grad_up]).astype(F32),
-        grad_down.astype(F32).T,
-    ]
-    both_gains = jnp.stack([grad_gain_attn, grad_gain_mlp])
-    placed_gains = jnp.where((feature_owner == tp)[None], jnp.concatenate([both_gains] * n_tp, axis=1), 0.0)
-    latent_gains = jnp.concatenate([grad_gain_query, grad_gain_kv]) * (tp == 0)
-    squares = jnp.stack([jnp.sum(g * g) for g in owned])
-    small = lax.psum(
-        jnp.concatenate([placed_gains.reshape(-1), latent_gains, squares]), ("fsdp", "ctx", "tp")
-    )
-    all_gains = small[: 2 * D].reshape(2, D)
-    all_latent = small[2 * D : 2 * D + QR + KVR]
+    def heads_only(g):
+        return g.reshape(g.shape[0], heads_all, 128)[:, :, :HEAD].reshape(g.shape[0], heads_all * HEAD)
+
     share = g_latent.shape[0]
-    place = lax.axis_index("fsdp") * n_ctx + core
-    owned.append(own_features(all_gains))
-    owned.append(lax.dynamic_slice_in_dim(all_latent, place * share, share, 0))
-    totals = [small[2 * D + QR + KVR + n] for n in range(7)]
-    totals += [jnp.sum(all_gains * all_gains), jnp.sum(all_latent * all_latent)]
+    my_share = (lax.axis_index("fsdp") * n_ctx + core) * share
+    if fused:
+        grad_input, pack, wd_grad, small, scalars = latent_backward(
+            d_q, d_e, d_kr, up, lat_sum, down_t, tokens, gain_attn[None], d_hidden, tcos, tsin, gains_lat,
+            grad_out, grad_qup, grad_kvup, spread(n_fsdp * n_ctx), grad_gain_mlp, grad_squares,
+        )
+        lanes = heads * 128
+        owned = [
+            wd_grad[:96].astype(F32).T,
+            wd_grad[96:132].astype(F32).T,
+            heads_only(jnp.concatenate([pack[320:416], pack[416:512]], axis=1)).astype(F32),
+            jnp.concatenate([pack[512:544], pack[544:576]], axis=1).astype(F32),
+            pack[:320].astype(F32).T,
+            grads[:2].astype(F32),
+            grads[2].astype(F32).T,
+            small[1:3, :width],
+            lax.dynamic_slice_in_dim(small[0], my_share, share, 0),
+        ]
+        totals = [scalars[0, n] for n in range(9)]
+    else:
+        q_up_here = up[:, : w_qup.shape[0]].reshape(QR, heads * 128)
+        kv_up_here = up[:, w_qup.shape[0] :].reshape(KVR, heads * 128)
+        d_lat_part = jnp.concatenate([dot_nt(d_q, q_up_here), dot_nt(d_e, kv_up_here), d_kr[:, NOPE:HEAD]], axis=1)
+        own_rows = lambda v, which: lax.dynamic_slice_in_dim(v, which * rows, rows, 0)
+        from_other = swap_cores(own_rows(d_lat_part, 1 - core).astype(BF)).astype(F32)
+        d_lat = lax.psum((own_rows(d_lat_part, core) + from_other).astype(BF), "tp").astype(F32)
+        d_rope = d_lat[:, QR + KVR : LAT]
+        k_one, k_two = d_rope[:, : ROPE // 2], d_rope[:, ROPE // 2 :]
+        d_rope_raw = jnp.concatenate([k_one * own_cos + k_two * own_sin, k_two * own_cos - k_one * own_sin], axis=1)
+        d_query_latent, grad_gain_query = norm_backward(d_lat[:, :QR], query_latent, factor_query, gain_query)
+        d_kv_latent, grad_gain_kv = norm_backward(d_lat[:, QR : QR + KVR], kv_latent, factor_kv, gain_kv)
+        d_latents = jnp.concatenate([d_query_latent, d_kv_latent, d_rope_raw], axis=1)
+        in_inner = jnp.sum(d_latents * latents, axis=1, keepdims=True) / D
+        d_latents = (d_latents * factor_one).astype(BF)
+        grad_both = dot_tn(d_latents, scaled_in).astype(BF)
+        d_in = dot_nn(d_latents, down_t[:LAT])
+        grad_gain_attn = jnp.sum(d_in * inputs, axis=0)
+        grad_input = (d_hidden + d_in * gain_attn - inputs * (factor_one**2 * in_inner)).astype(BF)
+
+        def scatter_up(g):
+            if not by_head:
+                return scatter_grads(g)
+            n_rows, n_cols = g.shape
+            g = g.reshape(n_fsdp, n_ctx, n_rows // (n_fsdp * n_ctx), n_cols)
+            other = swap_cores(take(g, 1 - core, 1))
+            return scatter_fsdp(in_core_order(take(g, core, 1), other, core, 2))
+
+        owned = [
+            scatter_grads(grad_both[:QR]).astype(F32).T,
+            scatter_grads(grad_both[QR:]).astype(F32).T,
+            heads_only(scatter_up(grad_qup)).astype(F32),
+            scatter_up(grad_kvup).astype(F32),
+            scatter_grads(grad_out).astype(F32).T,
+            jnp.stack([grad_gate, grad_up]).astype(F32),
+            grad_down.astype(F32).T,
+        ]
+        both_gains = jnp.stack([grad_gain_attn, grad_gain_mlp])
+        placed_gains = jnp.where((feature_owner == tp)[None], jnp.concatenate([both_gains] * n_tp, axis=1), 0.0)
+        latent_gains = jnp.concatenate([grad_gain_query, grad_gain_kv]) * (tp == 0)
+        squares = jnp.stack([jnp.sum(g * g) for g in owned])
+        small = lax.psum(
+            jnp.concatenate([placed_gains.reshape(-1), latent_gains, squares]), ("fsdp", "ctx", "tp")
+        )
+        all_gains = small[: 2 * D].reshape(2, D)
+        all_latent = small[2 * D : 2 * D + QR + KVR]
+        owned.append(own_features(all_gains))
+        owned.append(lax.dynamic_slice_in_dim(all_latent, my_share, share, 0))
+        totals = [small[2 * D + QR + KVR + n] for n in range(7)]
+        totals += [jnp.sum(all_gains * all_gains), jnp.sum(all_latent * all_latent)]
     entry_counts = (
         D * QR,
         D * (KVR + ROPE),

time: 953 us -> 823 us (0.86)
  Pallas kernels: 555 us -> 639 us
  blocking collectives: 82.5 us -> 0 us
  local copies, waits for them, and re-layouts: 99.7 us -> 39.9 us
  other arithmetic: 98.9 us -> 44.8 us
  starting transfers between devices: 23.4 us -> 0.86 us
  waiting for transfers between devices: 35.5 us -> 50.7 us
    pallas_call x2, Pallas kernels: 132 us -> 207 us  [the longest x1 111 us: latent_backward(): pl.pallas_call(latent_back_kernel, out_shape=[jax.ShapeDtypeStruct((rows,...]
    all_gather x1, waiting for transfers between devices: 0.01 us -> 50.7 us  [local(): lax.all_gather(w_gateup.astype(BF), ('fsdp', 'ctx'), axis=1, tiled=True)]
    all_gather x4 -> x0, blocking collectives: 44.6 us -> none  [the longest x3 34.4 us: gather_shards(): return lax.all_gather(v, ('fsdp', 'ctx'), axis=0, tiled=True)]
    psum x1 -> x0, blocking collectives: 37.9 us -> none  [local(): lax.psum(jnp.concatenate([placed_gains.reshape(-1), latent_gains, squares...]
    ppermute x23 -> x0, waiting for transfers between devices: 35.4 us -> none  [keep_half(): other = lax.ppermute(take(v, 1 - which, axis), name, pairs)]
    concatenate x9 -> x1, local copies, waits for them, and re-layouts: 23.7 us -> 0.22 us  [local(): jnp.concatenate([pack[320:416], pack[416:512]], axis=1)]
    ppermute x23 -> x0, starting transfers between devices: 22 us -> none  [keep_half(): other = lax.ppermute(take(v, 1 - which, axis), name, pairs)]
    reduce_sum x14 -> x0, other arithmetic: 20.5 us -> none  [the longest x7 12.3 us: local(): squares = jnp.stack([jnp.sum(g * g) for g in owned])]
  transfers between devices with their start and end apart: 34 -> 6, of which waited for: 17 -> 1; matrix products, arithmetic and copies ran while one was open for 19% -> 9% of each run, Pallas kernels for 23% -> 36%
where the time goes in v3:
time: 823 us; the launch traced here: 817 us
  Pallas kernels  639 us (78%)
  waiting for transfers between devices  50.7 us (6%)
  other arithmetic  44.8 us (5%)
  local copies, waits for them, and re-layouts  39.9 us (5%)
  between operations  22 us (3%)
  matrix products  19.7 us (2%)
    pallas_call x1, Pallas kernels, block_forward(): pl.pallas_call(block_kernel, out_shape=[wide, wide, wide, jax.ShapeDtypeS...  184 us
    pallas_call x1, Pallas kernels, grad_reduce(): pl.pallas_call(grad_kernel, out_shape=[jax.ShapeDtypeStruct((rows, D), BF...  162 us
    pallas_call x1, Pallas kernels, latent_backward(): pl.pallas_call(latent_back_kernel, out_shape=[jax.ShapeDtypeStruct((rows,...  111 us
    pallas_call x1, Pallas kernels, latent_forward(): pl.pallas_call(latent_kernel, out_shape=[jax.ShapeDtypeStruct((LAT_WIDE,...  96.1 us
    all_gather x1, waiting for transfers between devices, local(): lax.all_gather(w_gateup.astype(BF), ('fsdp', 'ctx'), axis=1, tiled=True)  50.7 us
    pallas_call x1, Pallas kernels, attend_backward(): pl.pallas_call(attend_backward_kernel, grid=(heads, rows // BQ), in_specs...  48.7 us
    pallas_call x1, Pallas kernels, attend_forward(): pl.pallas_call(attend_forward_kernel, grid=(heads, rows // BQ), in_specs=...  38 us
    unnamed x116, local copies, waits for them, and re-layouts  32.7 us
  transfers between devices with their start and end apart: 6, of which 1 were waited for; matrix products, arithmetic and copies ran while one was open for 9% of the time, Pallas kernels for 36%

profile of v3, /device:TPU:0, one launch (start us, length us, event | category | flops | bytes accessed | tf_op | source)
XLA Modules:
  0.0 817.5 jit_solution(14976168332796417505)
XLA Ops:
  7.3 1.9 convert_bitcast_fusion.3
  9.3 2.7 convert_bitcast_fusion.1
  12.1 3.8 convert_element_type.152
  18.0 96.1 %latent_forward.1 = (bf16[1152,640]{1,0:T(8,128)(2,1)}, bf16[1088,1152]{1,0:T(8,128)(2,1)}, bf16[2048,1152]{1,0:T(8,128)(2,1)}, f32[16,2048]{1,0:T(8,128)S(1)}, ...) custom-call(bf16[1024,640]{1,0:T(8,128)(2,1)S(1)} %copy-done.2, ...), custom_call_target="tpu_custom_call" | custom-call | flops 1509949440 | bytes 157286400 | tf_op jit(solution)/shard_map/latent_forward/pallas_call | solution.py:422
  114.2 3.2 copy-done.12
  117.4 38.0 %attend_forward.1 = (bf16[5,64,2048]{2,1,0:T(8,128)(2,1)S(1)}, f32[5,1,2048]{2,1,0:T(1,128)S(1)}, bf16[5,128,2048]{2,1,0:T(8,128)(2,1)S(1)}, bf16[5,2048,128]{2,1,0:T(8,128)(2,1)S(1)}, bf16[5,80,2048]{2,1,0:T(8,128)(2,1)S(1)}) custom-call(bf16[2048,1152]{1,0:T(8,128)(2,1)S(1)} %copy-done.12, f32[16,2048]{1,0:T(8,128)S(1)} %get-tuple-element.74.cos_ref, ...), custom_call_target="tpu_custom_call" | custom-call | flops 6710886400 | bytes 31457280 | tf_op jit(solution)/shard_map/attend_forward/pallas_call | solution.py:120
  155.4 1.5 copy-done.15
  158.2 1.4 copy-done.13
  163.9 2.0 copy.102
  166.8 1.4 copy.97
  168.3 2.0 fusion.22.att_ref
  170.3 50.7 %all-gather.6.cloned.1.call-done.gu_any = bf16[2,2560,1600]{2,1,0:T(8,128)(2,1)} async-done(((bf16[2,320,1600]{2,1,0:T(8,128)(2,1)}), bf16[2,2560,1600]{2,1,0:T(8,128)(2,1)}) %all-gather.6.cloned.1.call-update) | async-done | bytes 16384016 | tf_op jit(solution)/shard_map/all_gather | solution.py:1483
  221.0 183.6 %block_forward.1 = (bf16[1024,2560]{1,0:T(8,128)(2,1)}, bf16[1024,2560]{1,0:T(8,128)(2,1)}, bf16[1024,2560]{1,0:T(8,128)(2,1)}, bf16[2560,1024]{1,0:T(8,128)(2,1...) custom-call(bf16[1024,640]{1,0:T(8,128)(2,1)} %fusion.22.att_ref, ...), custom_call_target="tpu_custom_call" | custom-call | flops 50331648000 | bytes 419430400 | tf_op jit(solution)/shard_map/block_forward/pallas_call | solution.py:691
  404.6 161.6 %grad_reduce.1 = (bf16[1024,2560]{1,0:T(8,128)(2,1)}, f32[1024,640]{1,0:T(8,128)}, f32[1,640]{1,0:T(1,128)}, bf16[3,320,1600]{2,1,0:T(8,128)(2,1)}, f32[8,128]{1,0:T(8,128)}) custom-call(f32[1024,1]{1,0:T(8,128)} %fusion.9.live_ref, f32[1,2560]{1,0:T(1,128)} %bitcast.89, bf16[1024,2560]{1,0:T(8,128)(2,1)} %get-tuple-element.82.dnp_any, ...), custom_call_target="tpu_custom_call" | custom-call | flops 25165824000 | bytes 419430400 | tf_op jit(solution)/shard_map/grad_reduce/pallas_call | solution.py:996
  566.3 8.0 copy.109
  574.3 7.2 convolution_convert_fusion.1
  583.0 6.6 convolution_convert_fusion.gout_ref
  591.0 48.7 %attend_backward.1 = (bf16[2048,640]{1,0:T(8,128)(2,1)S(1)}, bf16[2048,640]{1,0:T(8,128)(2,1)S(1)}, f32[2048,128]{1,0:T(8,128)S(1)}) custom-call(bf16[5,128,2048]{2,1,0:T(8,128)(2,1)S(1)} %copy-done.14, bf16[5,2048,128]{2,1,0:T(8,128)(2,1)} %copy-done.15, bf16[5,80,2048]{2,1,0:T(8,128)(2,1)S(1)} %copy-done.17, bf16[5,64,2048]{2,1,0:T(8,128)(2,1)S(1)} %copy-done.5, ...), custom_call_target="tpu_custom_call" | custom-call | flops 18874368000 | bytes 31457280 | tf_op jit(solution)/shard_map/attend_backward/pallas_call | solution.py:206
  640.7 2.3 convolution_convert_fusion.2.gkv_ref
  643.1 3.6 fusion.4.gq_ref
  646.7 111.3 %latent_backward.1 = (bf16[1024,640]{1,0:T(8,128)(2,1)}, bf16[576,640]{1,0:T(8,128)(2,1)}, bf16[160,640]{1,0:T(8,128)(2,1)}, f32[8,1024]{1,0:T(8,128)}, f32[8,128]{1,0:T(8,128)}) custom-call(bf16[2048,640]{1,0:T(8,128)(2,1)} %copy-done, bf16[2048,640]{1,0:T(8,128)(2,1)} %copy-done.1, f32[2048,128]{1,0:T(8,128)} %copy-done.6, bf16[8,128,640]{2,1,0:T(8,128)(2,1)} %copy-done.3, ...), custom_call_target="tpu_custom_call" | custom-call | flops 4529848320 | bytes 209715200 | tf_op jit(solution)/shard_map/latent_backward/pallas_call | solution.py:1348
  758.0 1.8 fusion.46
  765.9 2.0 copy.106
  773.6 2.0 copy.105
  782.2 1.9 multiply_subtract_fusion.6
  784.1 2.1 multiply_subtract_fusion.4
  786.2 3.6 multiply_subtract_fusion.2
  789.8 2.7 multiply_subtract_fusion.5
  792.6 5.7 multiply_subtract_fusion.1
  798.4 6.7 multiply_subtract_fusion
  805.0 1.7 copy.110
  806.8 2.9 add_convert_fusion
  (167 shorter events, 24.7 us)
Async XLA Ops:
  7.2 163.1 %all-gather.4.cloned.1.call-start = ((), (), s32[]{:S(2)}) async-start(), calls=%async_computation.1 | async-start | bytes 3686400 | tf_op jit(solution)/shard_map/all_gather | solution.py:1397
  9.2 161.1 %all-gather.8.cloned.1.call-start = ((), (), s32[]{:S(2)}) async-start(), calls=%async_computation.3 | async-start | bytes 9584640 | tf_op jit(solution)/shard_map/all_gather | solution.py:1397
  12.0 209.0 %all-gather.6.cloned.1.call-start = ((), (), s32[]{:S(2)}) async-start(), calls=%async_computation.2 | async-start | bytes 19169280 | tf_op jit(solution)/shard_map/all_gather | solution.py:1483
  15.9 789.1 %reduce-scatter.4.cloned.1.call-start = ((), (), s32[]{:S(2)}) async-start(), calls=%async_computation.4 | async-start | bytes 6553600
  16.8 97.3 %copy-start.11 = (f32[1,640]{1,0:T(1,128)}, f32[1,640]{1,0:T(1,128)S(1)}, u32[]{:S(2)}) copy-start(f32[1,640]{1,0:T(1,128)S(1)} %get-tuple-element.269.gain_ref) | copy-start | bytes 7684
  18.0 96.1 %copy-start.7 = (bf16[288,384]{1,0:T(8,128)(2,1)}, bf16[288,384]{1,0:T(8,128)(2,1)S(1)}, u32[]{:S(2)}) copy-start(bf16[288,384]{1,0:T(8,128)(2,1)S(1)} %fusion.11.sel_ref) | copy-start | bytes 663556
  114.1 41.3 %copy-start.3 = (bf16[8,128,640]{2,1,0:T(8,128)(2,1)}, bf16[8,128,640]{2,1,0:T(8,128)(2,1)S(1)}, u32[]{:S(2)}) copy-start(bf16[8,128,640]{2,1,0:T(8,128)(2,1)S(1)} %get-tuple-element.77.up_ref) | copy-start | bytes 3932164
  114.1 41.3 %copy-start.8 = (f32[1024,128]{1,0:T(8,128)}, f32[1024,128]{1,0:T(8,128)S(1)}, u32[]{:S(2)}) copy-start(f32[1024,128]{1,0:T(8,128)S(1)} %get-tuple-element.99.tcos) | copy-start | bytes 1572868
  114.1 41.3 %copy-start.9 = (f32[1024,128]{1,0:T(8,128)}, f32[1024,128]{1,0:T(8,128)S(1)}, u32[]{:S(2)}) copy-start(f32[1024,128]{1,0:T(8,128)S(1)} %get-tuple-element.100.tsin) | copy-start | bytes 1572868
  114.1 41.3 %copy-start.10 = (f32[16,1024]{1,0:T(8,128)}, f32[16,1024]{1,0:T(8,128)S(1)}, u32[]{:S(2)}) copy-start(f32[16,1024]{1,0:T(8,128)S(1)} %get-tuple-element.101.gains) | copy-start | bytes 196612
  160.6 6.2 collective-permute-start
  161.6 8.7 %copy-start.21 = (bf16[320,1024]{0,1:T(8,128)(2,1)}, bf16[320,1024]{0,1:T(8,128)(2,1)S(1)}, u32[]{:S(2)}) copy-start(bf16[320,1024]{0,1:T(8,128)(2,1)S(1)} %copy.111) | copy-start | bytes 1966084
  574.3 7.5 slice-start.8
  574.3 7.5 slice-start.9
  581.7 8.0 collective-permute-start.1
  583.0 7.1 copy-start.17
  583.0 57.6 %slice-start = ((s8[4718592]{0:T(1024)(128)(4,1)}), s8[4194304]{0:T(1024)(128)(4,1)S(1)}, s32[]{:S(2)}) async-start(s8[4718592]{0:T(1024)(128)(4,1)} %bitcast.73), calls=%async_computation.5 | async-start | bytes 8388608
  591.0 49.7 %slice-start.1 = ((s8[4718592]{0:T(1024)(128)(4,1)}), s8[524288]{0:T(1024)(128)(4,1)S(1)}, s32[]{:S(2)}) async-start(s8[4718592]{0:T(1024)(128)(4,1)} %bitcast.73), calls=%async_computation.6 | async-start | bytes 1048576
  646.7 118.0 %copy-start.26 = (f32[96,960]{0,1:T(8,128)S(1)}, f32[96,960]{0,1:T(8,128)}, u32[]{:S(2)}) copy-start(f32[96,960]{0,1:T(8,128)} %copy.101) | copy-start | bytes 1105924
  646.7 118.0 %copy-start.27 = (f32[96,960]{0,1:T(8,128)S(1)}, f32[96,960]{0,1:T(8,128)}, u32[]{:S(2)}) copy-start(f32[96,960]{0,1:T(8,128)} %copy.102) | copy-start | bytes 1105924
  765.9 11.1 %copy-start.39 = (f32[128]{0:T(128)S(1)}, f32[128]{0:T(128)}, u32[]{:S(2)}) copy-start(f32[128]{0:T(128)} %param.59) | copy-start | bytes 1540
  765.9 12.3 %copy-start.40 = (f32[128]{0:T(128)S(1)}, f32[128]{0:T(128)}, u32[]{:S(2)}) copy-start(f32[128]{0:T(128)} %param.50) | copy-start | bytes 1540
  765.9 16.3 %copy-start.33 = (f32[640,36]{0,1:T(8,128)S(1)}, f32[640,36]{0,1:T(8,128)}, u32[]{:S(2)}) copy-start(f32[640,36]{0,1:T(8,128)} %param.34) | copy-start | bytes 276484
  765.9 18.1 %copy-start.30 = (f32[640,96]{0,1:T(8,128)S(1)}, f32[640,96]{0,1:T(8,128)}, u32[]{:S(2)}) copy-start(f32[640,96]{0,1:T(8,128)} %param.33) | copy-start | bytes 737284
  768.9 17.3 %copy-start.19 = (f32[640,320]{0,1:T(8,128)S(1)}, f32[640,320]{0,1:T(8,128)}, u32[]{:S(2)}) copy-start(f32[640,320]{0,1:T(8,128)} %param.37) | copy-start | bytes 2457604
  772.7 19.8 %copy-start.25 = (f32[1600,320]{0,1:T(8,128)S(1)}, f32[1600,320]{0,1:T(8,128)}, u32[]{:S(2)}) copy-start(f32[1600,320]{0,1:T(8,128)} %param.48) | copy-start | bytes 6144004
  778.2 11.6 %copy-start.38 = (f32[128]{0:T(128)}, f32[128]{0:T(128)S(1)}, u32[]{:S(2)}) copy-start(f32[128]{0:T(128)S(1)} %get-tuple-element.316) | copy-start | bytes 1540
  780.1 9.7 %copy-start.36 = (f32[2,640]{1,0:T(2,128)}, f32[2,640]{1,0:T(2,128)S(1)}, u32[]{:S(2)}) copy-start(f32[2,640]{1,0:T(2,128)S(1)} %get-tuple-element.315) | copy-start | bytes 15364
  782.2 10.3 %copy-start.20 = (bf16[3,320,1600]{2,1,0:T(8,128)(2,1)S(1)}, bf16[3,320,1600]{2,1,0:T(8,128)(2,1)}, u32[]{:S(2)}) copy-start(bf16[3,320,1600]{2,1,0:T(8,128)(2,1)} %get-tuple-element.107) | copy-start | bytes 9216004
  786.2 12.1 %slice-start.2 = ((s8[4259840]{0:T(1024)(128)(4,1)}), s8[4194304]{0:T(1024)(128)(4,1)S(1)}, s32[]{:S(2)}) async-start(s8[4259840]{0:T(1024)(128)(4,1)} %bitcast.76), calls=%async_computation.7 | async-start | bytes 8388608
  786.2 12.1 %slice-start.4 = ((s8[4259840]{0:T(1024)(128)(4,1)}), s8[4194304]{0:T(1024)(128)(4,1)S(1)}, s32[]{:S(2)}) async-start(s8[4259840]{0:T(1024)(128)(4,1)} %bitcast.78), calls=%async_computation.9 | async-start | bytes 8388608
  786.2 12.1 %slice-start.6 = ((s8[4259840]{0:T(1024)(128)(4,1)}), s8[4194304]{0:T(1024)(128)(4,1)S(1)}, s32[]{:S(2)}) async-start(s8[4259840]{0:T(1024)(128)(4,1)} %bitcast.80), calls=%async_computation.11 | async-start | bytes 8388608
  (26 other events, 71.9 us)
Sparse Core Ops, SparseCore 0:
  10.5 59.5 all-gather.3
  72.5 54.9 all-gather.7
  130.0 90.9 all-gather.5
  574.4 94.1 reduce-scatter.3

commit v4 on v3

--- a/solution.py
+++ b/solution.py
@@ -51,14 +51,111 @@
     return lax.dot_general(a, b, (((0,), (0,)), ((), ())), preferred_element_type=F32)
 
 
+def torus_gather(piece, whole, sems, place, core):
+    x1s, x1r, y1s, y1r, c1s, c1r, x2s, x2r, y2s, y2r, cxs, cxr, cys, cyr, cds, cdr, own = sems
+    y, x = place // 2, place % 2
+    half = piece.shape[1] // 2
+    upper, lower = pl.ds(0, half), pl.ds(half, half)
+    to_core, to_x, to_y = {"ctx": 1 - core}, {"fsdp": y * 2 + 1 - x}, {"fsdp": (1 - y) * 2 + x}
+
+    def owner(yy, xx, cc):
+        return (yy * 2 + xx) * 2 + cc
+
+    me, px, py = owner(y, x, core), owner(y, 1 - x, core), owner(1 - y, x, core)
+    pd = owner(1 - y, 1 - x, core)
+
+    def remote(src, dst, send, recv, i, to):
+        return pltpu.make_async_remote_copy(
+            src_ref=src, dst_ref=dst, send_sem=send.at[i], recv_sem=recv.at[i], device_id=to, device_id_type=MESH
+        )
+
+    first = lambda i, p, send, recv, to: remote(piece.at[i], whole.at[p, i], send, recv, i, to)
+    part = lambda i, p, rows, send, recv, to: remote(whole.at[p, i, rows], whole.at[p, i, rows], send, recv, i, to)
+    full = lambda i, p, send, recv: remote(whole.at[p, i], whole.at[p, i], send, recv, i, to_core)
+    keep = lambda i: pltpu.make_async_copy(piece.at[i], whole.at[me, i], own.at[i])
+
+    def begin(i):
+        first(i, me, x1s, x1r, to_x).start()
+        first(i, me, y1s, y1r, to_y).start()
+        first(i, me, c1s, c1r, to_core).start()
+        keep(i).start()
+
+    def forward(i):
+        first(i, px, x1s, x1r, to_x).wait_recv()
+        part(i, px, upper, y2s, y2r, to_y).start()
+        full(i, px, cxs, cxr).start()
+        first(i, py, y1s, y1r, to_y).wait_recv()
+        part(i, py, lower, x2s, x2r, to_x).start()
+        full(i, py, cys, cyr).start()
+
+    def final(i):
+        part(i, pd, upper, y2s, y2r, to_y).wait_recv()
+        part(i, pd, lower, x2s, x2r, to_x).wait_recv()
+        full(i, pd, cds, cdr).start()
+
+    def drain(i):
+        first(i, owner(y, x, 1 - core), c1s, c1r, to_core).wait_recv()
+        full(i, owner(y, 1 - x, 1 - core), cxs, cxr).wait_recv()
+        full(i, owner(1 - y, x, 1 - core), cys, cyr).wait_recv()
+        full(i, owner(1 - y, 1 - x, 1 - core), cds, cdr).wait_recv()
+        first(i, me, x1s, x1r, to_x).wait_send()
+        first(i, me, y1s, y1r, to_y).wait_send()
+        first(i, me, c1s, c1r, to_core).wait_send()
+        part(i, px, upper, y2s, y2r, to_y).wait_send()
+        part(i, py, lower, x2s, x2r, to_x).wait_send()
+        full(i, px, cxs, cxr).wait_send()
+        full(i, py, cys, cyr).wait_send()
+        full(i, pd, cds, cdr).wait_send()
+        keep(i).wait()
+
+    return begin, forward, final, drain
+
+
+GATHER_SEMS = 17
+
+
 BQ = 512
 
 
-def attend_forward_kernel(
-    lat_ref, cos_ref, sin_ref, segq_ref, up_ref, o_ref, lse_ref, q_ref, k_ref, v_ref, stack_q, stack_kv, wq_t
-):
-    i = pl.program_id(1)
+def attend_forward_kernel(fused, *refs):
+    lat_ref, cos_ref, sin_ref, segq_ref, up_ref, *refs = refs
+    if fused:
+        down_any, out_any, *refs = refs
+    o_ref, lse_ref, q_ref, k_ref, v_ref, *refs = refs
+    if fused:
+        att_any, down_all, out_all, *refs = refs
+    stack_q, stack_kv, wq_t, *refs = refs
+    h, i = pl.program_id(0), pl.program_id(1)
     rows = lat_ref.shape[0]
+    heads, blocks = pl.num_programs(0), rows // BQ
+    if fused:
+        place, core = lax.axis_index("fsdp"), lax.axis_index("ctx")
+        stage, att_send, att_recv, *sems = refs
+        at = h * blocks + i
+        gathers = (
+            torus_gather(out_any, out_all, sems[:GATHER_SEMS], place, core),
+            torus_gather(down_any, down_all, sems[GATHER_SEMS:], place, core),
+        )
+
+        @pl.when(at == 0)
+        def _():
+            y, x = place // 2, place % 2
+            barrier = pltpu.get_barrier_semaphore()
+            for to in ({"ctx": 1 - core}, {"fsdp": y * 2 + 1 - x}, {"fsdp": (1 - y) * 2 + x}):
+                pl.semaphore_signal(barrier, inc=1, device_id=to, device_id_type=MESH)
+            pl.semaphore_wait(barrier, 3)
+            for begin, _, _, _ in gathers:
+                begin(0)
+
+        for n in range(2):
+
+            @pl.when(at == 8 + 3 * n)
+            def _():
+                gathers[n][1](0)
+
+            @pl.when(at == 15 + 3 * n)
+            def _():
+                gathers[n][2](0)
     pieces = up_ref.shape[0]
     nq, nk = QR // pieces, KVR // pieces
 
@@ -108,33 +205,82 @@
     carried = lax.fori_loop(0, i, lambda j, c: block(j, c, False), start)
     m, acc = block(i, carried, True)
     total = acc[VD : VD + 1]
-    o_ref[0, :, here] = (acc[:VD] / total).astype(BF)
+    o = (acc[:VD] / total).astype(BF)
+    o_ref[0, :, here] = o
     lse_ref[0, :, here] = m + jnp.log2(total)
-
-
-def attend_forward(lat, cos, sin, segq, up):
+    if fused:
+        count = blocks // 2
+
+        def spot(owner, hh, b):
+            return (
+                pl.ds(pl.multiple_of((owner * heads + hh) * VD, VD), VD),
+                pl.ds(pl.multiple_of(lax.rem(b, count) * BQ, BQ), BQ),
+            )
+
+        stage[h, i] = o
+        keep = lambda hh, b: pltpu.make_async_copy(stage.at[hh, b], att_any.at[spot(core, hh, b)], att_send.at[hh, b])
+        give = lambda hh, b, owner: pltpu.make_async_remote_copy(
+            src_ref=stage.at[hh, b], dst_ref=att_any.at[spot(owner, hh, b)], send_sem=att_send.at[hh, b],
+            recv_sem=att_recv.at[hh, lax.rem(b, count)], device_id={"ctx": 1 - core}, device_id_type=MESH,
+        )
+
+        @pl.when(i // count == core)
+        def _():
+            keep(h, i).start()
+
+        @pl.when(i // count != core)
+        def _():
+            give(h, i, core).start()
+
+        @pl.when(at == heads * blocks - 1)
+        def _():
+            def done(n):
+                hh, b = n // count, lax.rem(n, count)
+                keep(hh, core * count + b).wait()
+                give(hh, (1 - core) * count + b, core).wait_send()
+                give(hh, core * count + b, 1 - core).wait_recv()
+
+            each(heads * count, done)
+            for _, _, _, drain in gathers:
+                drain(0)
+
+
+def attend_forward(lat, cos, sin, segq, up, *pieces):
     heads = up.shape[2] // 128
     rows = lat.shape[0]
+    fused = len(pieces) > 0
+    anywhere = pl.BlockSpec(memory_space=pl.ANY)
+    dma = pltpu.SemaphoreType.DMA
+    more_out, more_scratch, params = [], [], {}
+    if fused:
+        more_out = [jax.ShapeDtypeStruct((2 * heads * VD, rows // 2), BF)]
+        more_out += [jax.ShapeDtypeStruct((up.shape[0],) + p.shape, BF) for p in pieces]
+        more_scratch = [pltpu.VMEM((heads, rows // BQ, VD, BQ), BF), dma((heads, rows // BQ)), dma((heads, rows // BQ // 2))]
+        more_scratch += [dma((1,))] * (2 * GATHER_SEMS)
+        params = {"collective_id": 6, "has_side_effects": True}
     whole = lambda a: pl.BlockSpec(a.shape, lambda h, i: (0,) * a.ndim)
     per_head = lambda a, b: pl.BlockSpec((1, a, b), lambda h, i: (h, 0, 0))
     return pl.pallas_call(
-        attend_forward_kernel,
+        functools.partial(attend_forward_kernel, fused),
         grid=(heads, rows // BQ),
         in_specs=[whole(lat), whole(cos), whole(sin), whole(segq)]
-        + [pl.BlockSpec((up.shape[0], up.shape[1], 128), lambda h, i: (0, 0, h))],
-        out_specs=[per_head(VD, rows), per_head(1, rows), per_head(128, rows), per_head(rows, 128), per_head(80, rows)],
+        + [pl.BlockSpec((up.shape[0], up.shape[1], 128), lambda h, i: (0, 0, h))]
+        + [anywhere] * len(pieces),
+        out_specs=[per_head(VD, rows), per_head(1, rows), per_head(128, rows), per_head(rows, 128), per_head(80, rows)]
+        + [anywhere] * len(more_out),
         out_shape=[
             jax.ShapeDtypeStruct((heads, VD, rows), BF),
             jax.ShapeDtypeStruct((heads, 1, rows), F32),
             jax.ShapeDtypeStruct((heads, 128, rows), BF),
             jax.ShapeDtypeStruct((heads, rows, 128), BF),
             jax.ShapeDtypeStruct((heads, 80, rows), BF),
-        ],
-        scratch_shapes=[pltpu.VMEM((QR, 128), F32), pltpu.VMEM((KVR, 128), F32), pltpu.VMEM((128, QR), BF)],
-        compiler_params=pltpu.CompilerParams(vmem_limit_bytes=40 * MIB),
+        ]
+        + more_out,
+        scratch_shapes=[pltpu.VMEM((QR, 128), F32), pltpu.VMEM((KVR, 128), F32), pltpu.VMEM((128, QR), BF)] + more_scratch,
+        compiler_params=pltpu.CompilerParams(vmem_limit_bytes=40 * MIB, **params),
         cost_estimate=pl.CostEstimate(flops=heads * rows * rows * 320, bytes_accessed=30 * MIB, transcendentals=0),
         name="attend_forward",
-    )(lat, cos, sin, segq, up)
+    )(lat, cos, sin, segq, up, *pieces)
 
 
 def attend_backward_kernel(q_ref, k_ref, v_ref, o_ref, do_ref, lse_ref, cos_ref, sin_ref, dq_ref, de_ref, dkr_ref, dq_acc, delta):
@@ -229,11 +375,12 @@
 
 
 def latent_kernel(
-    x_ref, gain_ref, gain2_ref, piece_ref, up_ref, sel_ref, freq_col, freq_lane, len_ref,
-    w_ref, total, lat_ref, cos_ref, sin_ref, segq_ref, upg_ref, tcos, tsin, gains,
+    x_ref, gain_ref, gain2_ref, piece_ref, up_ref, sel_ref, freq_col, freq_lane, len_ref, gu_any,
+    w_ref, total, lat_ref, cos_ref, sin_ref, segq_ref, upg_ref, tcos, tsin, gains, gu_all,
     gat, xb, near, cross, kvg,
     w_send, w_recv, u_send, u_recv, c_send, c_recv, *sems,
 ):
+    gather_sems, sems = sems[6:], sems[:6]
     z, core, place = lax.axis_index("tp"), lax.axis_index("ctx"), lax.axis_index("fsdp")
     is_end, is_mid, partner, across = line_places(z)
     to_mid, over, to_end, first, second = line_copies(xb, near, cross, total, sems, partner, across, LAT_LINE)
@@ -271,10 +418,13 @@
     def u_copy(d, source):
         return remote(up_ref.at[lax.rem(me + d, 2)], upg_ref.at[source], u_send.at[d], u_recv.at[source], peer(d))
 
+    begin, forward, final, drain = torus_gather(gu_any, gu_all, gather_sems, place, core)
     for d in range(1, peers):
         w_copy(d, me).start()
+    begin(0)
     for d in range(1, peers):
         u_copy(d, me).start()
+    begin(1)
     gat[me] = piece_ref[...]
     upg_ref[me] = up_ref[core]
 
@@ -370,10 +520,10 @@
         def _():
             first(n)
 
-        @pl.when(jnp.logical_and(is_mid, jnp.logical_and(n >= 1, n <= count)))
-        def _():
-            second(n - 1)
-            finish_rows(n - 1)
+        @pl.when(jnp.logical_and(is_mid, jnp.logical_and(n >= DEPTH, n < count + DEPTH)))
+        def _():
+            second(n - DEPTH)
+            finish_rows(n - DEPTH)
 
         @pl.when(jnp.logical_and(is_end, n < count))
         def _():
@@ -381,7 +531,13 @@
             to_end(n).wait_recv()
             finish_rows(n)
 
-    each(count + 1, serve)
+    each(7, serve)
+    forward(0)
+    each(4, lambda n: serve(n + 7))
+    forward(1)
+    each(count + DEPTH - 11, lambda n: serve(n + 11))
+    final(0)
+    final(1)
 
     @pl.when(is_mid)
     def _():
@@ -391,6 +547,8 @@
 
         each(count, sent)
 
+    drain(0)
+    drain(1)
     for d in range(1, peers):
         w_copy(d, me).wait_send()
         u_copy(d, me).wait_send()
@@ -409,7 +567,7 @@
     return jnp.equal((index // 36 * 48 + index % 36)[:, None], jnp.arange(peers * 48)[None]).astype(BF)
 
 
-def latent_forward(x, gain, gain2, piece, up, length):
+def latent_forward(x, gain, gain2, piece, up, length, gate_up):
     rows, width = x.shape
     peers = lax.axis_size("fsdp") * lax.axis_size("ctx")
     slot = rows * lax.axis_size("ctx")
@@ -432,9 +590,10 @@
             jax.ShapeDtypeStruct((rows, 128), F32),
             jax.ShapeDtypeStruct((rows, 128), F32),
             jax.ShapeDtypeStruct((16, QR + KVR), F32),
+            jax.ShapeDtypeStruct((peers,) + gate_up.shape, BF),
         ],
-        in_specs=[vmem] * 8 + [pl.BlockSpec(memory_space=pltpu.SMEM)],
-        out_specs=[vmem] * 10,
+        in_specs=[vmem] * 8 + [pl.BlockSpec(memory_space=pltpu.SMEM), pl.BlockSpec(memory_space=pl.ANY)],
+        out_specs=[vmem] * 10 + [pl.BlockSpec(memory_space=pl.ANY)],
         scratch_shapes=[
             pltpu.VMEM((peers, PIECE, width), BF),
             pltpu.VMEM((wide, LAT_WIDE), BF),
@@ -444,14 +603,16 @@
         ]
         + [dma((peers,))] * 4
         + [dma((rows // LAT_LINE,))] * 2
-        + [dma((count,))] * 6,
+        + [dma((count,))] * 6
+        + [dma((2,))] * GATHER_SEMS,
         compiler_params=pltpu.CompilerParams(collective_id=0, has_side_effects=True, vmem_limit_bytes=48 * MIB),
         cost_estimate=pl.CostEstimate(flops=rows * LAT_WIDE * width * 2, bytes_accessed=150 * MIB, transcendentals=0),
         name="latent_forward",
-    )(x, gain, gain2, piece, up, sel, frequency[:, None], jnp.tile(frequency, 8)[None], length)
-
-
-LINE = 32
+    )(x, gain, gain2, piece, up, sel, frequency[:, None], jnp.tile(frequency, 8)[None], length, gate_up)
+
+
+LINE = 16
+DEPTH = 4
 MLP_ROWS = 256
 TILES = ((0, 384), (384, 384), (768, 384), (1152, 448))
 
@@ -494,12 +655,12 @@
 
     def first(k):
         to_mid(k).wait_recv()
-        near[piece(k)] = (source[piece(k)].astype(F32) + near[piece(k)].astype(F32)).astype(BF)
+        near[piece(k)] = source[piece(k)] + near[piece(k)]
         over(k).start()
 
     def second(k):
         over(k).wait_recv()
-        total[piece(k)] = (near[piece(k)].astype(F32) + cross[piece(k)].astype(F32)).astype(BF)
+        total[piece(k)] = near[piece(k)] + cross[piece(k)]
         to_end(k).start()
 
     return to_mid, over, to_end, first, second
@@ -516,8 +677,8 @@
 def block_kernel(
     att_ref, x_ref, out_ref, gain_ref, live_ref, seed_any, gu_any, down_any,
     hid_any, dn_any, mo_any, n2t_any, act_any, dg_any, du_any,
-    xb, near, cross, total, gu, down, n2, n2t, seed, act, dg, du,
-    load_sem, seed_sem, hid_sem, dn_sem, mo_sem, n2t_sem, act_sem, dg_sem, du_sem, *sems,
+    xb, near, cross, total, gu, down, n2, n2t, seed, d_all, act, dg, du,
+    load_sem, down_sem, seed_sem, hid_sem, dn_sem, mo_sem, n2t_sem, act_sem, dg_sem, du_sem, *sems,
 ):
     z = lax.axis_index("tp")
     is_end, is_mid, partner, across = line_places(z)
@@ -530,20 +691,25 @@
     def rows_of(m):
         return pl.ds(pl.multiple_of(m * MLP_ROWS, MLP_ROWS), MLP_ROWS)
 
-    load_gu = pltpu.make_async_copy(gu_any, gu, load_sem.at[0])
-    load_down = pltpu.make_async_copy(down_any, down, load_sem.at[1])
+    peers, shard = gu_any.shape[0], gu_any.shape[2]
+    load_gu = lambda p, i: pltpu.make_async_copy(gu_any.at[p, i], gu.at[i, pl.ds(p * shard, shard)], load_sem.at[p, i])
+    load_down = pltpu.make_async_copy(down_any, down, down_sem)
     load_seed = lambda m: pltpu.make_async_copy(seed_any.at[rows_of(m)], seed, seed_sem.at[m])
     save_hid = lambda m: pltpu.make_async_copy(total.at[rows_of(m)], hid_any.at[rows_of(m)], hid_sem.at[m])
     save_dn = lambda m: pltpu.make_async_copy(xb.at[rows_of(m)], dn_any.at[rows_of(m)], dn_sem.at[m])
-    save_mo = lambda m: pltpu.make_async_copy(cross.at[rows_of(m)], mo_any.at[rows_of(m)], mo_sem.at[m])
+    save_mo = lambda m, n: pltpu.make_async_copy(
+        cross.at[rows_of(m), pl.ds(n * width, width)], mo_any.at[n, rows_of(m)], mo_sem.at[m, n]
+    )
     save_n2t = lambda m: pltpu.make_async_copy(n2t, n2t_any.at[:, rows_of(m)], n2t_sem.at[m])
     save_act = lambda m: pltpu.make_async_copy(act, act_any.at[rows_of(m)], act_sem.at[m])
     save_dg = lambda m: pltpu.make_async_copy(dg, dg_any.at[rows_of(m)], dg_sem.at[m])
     save_du = lambda m: pltpu.make_async_copy(du, du_any.at[rows_of(m)], du_sem.at[m])
 
     load_seed(0).start()
-    load_gu.start()
     load_down.start()
+    for p in range(peers):
+        load_gu(p, 0).start()
+        load_gu(p, 1).start()
     line_barrier(is_mid, is_end, partner, across)
 
     mine = pl.ds(pl.multiple_of(z * width, 128), width)
@@ -551,26 +717,49 @@
 
     def project(p):
         rows = pl.ds(pl.multiple_of(p * per, per), per)
-        part = dot_nt(att_ref[rows, :], out_ref[...]) * RESIDUAL_SCALE
+        part = dot_nt(att_ref[:, rows].astype(F32).T.astype(BF), out_ref[...]) * RESIDUAL_SCALE
         xb[rows, :] = part.astype(BF)
         xb[rows, mine] = (xb[rows, mine].astype(F32) + x_ref[rows, :].astype(F32)).astype(BF)
 
         @pl.when(is_end)
         def _():
-            for n in range(per // LINE):
-                to_mid(p * (per // LINE) + n).start()
+            each(per // LINE, lambda n: to_mid(p * (per // LINE) + n).start())
 
     each(xb.shape[0] // per, project)
 
     @pl.when(is_mid)
     def _():
-        first(0)
-
-        def both(k):
-            first(k + 1)
-            second(k)
-
-        each(group, both)
+        each(DEPTH, first)
+
+    load_down.wait()
+    ahead = group // len(TILES) // groups
+
+    def seed_product(m):
+        load_seed(m).wait()
+
+        def weigh(r):
+            here = pl.ds(pl.multiple_of(r * 32, 32), 32)
+            live = live_ref[pl.ds(pl.multiple_of(m * MLP_ROWS + r * 32, 32), 32), :]
+            seed[here, :] = (seed[here, :].astype(F32) * (live * RESIDUAL_SCALE)).astype(BF)
+
+        each(MLP_ROWS // 32, weigh)
+        for t, (at, size) in enumerate(TILES):
+            d_all[rows_of(m), pl.ds(at, size)] = dot_nn(seed[...], down[:, pl.ds(at, size)]).astype(BF)
+
+            @pl.when(is_mid)
+            def _():
+                def both(v):
+                    k = (m * len(TILES) + t) * ahead + v
+                    first(k + DEPTH)
+                    second(k)
+
+                each(ahead, both)
+
+        @pl.when(m + 1 < groups)
+        def _():
+            load_seed(m + 1).start()
+
+    each(groups, seed_product)
 
     def mlp(m):
         rows = rows_of(m)
@@ -584,15 +773,18 @@
             each(group, arrive)
 
         def serve(n):
-            k = (m + 1) * group + 1 + n
-
-            @pl.when(jnp.logical_and(is_mid, k < count))
-            def _():
-                first(k)
-
-            @pl.when(jnp.logical_and(is_mid, k <= count))
-            def _():
-                second(k - 1)
+            def one(v):
+                k = (m + 1) * group + DEPTH + n * (group // 8) + v
+
+                @pl.when(jnp.logical_and(is_mid, k < count))
+                def _():
+                    first(k)
+
+                @pl.when(jnp.logical_and(is_mid, k < count + DEPTH))
+                def _():
+                    second(k - DEPTH)
+
+            each(group // 8, one)
 
         save_hid(m).start()
 
@@ -617,25 +809,17 @@
 
         each(D // 256, turn)
         save_n2t(m).start()
-        load_seed(m).wait()
-
-        def weigh(r):
-            here = pl.ds(pl.multiple_of(r * 32, 32), 32)
-            live = live_ref[pl.ds(pl.multiple_of(m * MLP_ROWS + r * 32, 32), 32), :]
-            seed[here, :] = (seed[here, :].astype(F32) * (live * RESIDUAL_SCALE)).astype(BF)
-
-        each(MLP_ROWS // 32, weigh)
-
         @pl.when(m == 0)
         def _():
-            load_gu.wait()
-            load_down.wait()
+            for p in range(peers):
+                load_gu(p, 0).wait()
+                load_gu(p, 1).wait()
 
         for t, (at, size) in enumerate(TILES):
             cols = pl.ds(at, size)
             g = dot_nn(n2[...], gu[0, :, cols])
             u = dot_nn(n2[...], gu[1, :, cols])
-            d = dot_nn(seed[...], down[:, cols])
+            d = d_all[rows, cols].astype(F32)
             sig = jax.nn.sigmoid(g)
             act[:, cols] = (g * sig * u).astype(BF)
             dg[:, cols] = (d * u * sig * (1.0 + g * (1.0 - sig))).astype(BF)
@@ -645,24 +829,22 @@
         save_dg(m).start()
         save_du(m).start()
 
-        @pl.when(m + 1 < groups)
-        def _():
-            load_seed(m + 1).start()
-
         for n in range(4):
             cols = pl.ds(n * 640, 640)
             xb[rows, cols] = (dot_nt(dg[...], gu[0, cols, :]) + dot_nt(du[...], gu[1, cols, :])).astype(BF)
             cross[rows, cols] = dot_nt(act[...], down[cols, :]).astype(BF)
             serve(4 + n)
         save_dn(m).start()
-        save_mo(m).start()
+        for n in range(4):
+            save_mo(m, n).start()
 
     each(groups, mlp)
 
     def finish(m):
         save_hid(m).wait()
         save_dn(m).wait()
-        save_mo(m).wait()
+        for n in range(4):
+            save_mo(m, n).wait()
 
     each(groups, finish)
     save_n2t(groups - 1).wait()
@@ -680,7 +862,7 @@
 
 
 def block_forward(att, x, out_t, gain, live, seed, gate_up, down_t):
-    rows = att.shape[0]
+    rows, width = x.shape
     hidden_units = down_t.shape[1]
     count, groups = rows // LINE, rows // MLP_ROWS
     vmem = pl.BlockSpec(memory_space=pltpu.VMEM)
@@ -690,20 +872,23 @@
     dma = pltpu.SemaphoreType.DMA
     return pl.pallas_call(
         block_kernel,
-        out_shape=[wide, wide, wide, jax.ShapeDtypeStruct((D, rows), BF), units, units, units],
+        out_shape=[wide, wide, jax.ShapeDtypeStruct((4, rows, width), BF), jax.ShapeDtypeStruct((D, rows), BF), units, units, units],
         in_specs=[vmem] * 5 + [anywhere] * 3,
         out_specs=[anywhere] * 7,
         scratch_shapes=[pltpu.VMEM((rows, D), BF)] * 4
         + [
-            pltpu.VMEM(gate_up.shape, BF),
+            pltpu.VMEM((2, D, hidden_units), BF),
             pltpu.VMEM(down_t.shape, BF),
             pltpu.VMEM((MLP_ROWS, D), BF),
             pltpu.VMEM((D, MLP_ROWS), BF),
             pltpu.VMEM((MLP_ROWS, D), BF),
+            pltpu.VMEM((rows, hidden_units), BF),
         ]
         + [pltpu.VMEM((MLP_ROWS, hidden_units), BF)] * 3
-        + [dma((2,))]
-        + [dma((groups,))] * 8
+        + [dma(gate_up.shape[:2]), dma]
+        + [dma((groups,))] * 3
+        + [dma((groups, 4))]
+        + [dma((groups,))] * 4
         + [dma((count,))] * 6,
         compiler_params=pltpu.CompilerParams(collective_id=3, has_side_effects=True, vmem_limit_bytes=63 * MIB),
         cost_estimate=pl.CostEstimate(flops=rows * D * hidden_units * 12, bytes_accessed=400 * MIB, transcendentals=0),
@@ -711,7 +896,8 @@
     )(att, x, out_t, gain, live, seed, gate_up, down_t)
 
 
-LAG = 3
+LAG = 8
+ROWS = 32
 LOAD = 128
 
 
@@ -741,6 +927,12 @@
     def piece(k):
         return pl.ds(pl.multiple_of(k * LINE, LINE), LINE)
 
+    def band(e):
+        return pl.ds(pl.multiple_of(e * ROWS, ROWS), ROWS)
+
+    bands = total.shape[0] // ROWS
+    twice = ROWS // LINE
+
     def remote(src, dst, send, recv, to):
         return pltpu.make_async_remote_copy(
             src_ref=src, dst_ref=dst, send_sem=send, recv_sem=recv, device_id=to, device_id_type=MESH
@@ -754,8 +946,8 @@
     rows_of = lambda g: pl.ds(pl.multiple_of(g * LOAD, LOAD), LOAD)
     load_h = lambda g: local(hid_any.at[rows_of(g)], hbuf.at[g % 2], h_sem.at[g])
     load_c = lambda g: local(cot_any.at[rows_of(g)], cbuf.at[g % 2], c_sem.at[g])
-    save_sa = lambda e: local(sbuf.at[e % 2], sa_any.at[piece(e)], sa_sem.at[e])
-    save_dh = lambda e: local(dbuf.at[e % 2], dh_any.at[piece(e)], dh_sem.at[e])
+    save_sa = lambda e: local(sbuf.at[e % 2], sa_any.at[band(e)], sa_sem.at[e])
+    save_dh = lambda e: local(dbuf.at[e % 2], dh_any.at[band(e)], dh_sem.at[e])
 
     load_lhs.start()
     load_rhs(0).start()
@@ -788,7 +980,7 @@
         load_total.wait()
 
     def finish_rows(e):
-        per = LOAD // LINE
+        per = LOAD // ROWS
         g = e // per
 
         @pl.when(e % per == 0)
@@ -796,7 +988,7 @@
             load_h(g).wait()
             load_c(g).wait()
 
-            @pl.when(g + 1 < count // per)
+            @pl.when(g + 1 < bands // per)
             def _():
                 load_h(g + 1).start()
                 load_c(g + 1).start()
@@ -806,19 +998,19 @@
             save_sa(e - 2).wait()
             save_dh(e - 2).wait()
 
-        here = pl.ds(pl.multiple_of((e % per) * LINE, LINE), LINE)
-        live = live_ref[piece(e), :]
+        here = pl.ds(pl.multiple_of((e % per) * ROWS, ROWS), ROWS)
+        live = live_ref[band(e), :]
 
         def grads_of(dn, h, dy, gain, factor, inner):
             return dy * live + factor * (dn * gain) - h * (factor * factor * factor * inner)
 
-        dn = total[piece(e), :].astype(F32)
+        dn = total[band(e), :].astype(F32)
         h = hbuf[g % 2, here, :].astype(F32)
         factor = lax.rsqrt(jnp.mean(h * h, axis=1, keepdims=True) + EPS_NORM)
         inner = jnp.mean(dn * gain_ref[...] * h, axis=1, keepdims=True)
         dy = cbuf[g % 2, here, :].astype(F32)
         sbuf[e % 2] = (RESIDUAL_SCALE * grads_of(dn, h, dy, gain_ref[...], factor, inner)).astype(BF)
-        own_dn = total[piece(e), mine].astype(F32)
+        own_dn = total[band(e), mine].astype(F32)
         own_h = hbuf[g % 2, here, mine].astype(F32)
         own_dy = cbuf[g % 2, here, mine].astype(F32)
         dbuf[e % 2] = grads_of(own_dn, own_h, own_dy, gain_ref[:, mine], factor, inner)
@@ -830,21 +1022,29 @@
         @pl.when(jnp.logical_and(is_mid, n < count))
         def _():
             to_mid(n).wait_recv()
-            near[piece(n)] = (total[piece(n)].astype(F32) + near[piece(n)].astype(F32)).astype(BF)
+            near[piece(n)] = total[piece(n)] + near[piece(n)]
             over(n).start()
 
-        @pl.when(jnp.logical_and(is_mid, jnp.logical_and(n >= 1, n <= count)))
-        def _():
-            over(n - 1).wait_recv()
-            total[piece(n - 1)] = (near[piece(n - 1)].astype(F32) + cross[piece(n - 1)].astype(F32)).astype(BF)
-            to_end(n - 1).start()
-            finish_rows(n - 1)
+        @pl.when(jnp.logical_and(is_mid, jnp.logical_and(n >= DEPTH, n < count + DEPTH)))
+        def _():
+            k = n - DEPTH
+            over(k).wait_recv()
+            total[piece(k)] = near[piece(k)] + cross[piece(k)]
+            to_end(k).start()
+
+            @pl.when(k % twice == twice - 1)
+            def _():
+                finish_rows(k // twice)
 
         @pl.when(jnp.logical_and(is_end, jnp.logical_and(n >= LAG, n < count + LAG)))
         def _():
-            to_mid(n - LAG).wait_send()
-            to_end(n - LAG).wait_recv()
-            finish_rows(n - LAG)
+            k = n - LAG
+            to_mid(k).wait_send()
+            to_end(k).wait_recv()
+
+            @pl.when(k % twice == twice - 1)
+            def _():
+                finish_rows(k // twice)
 
     def flip(v, by):
         return v + by - 2 * v * by
@@ -955,12 +1155,20 @@
     first_stage(0)
     load_rhs(2).wait()
     products(2, 16 + groups)
+    served = 24 + groups
+
+    def serve_until(stop, served):
+        each(stop - served, lambda n: serve(n + served))
+        return stop
+
     first_stage(1)
+    served = serve_until(42, served)
     second_stage(0)
-    for n in range(24 + groups, count + LAG):
-        serve(n)
+    served = serve_until(50, served)
     first_stage(2)
+    served = serve_until(58, served)
     second_stage(1)
+    serve_until(count + LAG, served)
     second_stage(2)
     for i in range(3):
         for v in range(2):
@@ -970,7 +1178,7 @@
         x2_copy(i).wait_send()
         save_upper(i).wait()
         save_lower(i).wait()
-    for e in (count - 2, count - 1):
+    for e in (bands - 2, bands - 1):
         save_sa(e).wait()
         save_dh(e).wait()
 
@@ -1016,11 +1224,11 @@
             scratch(2, rows, units),
             scratch(2, LOAD, D),
             scratch(2, LOAD, D),
-            scratch(2, LINE, D),
-            pltpu.VMEM((2, LINE, width), F32),
+            scratch(2, ROWS, D),
+            pltpu.VMEM((2, ROWS, width), F32),
             scratch(2, rows, 256),
         ]
-        + [dma, dma, dma((3,)), dma((rows // LOAD,)), dma((rows // LOAD,)), dma((count,)), dma((count,)), dma((D // 256,)), dma((3, 2))]
+        + [dma, dma, dma((3,)), dma((rows // LOAD,)), dma((rows // LOAD,)), dma((rows // ROWS,)), dma((rows // ROWS,)), dma((D // 256,)), dma((3, 2))]
         + [dma((3, 4))] * 2
         + [dma((3, 2))] * 4
         + [dma((3,))] * 4
@@ -1033,6 +1241,7 @@
 
 PACK = 576
 HALF = PACK // 2
+SHARE = 256
 
 
 def torus(s1, xin, yin2, yin, xin2, sems, x, y, to_x, to_y):
@@ -1089,9 +1298,9 @@
 
 def latent_back_kernel(
     dq_ref, de_ref, dkr_ref, up_ref, sum_ref, w_ref, x_ref, gain_ref, dh_ref, tcos, tsin, gains, gout_ref, gq_ref, gkv_ref,
-    sel_ref, b2_ref, square_ref,
-    gin_ref, pack_out, wd_out, small_out, scalar_out,
-    uq, ukv, away, arrived, xb, near, cross, total, dl, dlt, xg, w_pack, small, small_in, scal_in,
+    sel_ref, b2_ref, square_ref, fold_ref,
+    gin_ref, pack_out, wd_out, small_out, scalar_out, gq_out, gkv_out,
+    uq, ukv, away, arrived, xb, near, cross, total, dl, dlt, xg, weight, w_pack, small, small_in, scal_in,
     s1, cin, xin, yin2, yin, xin2, s1w, cinw, xinw, yin2w, yinw, xin2w,
     lat_send, lat_recv, out_send, out_recv, q_send, q_recv, kv_send, kv_recv, w_send, w_recv,
     small_send, small_recv, scal_send, scal_recv, *sems,
@@ -1142,41 +1351,43 @@
         ukv[p * 32 : (p + 1) * 32, :] = up_ref[p, 96:128, :]
 
     lane = lax.broadcasted_iota(jnp.int32, (1, 128), 1)
-    hand = lambda e: remote(away.at[piece(e)], arrived.at[piece(e)], lat_send.at[e], lat_recv.at[e], to_core)
+    block = lambda e: pl.ds(pl.multiple_of(e * SHARE, SHARE), SHARE)
+    hand = lambda e: remote(away.at[block(e)], arrived.at[block(e)], lat_send.at[e], lat_recv.at[e], to_core)
+    shares = rows // SHARE
 
     def share(at):
-        here = pl.ds(pl.multiple_of(at, LAT_LINE), LAT_LINE)
+        here = pl.ds(pl.multiple_of(at, SHARE), SHARE)
         q = dot_nt(dq_ref[here, :], uq[...])
         kv = dot_nt(de_ref[here, :], ukv[...])
         rope = jnp.where(lane < ROPE, pltpu.roll(dkr_ref[here, :], NOPE, 1), 0.0)
         return q, kv, rope
 
     def send_away(e):
-        q, kv, rope = share((1 - core) * rows + e * LAT_LINE)
-        away[piece(e), 0:QR] = q.astype(BF)
-        away[piece(e), QR : QR + KVR] = kv.astype(BF)
-        away[piece(e), QR + KVR : LAT_WIDE] = rope.astype(BF)
+        q, kv, rope = share((1 - core) * rows + e * SHARE)
+        away[block(e), 0:QR] = q.astype(BF)
+        away[block(e), QR : QR + KVR] = kv.astype(BF)
+        away[block(e), QR + KVR : LAT_WIDE] = rope.astype(BF)
         hand(e).start()
 
-    each(count, send_away)
+    each(shares, send_away)
     for f in range(4):
         out_copy(f).start()
         q_copy(f).start()
         kv_copy(f).start()
 
     def keep(e):
-        q, kv, rope = share(core * rows + e * LAT_LINE)
+        q, kv, rope = share(core * rows + e * SHARE)
         hand(e).wait_recv()
-        got = arrived[piece(e), :].astype(F32)
-        xb[piece(e), 0:QR] = (q + got[:, 0:QR]).astype(BF)
-        xb[piece(e), QR : QR + KVR] = (kv + got[:, QR : QR + KVR]).astype(BF)
-        xb[piece(e), QR + KVR : LAT_WIDE] = (rope + got[:, QR + KVR :]).astype(BF)
+        got = arrived[block(e), :].astype(F32)
+        xb[block(e), 0:QR] = (q + got[:, 0:QR]).astype(BF)
+        xb[block(e), QR : QR + KVR] = (kv + got[:, QR : QR + KVR]).astype(BF)
+        xb[block(e), QR + KVR : LAT_WIDE] = (rope + got[:, QR + KVR :]).astype(BF)
 
         @pl.when(is_end)
         def _():
-            to_mid(e).start()
-
-    each(count, keep)
+            each(SHARE // LAT_LINE, lambda n: to_mid(e * (SHARE // LAT_LINE) + n).start())
+
+    each(shares, keep)
 
     small[...] = jnp.zeros_like(small)
     small[2:3, 0 : b2_ref.shape[1]] = b2_ref[...]
@@ -1212,17 +1423,16 @@
         dl[piece(e), 0:QR] = (dql * factor).astype(BF)
         dl[piece(e), QR : QR + KVR] = (dkl * factor).astype(BF)
         dl[piece(e), QR + KVR : LAT_WIDE] = (rope * factor).astype(BF)
-        d_in = dot_nn(dl[piece(e), :], w_ref[...])
-        xin_rows = x_ref[piece(e), :].astype(F32)
-        gin_ref[piece(e), :] = (
-            dh_ref[piece(e), :] + d_in * gain_ref[...] - xin_rows * (factor * factor * inner)
-        ).astype(BF)
-        small[1:2, 0 : d_in.shape[1]] += jnp.sum(d_in * xin_rows, axis=0, keepdims=True)
-        xg[piece(e), :] = (xin_rows * gain_ref[...]).astype(BF)
+        weight[piece(e), :] = jnp.broadcast_to(factor * factor * inner, (LAT_LINE, 128))
 
         @pl.when(e % 2 == 1)
         def _():
             pair = pl.ds(pl.multiple_of((e - 1) * LAT_LINE, 128), 128)
+            d_in = dot_nn(dl[pair, :], w_ref[...])
+            rows_in = x_ref[pair, :].astype(F32)
+            gin_ref[pair, :] = (dh_ref[pair, :] + d_in * gain_ref[...] - rows_in * weight[pair, 0:1]).astype(BF)
+            small[1:2, 0 : d_in.shape[1]] += jnp.sum(d_in * rows_in, axis=0, keepdims=True)
+            xg[pair, :] = (rows_in * gain_ref[...]).astype(BF)
             dlt[:, pair] = dl[pair, :].astype(F32).T.astype(BF)
 
     def serve(n):
@@ -1230,16 +1440,16 @@
         def _():
             first(n)
 
-        @pl.when(jnp.logical_and(is_mid, jnp.logical_and(n >= 1, n <= count)))
-        def _():
-            second(n - 1)
-            finish_rows(n - 1)
-
-        @pl.when(jnp.logical_and(is_end, jnp.logical_and(n >= 2, n < count + 2)))
-        def _():
-            to_mid(n - 2).wait_send()
-            to_end(n - 2).wait_recv()
-            finish_rows(n - 2)
+        @pl.when(jnp.logical_and(is_mid, jnp.logical_and(n >= DEPTH, n < count + DEPTH)))
+        def _():
+            second(n - DEPTH)
+            finish_rows(n - DEPTH)
+
+        @pl.when(jnp.logical_and(is_end, jnp.logical_and(n >= 4, n < count + 4)))
+        def _():
+            to_mid(n - 4).wait_send()
+            to_end(n - 4).wait_recv()
+            finish_rows(n - 4)
 
     begin, middle, last, drain = torus(s1, xin, yin2, yin, xin2, pack_sems, x, y, to_x, to_y)
     begin_w, middle_w, last_w, drain_w = torus(s1w, xinw, yin2w, yinw, xin2w, w_sems, x, y, to_x, to_y)
@@ -1257,7 +1467,11 @@
     middle()
     each(4, lambda n: serve(n + 7))
     last(pack_out)
-    each(count + 2 - 11, lambda n: serve(n + 11))
+    lanes = pack_out.shape[1]
+    gq_out[...] = dot_nn(pack_out[320:416, :], fold_ref[0:lanes, :]) + dot_nn(pack_out[416:512, :], fold_ref[lanes:, :])
+    gkv_out[:, 0:lanes] = pack_out[512:544, :].astype(F32)
+    gkv_out[:, lanes : 2 * lanes] = pack_out[544:576, :].astype(F32)
+    each(count + 4 - 11, lambda n: serve(n + 11))
 
     both = dot_nn(dlt[0:QR, :], xg[...])
     for p in range(peers):
@@ -1323,7 +1537,7 @@
         q_copy(f).wait_send()
         kv_copy(f).wait_send()
         w_copy(f).wait_send()
-    each(count, lambda e: hand(e).wait_send())
+    each(shares, lambda e: hand(e).wait_send())
 
     @pl.when(is_mid)
     def _():
@@ -1353,14 +1567,17 @@
             jax.ShapeDtypeStruct((PIECE, width), BF),
             jax.ShapeDtypeStruct((8, QR + KVR), F32),
             jax.ShapeDtypeStruct((8, 128), F32),
+            jax.ShapeDtypeStruct((QR // peers, args[-1].shape[1]), F32),
+            jax.ShapeDtypeStruct((KVR // peers, args[-1].shape[0]), F32),
         ],
         in_specs=[vmem] * len(args),
-        out_specs=[vmem] * 5,
+        out_specs=[vmem] * 7,
         scratch_shapes=[scratch(QR, lanes), scratch(KVR, lanes)]
         + [scratch(rows, LAT_WIDE)] * 7
         + [
             scratch(LAT_WIDE, rows),
             scratch(rows, width),
+            pltpu.VMEM((rows, 128), F32),
             scratch(peers, PIECE, width),
             pltpu.VMEM((8, QR + KVR), F32),
             pltpu.VMEM((peers, 8, QR + KVR), F32),
@@ -1371,7 +1588,7 @@
         + halves(HALF)
         + [scratch(4, PIECE, width), scratch(4, PIECE, width)]
         + halves(PIECE // 2)
-        + [dma((count,))] * 2
+        + [dma((rows // SHARE,))] * 2
         + [dma((4,))] * 8
         + [dma((peers,))] * 2
         + [dma((4,))] * 2
@@ -1479,9 +1696,6 @@
     own_segment = (own_index >= seq_length).astype(jnp.int32)
     live = (own_segment == 0).astype(F32)[:, None]
 
-    out_t = gather_shards(w_out.T.astype(BF))
-    gate_up = lax.all_gather(w_gateup.astype(BF), ("fsdp", "ctx"), axis=1, tiled=True)
-    ff_down_t = gather_shards(w_down.T.astype(BF))
     q_shard = jnp.pad(
         w_qup.astype(BF).reshape(w_qup.shape[0], heads_all, HEAD), ((0, 0), (0, 0), (0, 128 - HEAD))
     ).reshape(w_qup.shape[0], heads_all * 128)
@@ -1498,11 +1712,14 @@
         )
         up_pair = jnp.stack([up_shard[:, : heads * 128], up_shard[:, heads * 128 :]])
         gain_wide = jnp.pad(gains_norm[1].astype(F32), (0, LAT_WIDE - width))[None]
-        down_t, lat_sum, lat_all, cos_t, sin_t, seg_q, up, tcos, tsin, gains_lat = latent_forward(
-            tokens, gain_attn[None], gain_wide, piece, up_pair, lengths
+        down_t, lat_sum, lat_all, cos_t, sin_t, seg_q, up, tcos, tsin, gains_lat, gate_up = latent_forward(
+            tokens, gain_attn[None], gain_wide, piece, up_pair, lengths, w_gateup.astype(BF)
         )
         gain_mlp = lat_sum[rows : rows + n_tp, :width].reshape(D).astype(F32)
     else:
+        out_t = gather_shards(w_out.T.astype(BF))
+        gate_up = lax.all_gather(w_gateup.astype(BF), ("fsdp", "ctx"), axis=1, tiled=True)
+        ff_down_t = gather_shards(w_down.T.astype(BF))
         index = jnp.arange(slot, dtype=jnp.int32)
         segment = (index >= seq_length).astype(jnp.int32)
         position = (index - segment * seq_length).astype(F32)
@@ -1545,20 +1762,26 @@
         lat_all = jnp.concatenate([lat_both, seg_k, jnp.zeros((slot, 128 - HEAD - 2), BF)], axis=1)
     qn, kn = lat_all[:, :QR], lat_all[:, QR : QR + KVR]
 
-    att_heads, lse, q_t, k_rows, v_t = attend_forward(lat_all, cos_t, sin_t, seg_q, up)
-    att_flat = att_heads.reshape(heads * VD, slot)
-    own_cols = lambda v: lax.dynamic_slice_in_dim(v, core * rows, rows, 1)
-    if by_head:
-        other = swap_cores(lax.dynamic_slice_in_dim(att_flat, (1 - core) * rows, rows, 1))
-        att_t = in_core_order(own_cols(att_flat), other, core, 0)
+    if fused:
+        att_heads, lse, q_t, k_rows, v_t, att_t, ff_down_t, out_t = attend_forward(
+            lat_all, cos_t, sin_t, seg_q, up, w_down.T.astype(BF)[None], w_out.T.astype(BF)[None]
+        )
+        ff_down_t, out_t = ff_down_t.reshape(D, -1), out_t.reshape(D, -1)
     else:
-        att_t = own_cols(att_flat)
+        att_heads, lse, q_t, k_rows, v_t = attend_forward(lat_all, cos_t, sin_t, seg_q, up)
+        att_flat = att_heads.reshape(heads * VD, slot)
+        own_cols = lambda v: lax.dynamic_slice_in_dim(v, core * rows, rows, 1)
+        if by_head:
+            other = swap_cores(lax.dynamic_slice_in_dim(att_flat, (1 - core) * rows, rows, 1))
+            att_t = in_core_order(own_cols(att_flat), other, core, 0)
+        else:
+            att_t = own_cols(att_flat)
 
     feature_owner = jnp.arange(D) // width
     own_features = lambda v: lax.dynamic_slice_in_dim(v, tp * width, width, 1)
     if fused:
         hidden, d_normed_part, mlp_part, normed_two_t, activation, d_gate, d_up = block_forward(
-            att_t.T, tokens, out_t, gain_mlp[None], live, cotangent, gate_up, ff_down_t
+            att_t, tokens, out_t, gain_mlp[None], live, cotangent, gate_up, ff_down_t
         )
         attn_seed, d_hidden, grad_gain_mlp, grads, grad_squares = grad_reduce(
             live, gain_mlp[None], d_normed_part, hidden, cotangent, normed_two_t, d_gate, d_up, activation
@@ -1595,7 +1818,10 @@
         d_hidden = own_features(d_hidden_full)
         grad_gain_mlp = jnp.sum(own_features(d_normed * hidden_f) * factor_two, axis=0)
     mlp_part, attn_seed = lax.optimization_barrier((mlp_part, attn_seed))
-    mlp_out = lax.psum_scatter(mlp_part, "tp", scatter_dimension=1, tiled=True).astype(F32)
+    if fused:
+        mlp_out = lax.psum_scatter(mlp_part, "tp", scatter_dimension=0, tiled=False).astype(F32)
+    else:
+        mlp_out = lax.psum_scatter(mlp_part, "tp", scatter_dimension=1, tiled=True).astype(F32)
     layer_out = (own_features(hidden).astype(F32) + RESIDUAL_SCALE * mlp_out).astype(BF)
     d_att_t = lax.dot_general(out_t, attn_seed, (((0,), (1,)), ((), ())), preferred_element_type=F32).astype(BF)
     grad_out = dot_tn(attn_seed, att_t.T).astype(BF)
@@ -1617,16 +1843,20 @@
     share = g_latent.shape[0]
     my_share = (lax.axis_index("fsdp") * n_ctx + core) * share
     if fused:
-        grad_input, pack, wd_grad, small, scalars = latent_backward(
+        head_row = jnp.arange(heads_all * 128)
+        fold = jnp.equal(
+            jnp.where(head_row % 128 < HEAD, head_row // 128 * HEAD + head_row % 128, -1)[:, None],
+            jnp.arange(heads_all * HEAD)[None],
+        ).astype(BF)
+        grad_input, pack, wd_grad, small, scalars, grad_qup, grad_kvup = latent_backward(
             d_q, d_e, d_kr, up, lat_sum, down_t, tokens, gain_attn[None], d_hidden, tcos, tsin, gains_lat,
-            grad_out, grad_qup, grad_kvup, spread(n_fsdp * n_ctx), grad_gain_mlp, grad_squares,
+            grad_out, grad_qup, grad_kvup, spread(n_fsdp * n_ctx), grad_gain_mlp, grad_squares, fold,
         )
-        lanes = heads * 128
         owned = [
             wd_grad[:96].astype(F32).T,
             wd_grad[96:132].astype(F32).T,
-            heads_only(jnp.concatenate([pack[320:416], pack[416:512]], axis=1)).astype(F32),
-            jnp.concatenate([pack[512:544], pack[544:576]], axis=1).astype(F32),
+            grad_qup,
+            grad_kvup,
             pack[:320].astype(F32).T,
             grads[:2].astype(F32),
             grads[2].astype(F32).T,

time: 823 us -> 753 us (0.915)
  waiting for transfers between devices: 50.7 us -> 0.03 us
  local copies, waits for them, and re-layouts: 39.9 us -> 18.5 us
    all_gather x3 -> x0, waiting for transfers between devices: 50.7 us -> none  [the longest x1 50.7 us: local(): lax.all_gather(w_gateup.astype(BF), ('fsdp', 'ctx'), axis=1, tiled=True)]
    pallas_call x1, Pallas kernels: 96.1 us -> 126 us  [latent_forward(): pl.pallas_call(latent_kernel, out_shape=[jax.ShapeDtypeStruct((LAT_WIDE,...]
    pallas_call x1, Pallas kernels: 162 us -> 135 us  [grad_reduce(): pl.pallas_call(grad_kernel, out_shape=[jax.ShapeDtypeStruct((rows, D), BF...]
    unnamed x116 -> x105, local copies, waits for them, and re-layouts: 32.7 us -> 13.4 us
  transfers between devices with their start and end apart: 6 -> 2, of which waited for: 1 -> 0; matrix products, arithmetic and copies ran while one was open for 9% -> 8% of each run, Pallas kernels for 36% -> 21%
where the time goes in v4:
time: 753 us; the launch traced here: 744 us
  Pallas kernels  636 us (84%)
  other arithmetic  44.9 us (6%)
  matrix products  22.7 us (3%)
  between operations  22.2 us (3%)
  local copies, waits for them, and re-layouts  18.5 us (2%)
    pallas_call x1, Pallas kernels, block_forward(): pl.pallas_call(block_kernel, out_shape=[wide, wide, jax.ShapeDtypeStruct(...  159 us
    pallas_call x1, Pallas kernels, grad_reduce(): pl.pallas_call(grad_kernel, out_shape=[jax.ShapeDtypeStruct((rows, D), BF...  135 us
    pallas_call x1, Pallas kernels, latent_forward(): pl.pallas_call(latent_kernel, out_shape=[jax.ShapeDtypeStruct((LAT_WIDE,...  126 us
    pallas_call x1, Pallas kernels, latent_backward(): pl.pallas_call(latent_back_kernel, out_shape=[jax.ShapeDtypeStruct((rows,...  109 us
    pallas_call x1, Pallas kernels, attend_forward(): pl.pallas_call(functools.partial(attend_forward_kernel, fused), grid=(hea...  59 us
    pallas_call x1, Pallas kernels, attend_backward(): pl.pallas_call(attend_backward_kernel, grid=(heads, rows // BQ), in_specs...  49 us
    sub x7, other arithmetic, adamw_update(): parameter - LEARN_RATE * (first_hat / (jnp.sqrt(second_hat) + ADAM_EPS) +...  24.8 us
  transfers between devices with their start and end apart: 2, of which 0 were waited for; matrix products, arithmetic and copies ran while one was open for 8% of the time, Pallas kernels for 21%

profile of v4, /device:TPU:0, one launch (start us, length us, event | category | flops | bytes accessed | tf_op | source)
XLA Modules:
  0.0 744.4 jit_solution(8098254405138747428)
XLA Ops:
  7.3 1.2 copy.68
  11.3 3.8 convert_element_type.140.gu_any
  15.3 1.8 convert_bitcast_fusion.1.refs_5_
  17.4 126.0 %latent_forward.1 = (bf16[1152,640]{1,0:T(8,128)(2,1)}, bf16[1088,1152]{1,0:T(8,128)(2,1)}, bf16[2048,1152]{1,0:T(8,128)(2,1)}, f32[16,2048]{1,0:T(8,128)S(1)}, ...) custom-call(bf16[1024,640]{1,0:T(8,128)(2,1)S(1)} %copy-done.2, ...), custom_call_target="tpu_custom_call" | custom-call | flops 1509949440 | bytes 157286400 | tf_op jit(solution)/shard_map/latent_forward/pallas_call | solution.py:580
  147.2 59.0 %attend_forward.1 = (bf16[5,64,2048]{2,1,0:T(8,128)(2,1)S(1)}, f32[5,1,2048]{2,1,0:T(1,128)S(1)}, bf16[5,128,2048]{2,1,0:T(8,128)(2,1)S(1)}, bf16[5,2048,128]{2,...) custom-call(bf16[2048,1152]{1,0:T(8,128)(2,1)} %get-tuple-element.79, ...), custom_call_target="tpu_custom_call" | custom-call | flops 6710886400 | bytes 31457280 | tf_op jit(solution)/shard_map/attend_forward/pallas_call | solution.py:263
  206.2 1.0 copy-done.10
  207.2 1.5 copy-done.12
  208.7 1.5 copy-done.14
  210.2 1.2 copy-done.15
  211.4 1.1 copy-done.17
  212.4 158.7 %block_forward.1 = (bf16[1024,2560]{1,0:T(8,128)(2,1)}, bf16[1024,2560]{1,0:T(8,128)(2,1)}, bf16[4,1024,640]{2,1,0:T(8,128)(2,1)}, bf16[2560,1024]{1,0:T(8,128)(...) custom-call(bf16[640,1024]{1,0:T(8,128)(2,1)} %copy-done.10, ...), custom_call_target="tpu_custom_call" | custom-call | flops 50331648000 | bytes 419430400 | tf_op jit(solution)/shard_map/block_forward/pallas_call | solution.py:873
  371.1 134.9 %grad_reduce.1 = (bf16[1024,2560]{1,0:T(8,128)(2,1)}, f32[1024,640]{1,0:T(8,128)}, f32[1,640]{1,0:T(1,128)}, bf16[3,320,1600]{2,1,0:T(8,128)(2,1)}, f32[8,128]{1,0:T(8,128)}) custom-call(f32[1024,1]{1,0:T(8,128)} %fusion.11.live_ref, f32[1,2560]{1,0:T(1,128)} %bitcast.76, bf16[1024,2560]{1,0:T(8,128)(2,1)} %get-tuple-element.91.dnp_any, ...), custom_call_target="tpu_custom_call" | custom-call | flops 25165824000 | bytes 419430400 | tf_op jit(solution)/shard_map/grad_reduce/pallas_call | solution.py:1204
  506.0 8.1 %convolution_convert_fusion.1 = bf16[640,1024]{1,0:T(8,128)(2,1)} fusion(bf16[2560,640]{1,0:T(8,128)(2,1)} %bitcast.79, bf16[1024,2560]{1,0:T(8,128)(2,1)} %get-tuple-element.102), kind=kOutput, calls=%fused_computation.17 | convolution fusion | flops 3356098560 | bytes 9830400 | tf_op jit(solution)/shard_map/dot_general | solution.py:1826
  514.2 2.3 constant_dynamic-slice_fusion.2
  516.5 8.6 %convolution_convert_fusion.gout_ref = bf16[2560,640]{1,0:T(8,128)(2,1)} fusion(bf16[1024,2560]{1,0:T(8,128)(2,1)} %get-tuple-element.102, bf16[640,1024]{1,0:T(8,128)(2,1)S(1)} %copy-done.11), kind=kOutput, calls=%fused_computation.3 | convolution fusion | flops 3357081600 | bytes 9830400 | tf_op jit(solution)/shard_map/dot_general | solution.py:51
  525.1 2.0 fusion.fold_ref
  527.1 2.6 maximum_select_fusion.do_ref
  529.8 49.0 %attend_backward.1 = (bf16[2048,640]{1,0:T(8,128)(2,1)S(1)}, bf16[2048,640]{1,0:T(8,128)(2,1)S(1)}, f32[2048,128]{1,0:T(8,128)S(1)}) custom-call(bf16[5,128,2048]{2,1,0:T(8,128)(2,1)S(1)} %copy-done.13, bf16[5,2048,128]{2,1,0:T(8,128)(2,1)} %copy-done.14, bf16[5,80,2048]{2,1,0:T(8,128)(2,1)S(1)} %copy-done.16, bf16[5,64,2048]{2,1,0:T(8,128)(2,1)S(1)} %copy-done.18, ...), custom_call_target="tpu_custom_call" | custom-call | flops 18874368000 | bytes 31457280 | tf_op jit(solution)/shard_map/attend_backward/pallas_call | solution.py:352
  579.8 2.3 convolution_convert_fusion.2.gkv_ref
  582.2 3.6 fusion.6.gq_ref
  585.9 108.5 %latent_backward.1 = (bf16[1024,640]{1,0:T(8,128)(2,1)}, bf16[576,640]{1,0:T(8,128)(2,1)}, bf16[160,640]{1,0:T(8,128)(2,1)}, f32[8,1024]{1,0:T(8,128)}, f32[8,12...) custom-call(bf16[2048,640]{1,0:T(8,128)(2,1)} %copy-done, bf16[2048,640]{1,0:T(8,128)(2,1)} %copy-done.1, ...), custom_call_target="tpu_custom_call" | custom-call | flops 4529848320 | bytes 209715200 | tf_op jit(solution)/shard_map/latent_backward/pallas_call | solution.py:1562
  694.5 1.6 fusion.55
  704.5 1.3 fusion.35
  706.4 1.8 multiply_subtract_fusion.6
  708.2 2.2 multiply_subtract_fusion.4
  710.4 2.6 multiply_subtract_fusion.3
  713.1 3.3 multiply_subtract_fusion.2
  716.4 2.6 multiply_subtract_fusion.5
  719.1 5.7 multiply_subtract_fusion.1
  724.8 6.7 multiply_subtract_fusion
  731.5 3.3 fusion.4
  734.8 1.1 copy.76
  (136 shorter events, 11.3 us)
Async XLA Ops:
  7.2 724.3 %reduce-scatter.2.cloned.1.call-start = ((), (), s32[]{:S(2)}) async-start(), calls=%async_computation.1 | async-start | bytes 6553600 | tf_op jit(solution)/shard_map/reduce_scatter | solution.py:1822
  10.4 6.9 copy-start.9
  10.5 6.8 copy-start.5
  145.0 61.2 %copy-start.3 = (bf16[8,128,640]{2,1,0:T(8,128)(2,1)}, bf16[8,128,640]{2,1,0:T(8,128)(2,1)S(1)}, u32[]{:S(2)}) copy-start(bf16[8,128,640]{2,1,0:T(8,128)(2,1)S(1)} %get-tuple-element.83.refs_4_.up_ref) | copy-start | bytes 3932164
  145.0 61.2 %copy-start.8 = (f32[16,1024]{1,0:T(8,128)}, f32[16,1024]{1,0:T(8,128)S(1)}, u32[]{:S(2)}) copy-start(f32[16,1024]{1,0:T(8,128)S(1)} %get-tuple-element.111.gains) | copy-start | bytes 196612
  516.5 10.6 %collective-permute-start = (bf16[320,1024]{1,0:T(8,128)(2,1)}, bf16[320,1024]{1,0:T(8,128)(2,1)}, u32[]{:S(2)}, u32[]{:S(2)}) collective-permute-start(bf16[320,1024]{1,0:T(8,128)(2,1)} %get-tuple-element.153), channel_id=1, source_target_pairs={{0,4},{4,0},{1,5},{5,1},{2,6},{6,2},{3,7},{7,3},{8,12},{12,8},{9,1... | collective-permute-start | bytes 1966088 | tf_op jit(solution)/shard_map/ppermute | solution.py:1604
  516.5 13.3 %copy-start.18 = (bf16[5,64,2048]{2,1,0:T(8,128)(2,1)S(1)}, bf16[5,64,2048]{2,1,0:T(8,128)(2,1)}, u32[]{:S(2)}) copy-start(bf16[5,64,2048]{2,1,0:T(8,128)(2,1)} %copy-done.17) | copy-start | bytes 3932164
  525.1 54.7 %slice-start.6 = ((s8[4718592]{0:T(1024)(128)(4,1)}), s8[4194304]{0:T(1024)(128)(4,1)S(1)}, s32[]{:S(2)}) async-start(s8[4718592]{0:T(1024)(128)(4,1)} %bitcast.80), calls=%async_computation.8 | async-start | bytes 8388608
  529.8 50.0 %slice-start.7 = ((s8[4718592]{0:T(1024)(128)(4,1)}), s8[524288]{0:T(1024)(128)(4,1)S(1)}, s32[]{:S(2)}) async-start(s8[4718592]{0:T(1024)(128)(4,1)} %bitcast.80), calls=%async_computation.9 | async-start | bytes 1048576
  585.9 117.6 %copy-start.39 = (f32[128]{0:T(128)S(1)}, f32[128]{0:T(128)}, u32[]{:S(2)}) copy-start(f32[128]{0:T(128)} %param.59) | copy-start | bytes 1540
  585.9 118.1 %copy-start.40 = (f32[128]{0:T(128)S(1)}, f32[128]{0:T(128)}, u32[]{:S(2)}) copy-start(f32[128]{0:T(128)} %param.50) | copy-start | bytes 1540
  585.9 118.6 %copy-start.37 = (f32[2,640]{1,0:T(2,128)S(1)}, f32[2,640]{1,0:T(2,128)}, u32[]{:S(2)}) copy-start(f32[2,640]{1,0:T(2,128)} %param.58) | copy-start | bytes 15364
  585.9 120.0 %copy-start.36 = (f32[2,640]{1,0:T(2,128)S(1)}, f32[2,640]{1,0:T(2,128)}, u32[]{:S(2)}) copy-start(f32[2,640]{1,0:T(2,128)} %param.49) | copy-start | bytes 15364
  585.9 120.6 %copy-start.33 = (f32[640,36]{0,1:T(8,128)S(1)}, f32[640,36]{0,1:T(8,128)}, u32[]{:S(2)}) copy-start(f32[640,36]{0,1:T(8,128)} %param.34) | copy-start | bytes 276484
  585.9 122.3 %copy-start.28 = (f32[640,96]{0,1:T(8,128)S(1)}, f32[640,96]{0,1:T(8,128)}, u32[]{:S(2)}) copy-start(f32[640,96]{0,1:T(8,128)} %param.33) | copy-start | bytes 737284
  585.9 122.3 %copy-start.34 = (f32[640,96]{0,1:T(8,128)S(1)}, f32[640,96]{0,1:T(8,128)}, u32[]{:S(2)}) copy-start(f32[640,96]{0,1:T(8,128)} %param.42) | copy-start | bytes 737284
  585.9 124.5 %copy-start.24 = (f32[96,960]{1,0:T(8,128)S(1)}, f32[96,960]{1,0:T(8,128)}, u32[]{:S(2)}) copy-start(f32[96,960]{1,0:T(8,128)} %param.35) | copy-start | bytes 1105924
  585.9 127.1 %copy-start.29 = (f32[640,320]{0,1:T(8,128)S(1)}, f32[640,320]{0,1:T(8,128)}, u32[]{:S(2)}) copy-start(f32[640,320]{0,1:T(8,128)} %param.46) | copy-start | bytes 2457604
  585.9 130.5 %copy-start.31 = (f32[32,1280]{1,0:T(8,128)S(1)}, f32[32,1280]{1,0:T(8,128)}, u32[]{:S(2)}) copy-start(f32[32,1280]{1,0:T(8,128)} %param.36) | copy-start | bytes 491524
  704.0 9.0 %copy-start.38 = (f32[128]{0:T(128)}, f32[128]{0:T(128)S(1)}, u32[]{:S(2)}) copy-start(f32[128]{0:T(128)S(1)} %get-tuple-element.213) | copy-start | bytes 1540
  705.8 7.2 copy-start.35
  706.4 6.6 copy-start.21
  708.2 10.8 %copy-start.23 = (f32[1600,320]{0,1:T(8,128)S(1)}, f32[1600,320]{0,1:T(8,128)}, u32[]{:S(2)}) copy-start(f32[1600,320]{0,1:T(8,128)} %param.48) | copy-start | bytes 6144004
  710.4 6.0 copy-start.30
  710.4 8.6 %copy-start.22 = (bf16[3,320,1600]{2,1,0:T(8,128)(2,1)S(1)}, bf16[3,320,1600]{2,1,0:T(8,128)(2,1)}, u32[]{:S(2)}) copy-start(bf16[3,320,1600]{2,1,0:T(8,128)(2,1)} %get-tuple-element.119) | copy-start | bytes 9216004
  713.0 6.0 copy-start.19
  713.1 11.7 %slice-start = ((s8[4259840]{0:T(1024)(128)(4,1)}), s8[4194304]{0:T(1024)(128)(4,1)S(1)}, s32[]{:S(2)}) async-start(s8[4259840]{0:T(1024)(128)(4,1)} %bitcast.66), calls=%async_computation.2 | async-start | bytes 8388608
  713.1 11.7 %slice-start.2 = ((s8[4259840]{0:T(1024)(128)(4,1)}), s8[4194304]{0:T(1024)(128)(4,1)S(1)}, s32[]{:S(2)}) async-start(s8[4259840]{0:T(1024)(128)(4,1)} %bitcast.68), calls=%async_computation.4 | async-start | bytes 8388608
  713.1 11.7 %slice-start.4 = ((s8[4259840]{0:T(1024)(128)(4,1)}), s8[4194304]{0:T(1024)(128)(4,1)S(1)}, s32[]{:S(2)}) async-start(s8[4259840]{0:T(1024)(128)(4,1)} %bitcast.70), calls=%async_computation.6 | async-start | bytes 8388608
  719.0 5.7 slice-start.1
  719.1 5.7 slice-start.3
  719.1 5.7 slice-start.5
  (20 other events, 48.6 us)
Sparse Core Ops, SparseCore 0:
  506.1 92.0 reduce-scatter.1

commit v5 on v4

--- a/solution.py
+++ b/solution.py
@@ -2,6 +2,7 @@
 
 import jax
 import jax.numpy as jnp
+import numpy as np
 from jax import lax
 from jax.experimental import pallas as pl
 from jax.experimental.pallas import tpu as pltpu
@@ -133,8 +134,8 @@
         stage, att_send, att_recv, *sems = refs
         at = h * blocks + i
         gathers = (
-            torus_gather(out_any, out_all, sems[:GATHER_SEMS], place, core),
-            torus_gather(down_any, down_all, sems[GATHER_SEMS:], place, core),
+            torus_gather(down_any, down_all, sems[:GATHER_SEMS], place, core),
+            torus_gather(out_any, out_all, sems[GATHER_SEMS:], place, core),
         )
 
         @pl.when(at == 0)
@@ -149,13 +150,9 @@
 
         for n in range(2):
 
-            @pl.when(at == 8 + 3 * n)
+            @pl.when(at == (heads * blocks * (13 + 4 * n)) // 20)
             def _():
                 gathers[n][1](0)
-
-            @pl.when(at == 15 + 3 * n)
-            def _():
-                gathers[n][2](0)
     pieces = up_ref.shape[0]
     nq, nk = QR // pieces, KVR // pieces
 
@@ -241,6 +238,8 @@
                 give(hh, core * count + b, 1 - core).wait_recv()
 
             each(heads * count, done)
+            for _, _, final, _ in gathers:
+                final(0)
             for _, _, _, drain in gathers:
                 drain(0)
 
@@ -277,7 +276,7 @@
         ]
         + more_out,
         scratch_shapes=[pltpu.VMEM((QR, 128), F32), pltpu.VMEM((KVR, 128), F32), pltpu.VMEM((128, QR), BF)] + more_scratch,
-        compiler_params=pltpu.CompilerParams(vmem_limit_bytes=40 * MIB, **params),
+        compiler_params=pltpu.CompilerParams(vmem_limit_bytes=(62 if fused else 40) * MIB, **params),
         cost_estimate=pl.CostEstimate(flops=heads * rows * rows * 320, bytes_accessed=30 * MIB, transcendentals=0),
         name="attend_forward",
     )(lat, cos, sin, segq, up, *pieces)
@@ -371,16 +370,17 @@
 
 
 LAT_LINE = 64
+LAT_DEPTH = 2
 PIECE = 160
 
 
 def latent_kernel(
     x_ref, gain_ref, gain2_ref, piece_ref, up_ref, sel_ref, freq_col, freq_lane, len_ref, gu_any,
     w_ref, total, lat_ref, cos_ref, sin_ref, segq_ref, upg_ref, tcos, tsin, gains, gu_all,
-    gat, xb, near, cross, kvg,
-    w_send, w_recv, u_send, u_recv, c_send, c_recv, *sems,
+    gat, up_all, xb, near, cross, kvg,
+    c_send, c_recv, *sems,
 ):
-    gather_sems, sems = sems[6:], sems[:6]
+    gather_sems, w_sems, u_sems, sems = sems[40:], sems[6:23], sems[23:40], sems[:6]
     z, core, place = lax.axis_index("tp"), lax.axis_index("ctx"), lax.axis_index("fsdp")
     is_end, is_mid, partner, across = line_places(z)
     to_mid, over, to_end, first, second = line_copies(xb, near, cross, total, sems, partner, across, LAT_LINE)
@@ -394,39 +394,24 @@
             src_ref=src, dst_ref=dst, send_sem=send, recv_sem=recv, device_id=to, device_id_type=MESH
         )
 
-    def peer(d):
-        to = lax.rem(me + d, peers)
-        return {"fsdp": to // 2, "ctx": lax.rem(to, 2)}
-
+    y, x = place // 2, place % 2
     barrier = pltpu.get_barrier_semaphore()
-    for d in range(1, peers):
-        pl.semaphore_signal(barrier, inc=1, device_id=peer(d), device_id_type=MESH)
-    pl.semaphore_signal(barrier, inc=1, device_id={"tp": partner}, device_id_type=MESH)
+    for to in ({"ctx": 1 - core}, {"fsdp": y * 2 + 1 - x}, {"fsdp": (1 - y) * 2 + x}, {"tp": partner}):
+        pl.semaphore_signal(barrier, inc=1, device_id=to, device_id_type=MESH)
 
     @pl.when(is_mid)
     def _():
         pl.semaphore_signal(barrier, inc=1, device_id={"tp": across}, device_id_type=MESH)
-        pl.semaphore_wait(barrier, peers + 1)
+        pl.semaphore_wait(barrier, 5)
 
     @pl.when(is_end)
     def _():
-        pl.semaphore_wait(barrier, peers)
-
-    def w_copy(d, source):
-        return remote(piece_ref, gat.at[source], w_send.at[d], w_recv.at[source], peer(d))
-
-    def u_copy(d, source):
-        return remote(up_ref.at[lax.rem(me + d, 2)], upg_ref.at[source], u_send.at[d], u_recv.at[source], peer(d))
+        pl.semaphore_wait(barrier, 4)
 
     begin, forward, final, drain = torus_gather(gu_any, gu_all, gather_sems, place, core)
-    for d in range(1, peers):
-        w_copy(d, me).start()
-    begin(0)
-    for d in range(1, peers):
-        u_copy(d, me).start()
-    begin(1)
-    gat[me] = piece_ref[...]
-    upg_ref[me] = up_ref[core]
+    begin_w, forward_w, final_w, drain_w = torus_gather(piece_ref, gat, w_sems, place, core)
+    begin_u, forward_u, final_u, drain_u = torus_gather(up_ref, up_all, u_sems, place, core)
+    begin_w(0)
 
     length = len_ref[0, 0]
     slot = cos_ref.shape[1]
@@ -455,12 +440,16 @@
 
     each(rows // LAT_LINE, table)
 
-    for d in range(1, peers):
-        w_copy(d, lax.rem(me + peers - d, peers)).wait_recv()
+    forward_w(0)
+    begin_u(0)
+    begin(0)
+    begin(1)
+    final_w(0)
+    drain_w(0)
     for p in range(peers):
-        w_ref[p * 96 : (p + 1) * 96, :] = gat[p, 0:96, :]
-        kvg[p * 48 : (p + 1) * 48, :] = gat[p, 96:144, :]
-        gains[:, p * 128 : (p + 1) * 128] = gat[p, 144:160, 0:128].astype(F32)
+        w_ref[p * 96 : (p + 1) * 96, :] = gat[p, 0, 0:96, :]
+        kvg[p * 48 : (p + 1) * 48, :] = gat[p, 0, 96:144, :]
+        gains[:, p * 128 : (p + 1) * 128] = gat[p, 0, 144:160, 0:128].astype(F32)
     w_ref[QR:LAT, :] = dot_nn(sel_ref[...], kvg[...]).astype(BF)
     w_ref[LAT:LAT_WIDE, :] = jnp.zeros((LAT_WIDE - LAT, w_ref.shape[1]), BF)
 
@@ -520,10 +509,10 @@
         def _():
             first(n)
 
-        @pl.when(jnp.logical_and(is_mid, jnp.logical_and(n >= DEPTH, n < count + DEPTH)))
-        def _():
-            second(n - DEPTH)
-            finish_rows(n - DEPTH)
+        @pl.when(jnp.logical_and(is_mid, jnp.logical_and(n >= LAT_DEPTH, n < count + LAT_DEPTH)))
+        def _():
+            second(n - LAT_DEPTH)
+            finish_rows(n - LAT_DEPTH)
 
         @pl.when(jnp.logical_and(is_end, n < count))
         def _():
@@ -531,11 +520,17 @@
             to_end(n).wait_recv()
             finish_rows(n)
 
-    each(7, serve)
+    each(2, serve)
+    forward_u(0)
+    each(4, lambda n: serve(n + 2))
     forward(0)
-    each(4, lambda n: serve(n + 7))
+    each(4, lambda n: serve(n + 6))
     forward(1)
-    each(count + DEPTH - 11, lambda n: serve(n + 11))
+    final_u(0)
+    each(count + LAT_DEPTH - 10, lambda n: serve(n + 10))
+    drain_u(0)
+    for p in range(peers):
+        upg_ref[p] = up_all[p, 0, pl.ds(pl.multiple_of(core * 128, 128), 128), :]
     final(0)
     final(1)
 
@@ -549,10 +544,6 @@
 
     drain(0)
     drain(1)
-    for d in range(1, peers):
-        w_copy(d, me).wait_send()
-        u_copy(d, me).wait_send()
-        u_copy(d, lax.rem(me + peers - d, peers)).wait_recv()
 
     def passed(e):
         handover(e).wait_send()
@@ -563,8 +554,8 @@
 
 
 def spread(peers):
-    index = jnp.arange(KVR + ROPE)
-    return jnp.equal((index // 36 * 48 + index % 36)[:, None], jnp.arange(peers * 48)[None]).astype(BF)
+    index = np.arange(KVR + ROPE)
+    return jnp.asarray((index // 36 * 48 + index % 36)[:, None] == np.arange(peers * 48)[None], BF)
 
 
 def latent_forward(x, gain, gain2, piece, up, length, gate_up):
@@ -574,7 +565,7 @@
     wide = rows + LAT_LINE
     count = wide // LAT_LINE
     sel = spread(peers)
-    frequency = ROPE_BASE ** (-2.0 * jnp.arange(ROPE // 2, dtype=F32) / ROPE)
+    frequency = (ROPE_BASE ** (-2.0 * np.arange(ROPE // 2) / ROPE)).astype(np.float32)
     vmem = pl.BlockSpec(memory_space=pltpu.VMEM)
     dma = pltpu.SemaphoreType.DMA
     return pl.pallas_call(
@@ -586,7 +577,7 @@
             jax.ShapeDtypeStruct((ROPE // 2, slot), F32),
             jax.ShapeDtypeStruct((ROPE // 2, slot), F32),
             jax.ShapeDtypeStruct((16, slot), BF),
-            jax.ShapeDtypeStruct((peers,) + up.shape[1:], BF),
+            jax.ShapeDtypeStruct((peers, up.shape[1] // 2, up.shape[2]), BF),
             jax.ShapeDtypeStruct((rows, 128), F32),
             jax.ShapeDtypeStruct((rows, 128), F32),
             jax.ShapeDtypeStruct((16, QR + KVR), F32),
@@ -595,20 +586,21 @@
         in_specs=[vmem] * 8 + [pl.BlockSpec(memory_space=pltpu.SMEM), pl.BlockSpec(memory_space=pl.ANY)],
         out_specs=[vmem] * 10 + [pl.BlockSpec(memory_space=pl.ANY)],
         scratch_shapes=[
-            pltpu.VMEM((peers, PIECE, width), BF),
+            pltpu.VMEM((peers, 1, PIECE, width), BF),
+            pltpu.VMEM((peers,) + up.shape, BF),
             pltpu.VMEM((wide, LAT_WIDE), BF),
             pltpu.VMEM((wide, LAT_WIDE), BF),
             pltpu.VMEM((wide, LAT_WIDE), BF),
             pltpu.VMEM((peers * 48, width), BF),
         ]
-        + [dma((peers,))] * 4
         + [dma((rows // LAT_LINE,))] * 2
         + [dma((count,))] * 6
+        + [dma((1,))] * (2 * GATHER_SEMS)
         + [dma((2,))] * GATHER_SEMS,
-        compiler_params=pltpu.CompilerParams(collective_id=0, has_side_effects=True, vmem_limit_bytes=48 * MIB),
+        compiler_params=pltpu.CompilerParams(collective_id=0, has_side_effects=True, vmem_limit_bytes=62 * MIB),
         cost_estimate=pl.CostEstimate(flops=rows * LAT_WIDE * width * 2, bytes_accessed=150 * MIB, transcendentals=0),
         name="latent_forward",
-    )(x, gain, gain2, piece, up, sel, frequency[:, None], jnp.tile(frequency, 8)[None], length, gate_up)
+    )(x, gain, gain2, piece, up, sel, jnp.asarray(frequency[:, None]), jnp.asarray(np.tile(frequency, 8)[None]), length, gate_up)
 
 
 LINE = 16
@@ -1298,7 +1290,7 @@
 
 def latent_back_kernel(
     dq_ref, de_ref, dkr_ref, up_ref, sum_ref, w_ref, x_ref, gain_ref, dh_ref, tcos, tsin, gains, gout_ref, gq_ref, gkv_ref,
-    sel_ref, b2_ref, square_ref, fold_ref,
+    sel_ref, b2_ref, square_ref, limit_ref, fold_ref,
     gin_ref, pack_out, wd_out, small_out, scalar_out, gq_out, gkv_out,
     uq, ukv, away, arrived, xb, near, cross, total, dl, dlt, xg, weight, w_pack, small, small_in, scal_in,
     s1, cin, xin, yin2, yin, xin2, s1w, cinw, xinw, yin2w, yinw, xin2w,
@@ -1440,16 +1432,16 @@
         def _():
             first(n)
 
-        @pl.when(jnp.logical_and(is_mid, jnp.logical_and(n >= DEPTH, n < count + DEPTH)))
-        def _():
-            second(n - DEPTH)
-            finish_rows(n - DEPTH)
-
-        @pl.when(jnp.logical_and(is_end, jnp.logical_and(n >= 4, n < count + 4)))
-        def _():
-            to_mid(n - 4).wait_send()
-            to_end(n - 4).wait_recv()
-            finish_rows(n - 4)
+        @pl.when(jnp.logical_and(is_mid, jnp.logical_and(n >= LAT_DEPTH, n < count + LAT_DEPTH)))
+        def _():
+            second(n - LAT_DEPTH)
+            finish_rows(n - LAT_DEPTH)
+
+        @pl.when(jnp.logical_and(is_end, jnp.logical_and(n >= 3, n < count + 3)))
+        def _():
+            to_mid(n - 3).wait_send()
+            to_end(n - 3).wait_recv()
+            finish_rows(n - 3)
 
     begin, middle, last, drain = torus(s1, xin, yin2, yin, xin2, pack_sems, x, y, to_x, to_y)
     begin_w, middle_w, last_w, drain_w = torus(s1w, xinw, yin2w, yinw, xin2w, w_sems, x, y, to_x, to_y)
@@ -1471,7 +1463,7 @@
     gq_out[...] = dot_nn(pack_out[320:416, :], fold_ref[0:lanes, :]) + dot_nn(pack_out[416:512, :], fold_ref[lanes:, :])
     gkv_out[:, 0:lanes] = pack_out[512:544, :].astype(F32)
     gkv_out[:, lanes : 2 * lanes] = pack_out[544:576, :].astype(F32)
-    each(count + 4 - 11, lambda n: serve(n + 11))
+    each(count + 3 - 11, lambda n: serve(n + 11))
 
     both = dot_nn(dlt[0:QR, :], xg[...])
     for p in range(peers):
@@ -1524,7 +1516,8 @@
     for d in range(1, 4):
         scal_copy(d, lax.rem(z + 4 - d, 4)).wait_recv()
     scalars = (scal_in[0] + scal_in[1]) + (scal_in[2] + scal_in[3])
-    scalar_out[...] = jnp.where(lane == 8, total_square(whole[0:1]), scalars)
+    scalars = jnp.where(lane == 8, total_square(whole[0:1]), scalars)
+    scalar_out[...] = limit_ref[...] / jnp.maximum(jnp.sqrt(scalars), limit_ref[...])
 
     for d in range(1, peers):
         small_copy(d, me).wait_send()
@@ -1710,10 +1703,10 @@
             ],
             axis=0,
         )
-        up_pair = jnp.stack([up_shard[:, : heads * 128], up_shard[:, heads * 128 :]])
+        up_pair = jnp.concatenate([up_shard[:, : heads * 128], up_shard[:, heads * 128 :]])[None]
         gain_wide = jnp.pad(gains_norm[1].astype(F32), (0, LAT_WIDE - width))[None]
         down_t, lat_sum, lat_all, cos_t, sin_t, seg_q, up, tcos, tsin, gains_lat, gate_up = latent_forward(
-            tokens, gain_attn[None], gain_wide, piece, up_pair, lengths, w_gateup.astype(BF)
+            tokens, gain_attn[None], gain_wide, piece[None], up_pair, lengths, w_gateup.astype(BF)
         )
         gain_mlp = lat_sum[rows : rows + n_tp, :width].reshape(D).astype(F32)
     else:
@@ -1840,17 +1833,25 @@
     def heads_only(g):
         return g.reshape(g.shape[0], heads_all, 128)[:, :, :HEAD].reshape(g.shape[0], heads_all * HEAD)
 
+    entry_counts = (
+        D * QR,
+        D * (KVR + ROPE),
+        QR * H * HEAD,
+        KVR * H * (NOPE + VD),
+        H * VD * D,
+        2 * D * FF,
+        FF * D,
+        2 * D,
+        QR + KVR,
+    )
+    limits = [CLIP_RMS * n**0.5 for n in entry_counts]
     share = g_latent.shape[0]
     my_share = (lax.axis_index("fsdp") * n_ctx + core) * share
     if fused:
-        head_row = jnp.arange(heads_all * 128)
-        fold = jnp.equal(
-            jnp.where(head_row % 128 < HEAD, head_row // 128 * HEAD + head_row % 128, -1)[:, None],
-            jnp.arange(heads_all * HEAD)[None],
-        ).astype(BF)
+        fold = jnp.asarray(np.kron(np.eye(heads_all), np.eye(128, HEAD)), BF)
         grad_input, pack, wd_grad, small, scalars, grad_qup, grad_kvup = latent_backward(
             d_q, d_e, d_kr, up, lat_sum, down_t, tokens, gain_attn[None], d_hidden, tcos, tsin, gains_lat,
-            grad_out, grad_qup, grad_kvup, spread(n_fsdp * n_ctx), grad_gain_mlp, grad_squares, fold,
+            grad_out, grad_qup, grad_kvup, spread(n_fsdp * n_ctx), grad_gain_mlp, grad_squares, jnp.array([limits + [1.0] * 119], F32), fold,
         )
         owned = [
             wd_grad[:96].astype(F32).T,
@@ -1863,7 +1864,7 @@
             small[1:3, :width],
             lax.dynamic_slice_in_dim(small[0], my_share, share, 0),
         ]
-        totals = [scalars[0, n] for n in range(9)]
+        factors = [scalars[0, n] for n in range(9)]
     else:
         q_up_here = up[:, : w_qup.shape[0]].reshape(QR, heads * 128)
         kv_up_here = up[:, w_qup.shape[0] :].reshape(KVR, heads * 128)
@@ -1914,21 +1915,10 @@
         owned.append(lax.dynamic_slice_in_dim(all_latent, my_share, share, 0))
         totals = [small[2 * D + QR + KVR + n] for n in range(7)]
         totals += [jnp.sum(all_gains * all_gains), jnp.sum(all_latent * all_latent)]
-    entry_counts = (
-        D * QR,
-        D * (KVR + ROPE),
-        QR * H * HEAD,
-        KVR * H * (NOPE + VD),
-        H * VD * D,
-        2 * D * FF,
-        FF * D,
-        2 * D,
-        QR + KVR,
-    )
+        factors = [limit / jnp.maximum(jnp.sqrt(total), limit) for limit, total in zip(limits, totals)]
     new_params, new_firsts, new_seconds = [], [], []
     for n in range(9):
-        limit = CLIP_RMS * entry_counts[n] ** 0.5
-        clipped = owned[n] * (limit / jnp.maximum(jnp.sqrt(totals[n]), limit))
+        clipped = owned[n] * factors[n]
         updated, first_new, second_new = adamw_update(
             params[n], clipped, firsts[n], seconds[n], WEIGHT_DECAY if n < 7 else 0.0
         )

time: 753 us -> 722 us (0.959)
  Pallas kernels: 636 us -> 616 us
  local copies, waits for them, and re-layouts: 18.5 us -> 9.97 us
    pallas_call x1, Pallas kernels: 126 us -> 111 us  [latent_forward(): pl.pallas_call(latent_kernel, out_shape=[jax.ShapeDtypeStruct((LAT_WIDE,...]
  transfers between devices with their start and end apart: 2 -> 2, of which waited for: 0 -> 0; matrix products, arithmetic and copies ran while one was open for 8% -> 8% of each run, Pallas kernels for 21% -> 22%
where the time goes in v5:
time: 722 us; the launch traced here: 713 us
  Pallas kernels  616 us (85%)
  other arithmetic  49.3 us (7%)
  matrix products  22.1 us (3%)
  between operations  15.4 us (2%)
  local copies, waits for them, and re-layouts  9.97 us (1%)
    pallas_call x1, Pallas kernels, block_forward(): pl.pallas_call(block_kernel, out_shape=[wide, wide, jax.ShapeDtypeStruct(...  158 us
    pallas_call x1, Pallas kernels, grad_reduce(): pl.pallas_call(grad_kernel, out_shape=[jax.ShapeDtypeStruct((rows, D), BF...  135 us
    pallas_call x1, Pallas kernels, latent_forward(): pl.pallas_call(latent_kernel, out_shape=[jax.ShapeDtypeStruct((LAT_WIDE,...  111 us
    pallas_call x1, Pallas kernels, latent_backward(): pl.pallas_call(latent_back_kernel, out_shape=[jax.ShapeDtypeStruct((rows,...  107 us
    pallas_call x1, Pallas kernels, attend_forward(): pl.pallas_call(functools.partial(attend_forward_kernel, fused), grid=(hea...  56.8 us
    pallas_call x1, Pallas kernels, attend_backward(): pl.pallas_call(attend_backward_kernel, grid=(heads, rows // BQ), in_specs...  48.9 us
    sub x7, other arithmetic, adamw_update(): parameter - LEARN_RATE * (first_hat / (jnp.sqrt(second_hat) + ADAM_EPS) +...  29.6 us
    dot_general x3, matrix products, dot_tn(): lax.dot_general(a, b, (((0,), (0,)), ((), ())), preferred_element_type=F32)  15 us
  transfers between devices with their start and end apart: 2, of which 0 were waited for; matrix products, arithmetic and copies ran while one was open for 8% of the time, Pallas kernels for 22%

profile of v5, /device:TPU:0, one launch (start us, length us, event | category | flops | bytes accessed | tf_op | source)
XLA Modules:
  0.0 713.4 jit_solution(10868920365595029471)
XLA Ops:
  7.3 1.2 copy.74
  8.7 0.9 convert_element_type.129
  12.3 3.9 convert_element_type.130.gu_any
  16.3 1.1 convert_bitcast_fusion.1.refs_5_
  17.5 0.8 convert_bitcast_fusion.3.refs_6_
  19.0 111.3 %latent_forward.1 = (bf16[1152,640]{1,0:T(8,128)(2,1)}, bf16[1088,1152]{1,0:T(8,128)(2,1)}, bf16[2048,1152]{1,0:T(8,128)(2,1)}, f32[16,2048]{1,0:T(8,128)}, f32[...) custom-call(bf16[1024,640]{1,0:T(8,128)(2,1)} %x_ref.5, ...), custom_call_target="tpu_custom_call" | custom-call | flops 1509949440 | bytes 157286400 | tf_op jit(solution)/shard_map/latent_forward/pallas_call | solution.py:571
  131.6 0.9 fusion.10.live_ref
  132.4 56.8 %attend_forward.1 = (bf16[5,64,2048]{2,1,0:T(8,128)(2,1)}, f32[5,1,2048]{2,1,0:T(1,128)}, bf16[5,128,2048]{2,1,0:T(8,128)(2,1)}, bf16[5,2048,128]{2,1,0:T(8,128)...) custom-call(bf16[2048,1152]{1,0:T(8,128)(2,1)} %get-tuple-element.79, ...), custom_call_target="tpu_custom_call" | custom-call | flops 6710886400 | bytes 31457280 | tf_op jit(solution)/shard_map/attend_forward/pallas_call | solution.py:262
  189.2 157.8 %block_forward.1 = (bf16[1024,2560]{1,0:T(8,128)(2,1)}, bf16[1024,2560]{1,0:T(8,128)(2,1)}, bf16[4,1024,640]{2,1,0:T(8,128)(2,1)}, bf16[2560,1024]{1,0:T(8,128)(...) custom-call(bf16[640,1024]{1,0:T(8,128)(2,1)} %get-tuple-element.84.att_ref, ...), custom_call_target="tpu_custom_call" | custom-call | flops 50331648000 | bytes 419430400 | tf_op jit(solution)/shard_map/block_forward/pallas_call | solution.py:865
  347.0 134.8 %grad_reduce.1 = (bf16[1024,2560]{1,0:T(8,128)(2,1)}, f32[1024,640]{1,0:T(8,128)}, f32[1,640]{1,0:T(1,128)}, bf16[3,320,1600]{2,1,0:T(8,128)(2,1)}, f32[8,128]{1,0:T(8,128)}) custom-call(f32[1024,1]{1,0:T(8,128)} %fusion.10.live_ref, f32[1,2560]{1,0:T(1,128)} %bitcast.77, bf16[1024,2560]{1,0:T(8,128)(2,1)} %get-tuple-element.91.dnp_any, ...), custom_call_target="tpu_custom_call" | custom-call | flops 25165824000 | bytes 419430400 | tf_op jit(solution)/shard_map/grad_reduce/pallas_call | solution.py:1196
  481.9 7.1 convolution_convert_fusion.1
  489.2 9.0 %convolution_convert_fusion.gout_ref = bf16[2560,640]{1,0:T(8,128)(2,1)} fusion(bf16[1024,2560]{1,0:T(8,128)(2,1)} %get-tuple-element.102, bf16[640,1024]{1,0:T(8,128)(2,1)} %get-tuple-element.84.att_ref), kind=kOutput, calls=%fused_computation.1 | convolution fusion | flops 3357081600 | bytes 9830400 | tf_op jit(solution)/shard_map/dot_general | solution.py:52
  499.8 48.9 %attend_backward.1 = (bf16[2048,640]{1,0:T(8,128)(2,1)S(1)}, bf16[2048,640]{1,0:T(8,128)(2,1)S(1)}, f32[2048,128]{1,0:T(8,128)S(1)}) custom-call(bf16[5,128,2048]{2,1,0:T(8,128)(2,1)S(1)} %copy-done.5, bf16[5,2048,128]{2,1,0:T(8,128)(2,1)} %get-tuple-element.99.k_ref, bf16[5,80,2048]{2,1,0:T(8,128)(2,1)S(1)} %copy-done.6, ...), custom_call_target="tpu_custom_call" | custom-call | flops 18874368000 | bytes 31457280 | tf_op jit(solution)/shard_map/attend_backward/pallas_call | solution.py:351
  548.7 1.0 copy-done.2
  549.7 2.4 convolution_convert_fusion.2.gkv_ref
  552.2 3.6 fusion.5.gq_ref
  555.9 106.8 %latent_backward.1 = (bf16[1024,640]{1,0:T(8,128)(2,1)}, bf16[576,640]{1,0:T(8,128)(2,1)}, bf16[160,640]{1,0:T(8,128)(2,1)}, f32[8,1024]{1,0:T(8,128)}, f32[8,12...) custom-call(bf16[2048,640]{1,0:T(8,128)(2,1)} %copy-done, bf16[2048,640]{1,0:T(8,128)(2,1)} %copy-done.1, ...), custom_call_target="tpu_custom_call" | custom-call | flops 4529848320 | bytes 209715200 | tf_op jit(solution)/shard_map/latent_backward/pallas_call | solution.py:1555
  662.7 0.8 slice.82
  663.5 1.6 fusion.34
  665.1 1.2 fusion.24
  666.3 1.2 multiply_add_fusion.8
  667.5 2.0 fusion.23
  669.4 1.2 multiply_add_fusion.7
  670.7 2.4 multiply_subtract_fusion.6
  673.1 3.0 multiply_subtract_fusion.4
  676.1 3.1 multiply_subtract_fusion.3
  679.3 4.6 multiply_subtract_fusion.2
  683.9 2.5 multiply_subtract_fusion.5
  686.4 6.8 multiply_subtract_fusion.1
  693.2 7.3 %multiply_subtract_fusion = (f32[2,320,1600]{2,1,0:T(8,128)}, f32[2,320,1600]{2,1,0:T(8,128)}, f32[2,320,1600]{2,1,0:T(8,128)}, f32[2,320,1600]{2,1,0:T(8,128)}) fusion(f32[2,320,1600]{2,1,0:T(8,128)S(1)} %bitcast.67, f32[]{:T(128)} %bitcast.27, f32[2,320,1600]{2,1,0:T(8,128)S(1)} %bitcast.69, f32[2,320,1600]{2,1,0:T(8,128)S(1)} %bitcast.71, ...), kind=kLoop, calls=%fused_computation.3 | loop fusion | flops 17408000 | bytes 30720004 | tf_op jit(solution)/shard_map/sub | solution.py:1658
  700.5 3.3 fusion.3
  703.8 1.1 copy.82
  (106 shorter events, 7.7 us)
Async XLA Ops:
  7.2 693.3 %reduce-scatter.2.cloned.1.call-start = ((), (), s32[]{:S(2)}) async-start(), calls=%async_computation.1 | async-start | bytes 6553600 | tf_op jit(solution)/shard_map/reduce_scatter | solution.py:1815
  12.3 4.0 copy-start.17
  12.3 4.0 copy-start.21
  12.3 4.0 copy-start.30
  12.3 4.0 copy-start.9
  489.1 9.2 %collective-permute-start = (bf16[320,1024]{1,0:T(8,128)(2,1)S(1)}, bf16[320,1024]{1,0:T(8,128)(2,1)S(1)}, u32[]{:S(2)}, u32[]{:S(2)}) collective-permute-start(bf16[320,1024]{1,0:T(8,128)(2,1)S(1)} %get-tuple-element.153), channel_id=1, source_target_pairs={{0,4},{4,0},{1,5},{5,1},{2,6},{6,2},{3,7},{7,3},{8,12},{12,8},{9,1... | collective-permute-start | bytes 1966088 | tf_op jit(solution)/shard_map/ppermute | solution.py:1597
  489.2 9.5 %copy-start.5 = (bf16[5,128,2048]{2,1,0:T(8,128)(2,1)S(1)}, bf16[5,128,2048]{2,1,0:T(8,128)(2,1)}, u32[]{:S(2)}) copy-start(bf16[5,128,2048]{2,1,0:T(8,128)(2,1)} %get-tuple-element.98.q_ref) | copy-start | bytes 7864324
  489.2 9.5 %copy-start.7 = (bf16[5,64,2048]{2,1,0:T(8,128)(2,1)S(1)}, bf16[5,64,2048]{2,1,0:T(8,128)(2,1)}, u32[]{:S(2)}) copy-start(bf16[5,64,2048]{2,1,0:T(8,128)(2,1)} %get-tuple-element.101.o_ref) | copy-start | bytes 3932164
  489.2 60.5 %slice-start.6 = ((s8[4718592]{0:T(1024)(128)(4,1)}), s8[4194304]{0:T(1024)(128)(4,1)S(1)}, s32[]{:S(2)}) async-start(s8[4718592]{0:T(1024)(128)(4,1)} %bitcast.81), calls=%async_computation.8 | async-start | bytes 8388608
  499.8 49.9 %slice-start.7 = ((s8[4718592]{0:T(1024)(128)(4,1)}), s8[524288]{0:T(1024)(128)(4,1)S(1)}, s32[]{:S(2)}) async-start(s8[4718592]{0:T(1024)(128)(4,1)} %bitcast.81), calls=%async_computation.9 | async-start | bytes 1048576
  555.8 109.3 %copy-start.28 = (f32[128]{0:T(128)S(1)}, f32[128]{0:T(128)}, u32[]{:S(2)}) copy-start(f32[128]{0:T(128)} %param.65) | copy-start | bytes 1540
  555.8 110.5 %copy-start.29 = (f32[128]{0:T(128)S(1)}, f32[128]{0:T(128)}, u32[]{:S(2)}) copy-start(f32[128]{0:T(128)} %param.56) | copy-start | bytes 1540
  555.8 111.7 %copy-start.26 = (f32[2,640]{1,0:T(2,128)S(1)}, f32[2,640]{1,0:T(2,128)}, u32[]{:S(2)}) copy-start(f32[2,640]{1,0:T(2,128)} %param.64) | copy-start | bytes 15364
  555.8 113.6 %copy-start.24 = (f32[2,640]{1,0:T(2,128)S(1)}, f32[2,640]{1,0:T(2,128)}, u32[]{:S(2)}) copy-start(f32[2,640]{1,0:T(2,128)} %param.55) | copy-start | bytes 15364
  555.8 117.3 %copy-start.18 = (f32[640,96]{0,1:T(8,128)S(1)}, f32[640,96]{0,1:T(8,128)}, u32[]{:S(2)}) copy-start(f32[640,96]{0,1:T(8,128)} %param.39) | copy-start | bytes 737284
  555.8 117.3 %copy-start.22 = (f32[640,96]{0,1:T(8,128)S(1)}, f32[640,96]{0,1:T(8,128)}, u32[]{:S(2)}) copy-start(f32[640,96]{0,1:T(8,128)} %param.48) | copy-start | bytes 737284
  555.8 137.3 %slice-start.4 = ((s8[4259840]{0:T(1024)(128)(4,1)}), s8[65536]{0:T(1024)(128)(4,1)S(1)}, s32[]{:S(2)}) async-start(s8[4259840]{0:T(1024)(128)(4,1)} %bitcast.70), calls=%async_computation.6 | async-start | bytes 131072
  662.6 13.4 %copy-start.14 = (f32[96,960]{1,0:T(8,128)S(1)}, f32[96,960]{1,0:T(8,128)}, u32[]{:S(2)}) copy-start(f32[96,960]{1,0:T(8,128)} %param.41) | copy-start | bytes 1105924
  662.7 13.4 %copy-start.15 = (f32[96,960]{1,0:T(8,128)S(1)}, f32[96,960]{1,0:T(8,128)}, u32[]{:S(2)}) copy-start(f32[96,960]{1,0:T(8,128)} %get-tuple-element.205) | copy-start | bytes 1105924
  666.3 12.9 %copy-start.27 = (f32[128]{0:T(128)}, f32[128]{0:T(128)S(1)}, u32[]{:S(2)}) copy-start(f32[128]{0:T(128)S(1)} %get-tuple-element.211) | copy-start | bytes 1540
  669.4 9.8 %copy-start.23 = (f32[2,640]{1,0:T(2,128)}, f32[2,640]{1,0:T(2,128)S(1)}, u32[]{:S(2)}) copy-start(f32[2,640]{1,0:T(2,128)S(1)} %get-tuple-element.210) | copy-start | bytes 15364
  670.7 13.2 %copy-start.20 = (f32[32,1280]{1,0:T(8,128)S(1)}, f32[32,1280]{1,0:T(8,128)}, u32[]{:S(2)}) copy-start(f32[32,1280]{1,0:T(8,128)} %param.42) | copy-start | bytes 491524
  673.1 20.1 %slice-start.5 = ((s8[4259840]{0:T(1024)(128)(4,1)}), s8[4194304]{0:T(1024)(128)(4,1)S(1)}, s32[]{:S(2)}) async-start(s8[4259840]{0:T(1024)(128)(4,1)} %bitcast.70), calls=%async_computation.7 | async-start | bytes 8388608
  676.1 7.8 %copy-start.19 = (f32[32,1280]{1,0:T(8,128)S(1)}, f32[32,1280]{1,0:T(8,128)}, u32[]{:S(2)}) copy-start(f32[32,1280]{1,0:T(8,128)} %get-tuple-element.206) | copy-start | bytes 491524
  676.1 10.3 %copy-start.13 = (f32[1600,320]{0,1:T(8,128)S(1)}, f32[1600,320]{0,1:T(8,128)}, u32[]{:S(2)}) copy-start(f32[1600,320]{0,1:T(8,128)} %param.54) | copy-start | bytes 6144004
  679.2 7.1 copy-start.10
  679.2 7.1 %copy-start.12 = (bf16[3,320,1600]{2,1,0:T(8,128)(2,1)S(1)}, bf16[3,320,1600]{2,1,0:T(8,128)(2,1)}, u32[]{:S(2)}) copy-start(bf16[3,320,1600]{2,1,0:T(8,128)(2,1)} %get-tuple-element.119) | copy-start | bytes 9216004
  686.4 6.8 slice-start
  686.4 6.8 slice-start.2
  686.4 6.8 slice-start.1
  686.4 6.8 slice-start.3
  700.5 3.3 copy-start.16
  (9 other events, 15.3 us)
Sparse Core Ops, SparseCore 0:
  482.0 92.7 reduce-scatter.1

commit v6 on v5

--- a/solution.py
+++ b/solution.py
@@ -1059,7 +1059,7 @@
     save_lower = lambda i: local(xin2.at[i], grad_any.at[i, lower], out_sem.at[i, 1])
 
     def plus(a, b):
-        return (a.astype(F32) + b.astype(F32)).astype(BF)
+        return a + b
 
     def products(i, n0):
         def for_other(j):
@@ -1247,7 +1247,7 @@
         )
 
     def plus(a, b):
-        return (a.astype(F32) + b.astype(F32)).astype(BF)
+        return a + b
 
     x_copy = lambda v: remote(s1.at[v * 2 + 1 - x, upper], xin.at[v], x_send.at[v], x_recv.at[v], to_x)
     y2_copy = lambda v: remote(s1.at[(1 - y) * 2 + v, lower], yin2.at[v], y2_send.at[v], y2_recv.at[v], to_y)

time: 722 us -> 726 us (level)
    pallas_call x1, Pallas kernels: 158 us -> 165 us  [block_forward(): pl.pallas_call(block_kernel, out_shape=[wide, wide, jax.ShapeDtypeStruct(...]
where the time goes in v6:
time: 726 us; the launch traced here: 721 us
  Pallas kernels  623 us (86%)
  other arithmetic  49.5 us (7%)
  matrix products  22.1 us (3%)
  between operations  15.4 us (2%)
  local copies, waits for them, and re-layouts  10 us (1%)
    pallas_call x1, Pallas kernels, block_forward(): pl.pallas_call(block_kernel, out_shape=[wide, wide, jax.ShapeDtypeStruct(...  165 us
    pallas_call x1, Pallas kernels, grad_reduce(): pl.pallas_call(grad_kernel, out_shape=[jax.ShapeDtypeStruct((rows, D), BF...  135 us
    pallas_call x1, Pallas kernels, latent_forward(): pl.pallas_call(latent_kernel, out_shape=[jax.ShapeDtypeStruct((LAT_WIDE,...  111 us
    pallas_call x1, Pallas kernels, latent_backward(): pl.pallas_call(latent_back_kernel, out_shape=[jax.ShapeDtypeStruct((rows,...  107 us
    pallas_call x1, Pallas kernels, attend_forward(): pl.pallas_call(functools.partial(attend_forward_kernel, fused), grid=(hea...  56.8 us
    pallas_call x1, Pallas kernels, attend_backward(): pl.pallas_call(attend_backward_kernel, grid=(heads, rows // BQ), in_specs...  48.9 us
    sub x7, other arithmetic, adamw_update(): parameter - LEARN_RATE * (first_hat / (jnp.sqrt(second_hat) + ADAM_EPS) +...  29.9 us
    dot_general x3, matrix products, dot_tn(): lax.dot_general(a, b, (((0,), (0,)), ((), ())), preferred_element_type=F32)  15 us
  transfers between devices with their start and end apart: 2, of which 0 were waited for; matrix products, arithmetic and copies ran while one was open for 8% of the time, Pallas kernels for 22%

profile of v6, /device:TPU:0, one launch (start us, length us, event | category | flops | bytes accessed | tf_op | source)
XLA Modules:
  0.0 720.7 jit_solution(17677457000764961895)
XLA Ops:
  7.3 1.2 copy.74
  8.7 0.9 convert_element_type.129
  12.3 3.9 convert_element_type.130.gu_any
  16.3 1.1 convert_bitcast_fusion.1.refs_5_
  17.5 0.8 convert_bitcast_fusion.3.refs_6_
  19.0 111.3 %latent_forward.1 = (bf16[1152,640]{1,0:T(8,128)(2,1)}, bf16[1088,1152]{1,0:T(8,128)(2,1)}, bf16[2048,1152]{1,0:T(8,128)(2,1)}, f32[16,2048]{1,0:T(8,128)}, f32[...) custom-call(bf16[1024,640]{1,0:T(8,128)(2,1)} %x_ref.5, ...), custom_call_target="tpu_custom_call" | custom-call | flops 1509949440 | bytes 157286400 | tf_op jit(solution)/shard_map/latent_forward/pallas_call | solution.py:571
  131.6 0.9 fusion.10.live_ref
  132.4 56.8 %attend_forward.1 = (bf16[5,64,2048]{2,1,0:T(8,128)(2,1)}, f32[5,1,2048]{2,1,0:T(1,128)}, bf16[5,128,2048]{2,1,0:T(8,128)(2,1)}, bf16[5,2048,128]{2,1,0:T(8,128)...) custom-call(bf16[2048,1152]{1,0:T(8,128)(2,1)} %get-tuple-element.79, ...), custom_call_target="tpu_custom_call" | custom-call | flops 6710886400 | bytes 31457280 | tf_op jit(solution)/shard_map/attend_forward/pallas_call | solution.py:262
  189.2 165.3 %block_forward.1 = (bf16[1024,2560]{1,0:T(8,128)(2,1)}, bf16[1024,2560]{1,0:T(8,128)(2,1)}, bf16[4,1024,640]{2,1,0:T(8,128)(2,1)}, bf16[2560,1024]{1,0:T(8,128)(...) custom-call(bf16[640,1024]{1,0:T(8,128)(2,1)} %get-tuple-element.84.att_ref, ...), custom_call_target="tpu_custom_call" | custom-call | flops 50331648000 | bytes 419430400 | tf_op jit(solution)/shard_map/block_forward/pallas_call | solution.py:865
  354.5 134.7 %grad_reduce.1 = (bf16[1024,2560]{1,0:T(8,128)(2,1)}, f32[1024,640]{1,0:T(8,128)}, f32[1,640]{1,0:T(1,128)}, bf16[3,320,1600]{2,1,0:T(8,128)(2,1)}, f32[8,128]{1,0:T(8,128)}) custom-call(f32[1024,1]{1,0:T(8,128)} %fusion.10.live_ref, f32[1,2560]{1,0:T(1,128)} %bitcast.77, bf16[1024,2560]{1,0:T(8,128)(2,1)} %get-tuple-element.91.dnp_any, ...), custom_call_target="tpu_custom_call" | custom-call | flops 25165824000 | bytes 419430400 | tf_op jit(solution)/shard_map/grad_reduce/pallas_call | solution.py:1196
  489.2 7.1 convolution_convert_fusion.1
  496.5 9.0 %convolution_convert_fusion.gout_ref = bf16[2560,640]{1,0:T(8,128)(2,1)} fusion(bf16[1024,2560]{1,0:T(8,128)(2,1)} %get-tuple-element.102, bf16[640,1024]{1,0:T(8,128)(2,1)} %get-tuple-element.84.att_ref), kind=kOutput, calls=%fused_computation.1 | convolution fusion | flops 3357081600 | bytes 9830400 | tf_op jit(solution)/shard_map/dot_general | solution.py:52
  507.1 48.9 %attend_backward.1 = (bf16[2048,640]{1,0:T(8,128)(2,1)S(1)}, bf16[2048,640]{1,0:T(8,128)(2,1)S(1)}, f32[2048,128]{1,0:T(8,128)S(1)}) custom-call(bf16[5,128,2048]{2,1,0:T(8,128)(2,1)S(1)} %copy-done.5, bf16[5,2048,128]{2,1,0:T(8,128)(2,1)} %get-tuple-element.99.k_ref, bf16[5,80,2048]{2,1,0:T(8,128)(2,1)S(1)} %copy-done.6, ...), custom_call_target="tpu_custom_call" | custom-call | flops 18874368000 | bytes 31457280 | tf_op jit(solution)/shard_map/attend_backward/pallas_call | solution.py:351
  556.1 1.0 copy-done.2
  557.1 2.3 convolution_convert_fusion.2.gkv_ref
  559.5 3.6 fusion.5.gq_ref
  563.2 106.6 %latent_backward.1 = (bf16[1024,640]{1,0:T(8,128)(2,1)}, bf16[576,640]{1,0:T(8,128)(2,1)}, bf16[160,640]{1,0:T(8,128)(2,1)}, f32[8,1024]{1,0:T(8,128)}, f32[8,12...) custom-call(bf16[2048,640]{1,0:T(8,128)(2,1)} %copy-done, bf16[2048,640]{1,0:T(8,128)(2,1)} %copy-done.1, ...), custom_call_target="tpu_custom_call" | custom-call | flops 4529848320 | bytes 209715200 | tf_op jit(solution)/shard_map/latent_backward/pallas_call | solution.py:1555
  669.8 0.8 slice.82
  670.6 1.6 fusion.34
  672.3 1.2 fusion.24
  673.4 1.2 multiply_add_fusion.8
  674.6 2.0 fusion.23
  676.6 1.2 multiply_add_fusion.7
  677.8 2.4 multiply_subtract_fusion.6
  680.2 3.0 multiply_subtract_fusion.4
  683.2 3.1 multiply_subtract_fusion.3
  686.4 4.6 multiply_subtract_fusion.2
  691.0 2.5 multiply_subtract_fusion.5
  693.5 6.8 multiply_subtract_fusion.1
  700.4 7.5 %multiply_subtract_fusion = (f32[2,320,1600]{2,1,0:T(8,128)}, f32[2,320,1600]{2,1,0:T(8,128)}, f32[2,320,1600]{2,1,0:T(8,128)}, f32[2,320,1600]{2,1,0:T(8,128)}) fusion(f32[2,320,1600]{2,1,0:T(8,128)S(1)} %bitcast.67, f32[]{:T(128)} %bitcast.27, f32[2,320,1600]{2,1,0:T(8,128)S(1)} %bitcast.69, f32[2,320,1600]{2,1,0:T(8,128)S(1)} %bitcast.71, ...), kind=kLoop, calls=%fused_computation.3 | loop fusion | flops 17408000 | bytes 30720004 | tf_op jit(solution)/shard_map/sub | solution.py:1658
  707.9 3.3 fusion.3
  711.1 1.1 copy.82
  (106 shorter events, 7.8 us)
Async XLA Ops:
  7.2 700.6 %reduce-scatter.2.cloned.1.call-start = ((), (), s32[]{:S(2)}) async-start(), calls=%async_computation.1 | async-start | bytes 6553600 | tf_op jit(solution)/shard_map/reduce_scatter | solution.py:1815
  12.3 4.0 copy-start.17
  12.3 4.0 copy-start.21
  12.3 4.0 copy-start.30
  12.3 4.0 copy-start.9
  496.4 9.2 %collective-permute-start = (bf16[320,1024]{1,0:T(8,128)(2,1)S(1)}, bf16[320,1024]{1,0:T(8,128)(2,1)S(1)}, u32[]{:S(2)}, u32[]{:S(2)}) collective-permute-start(bf16[320,1024]{1,0:T(8,128)(2,1)S(1)} %get-tuple-element.153), channel_id=1, source_target_pairs={{0,4},{4,0},{1,5},{5,1},{2,6},{6,2},{3,7},{7,3},{8,12},{12,8},{9,1... | collective-permute-start | bytes 1966088 | tf_op jit(solution)/shard_map/ppermute | solution.py:1597
  496.5 9.5 %copy-start.5 = (bf16[5,128,2048]{2,1,0:T(8,128)(2,1)S(1)}, bf16[5,128,2048]{2,1,0:T(8,128)(2,1)}, u32[]{:S(2)}) copy-start(bf16[5,128,2048]{2,1,0:T(8,128)(2,1)} %get-tuple-element.98.q_ref) | copy-start | bytes 7864324
  496.5 9.5 %copy-start.7 = (bf16[5,64,2048]{2,1,0:T(8,128)(2,1)S(1)}, bf16[5,64,2048]{2,1,0:T(8,128)(2,1)}, u32[]{:S(2)}) copy-start(bf16[5,64,2048]{2,1,0:T(8,128)(2,1)} %get-tuple-element.101.o_ref) | copy-start | bytes 3932164
  496.5 60.5 %slice-start.6 = ((s8[4718592]{0:T(1024)(128)(4,1)}), s8[4194304]{0:T(1024)(128)(4,1)S(1)}, s32[]{:S(2)}) async-start(s8[4718592]{0:T(1024)(128)(4,1)} %bitcast.81), calls=%async_computation.8 | async-start | bytes 8388608
  507.1 49.9 %slice-start.7 = ((s8[4718592]{0:T(1024)(128)(4,1)}), s8[524288]{0:T(1024)(128)(4,1)S(1)}, s32[]{:S(2)}) async-start(s8[4718592]{0:T(1024)(128)(4,1)} %bitcast.81), calls=%async_computation.9 | async-start | bytes 1048576
  563.1 109.1 %copy-start.28 = (f32[128]{0:T(128)S(1)}, f32[128]{0:T(128)}, u32[]{:S(2)}) copy-start(f32[128]{0:T(128)} %param.65) | copy-start | bytes 1540
  563.1 110.3 %copy-start.29 = (f32[128]{0:T(128)S(1)}, f32[128]{0:T(128)}, u32[]{:S(2)}) copy-start(f32[128]{0:T(128)} %param.56) | copy-start | bytes 1540
  563.1 111.5 %copy-start.26 = (f32[2,640]{1,0:T(2,128)S(1)}, f32[2,640]{1,0:T(2,128)}, u32[]{:S(2)}) copy-start(f32[2,640]{1,0:T(2,128)} %param.64) | copy-start | bytes 15364
  563.1 113.4 %copy-start.24 = (f32[2,640]{1,0:T(2,128)S(1)}, f32[2,640]{1,0:T(2,128)}, u32[]{:S(2)}) copy-start(f32[2,640]{1,0:T(2,128)} %param.55) | copy-start | bytes 15364
  563.1 117.1 %copy-start.18 = (f32[640,96]{0,1:T(8,128)S(1)}, f32[640,96]{0,1:T(8,128)}, u32[]{:S(2)}) copy-start(f32[640,96]{0,1:T(8,128)} %param.39) | copy-start | bytes 737284
  563.2 117.1 %copy-start.22 = (f32[640,96]{0,1:T(8,128)S(1)}, f32[640,96]{0,1:T(8,128)}, u32[]{:S(2)}) copy-start(f32[640,96]{0,1:T(8,128)} %param.48) | copy-start | bytes 737284
  563.2 137.1 %slice-start.4 = ((s8[4259840]{0:T(1024)(128)(4,1)}), s8[65536]{0:T(1024)(128)(4,1)S(1)}, s32[]{:S(2)}) async-start(s8[4259840]{0:T(1024)(128)(4,1)} %bitcast.70), calls=%async_computation.6 | async-start | bytes 131072
  669.8 13.4 %copy-start.14 = (f32[96,960]{1,0:T(8,128)S(1)}, f32[96,960]{1,0:T(8,128)}, u32[]{:S(2)}) copy-start(f32[96,960]{1,0:T(8,128)} %param.41) | copy-start | bytes 1105924
  669.8 13.4 %copy-start.15 = (f32[96,960]{1,0:T(8,128)S(1)}, f32[96,960]{1,0:T(8,128)}, u32[]{:S(2)}) copy-start(f32[96,960]{1,0:T(8,128)} %get-tuple-element.205) | copy-start | bytes 1105924
  673.4 12.9 %copy-start.27 = (f32[128]{0:T(128)}, f32[128]{0:T(128)S(1)}, u32[]{:S(2)}) copy-start(f32[128]{0:T(128)S(1)} %get-tuple-element.211) | copy-start | bytes 1540
  676.6 9.8 %copy-start.23 = (f32[2,640]{1,0:T(2,128)}, f32[2,640]{1,0:T(2,128)S(1)}, u32[]{:S(2)}) copy-start(f32[2,640]{1,0:T(2,128)S(1)} %get-tuple-element.210) | copy-start | bytes 15364
  677.8 13.2 %copy-start.20 = (f32[32,1280]{1,0:T(8,128)S(1)}, f32[32,1280]{1,0:T(8,128)}, u32[]{:S(2)}) copy-start(f32[32,1280]{1,0:T(8,128)} %param.42) | copy-start | bytes 491524
  680.2 20.1 %slice-start.5 = ((s8[4259840]{0:T(1024)(128)(4,1)}), s8[4194304]{0:T(1024)(128)(4,1)S(1)}, s32[]{:S(2)}) async-start(s8[4259840]{0:T(1024)(128)(4,1)} %bitcast.70), calls=%async_computation.7 | async-start | bytes 8388608
  683.2 7.8 %copy-start.19 = (f32[32,1280]{1,0:T(8,128)S(1)}, f32[32,1280]{1,0:T(8,128)}, u32[]{:S(2)}) copy-start(f32[32,1280]{1,0:T(8,128)} %get-tuple-element.206) | copy-start | bytes 491524
  683.2 10.3 %copy-start.13 = (f32[1600,320]{0,1:T(8,128)S(1)}, f32[1600,320]{0,1:T(8,128)}, u32[]{:S(2)}) copy-start(f32[1600,320]{0,1:T(8,128)} %param.54) | copy-start | bytes 6144004
  686.4 7.1 copy-start.10
  686.4 7.1 copy-start.12
  693.5 6.8 slice-start
  693.5 6.8 slice-start.2
  693.5 6.8 slice-start.1
  693.5 6.8 slice-start.3
  707.9 3.3 copy-start.16
  (9 other events, 15.2 us)
Sparse Core Ops, SparseCore 0:
  489.3 92.7 reduce-scatter.1
